TPU v7x, 32 devices: a whole 2x2x4 slice. The times are simulated.
32 devices in a mesh: wide: 16 (over z, y, core), field: 2 (over x).
Axes of the slice: x: 2, y: 2, z: 4, core: 2. Of those that a mesh axis runs over, the one named last changes fastest.
Arguments:
- fine_field_in: bfloat16 [128, 32, 512], P('wide', 'field'), may hold values from -6 to 6
- fine_points: float32 [256, 3, 1024], P(('wide', 'field')), may hold values from -1 to 1
- coarse_points: float32 [256, 3, 1024], P(('wide', 'field')), may hold values from -1 to 1
- quad_weights: float32 [256, 1024], P(('wide', 'field')), may hold values from 0.00390625 to 0.01171875
- pair_fine: int32 [256], P('wide'), may hold values from 0 to 7, as said below
- pair_owner: int32 [256, 1], P('wide'), may hold values from 0 to 15; in each aligned block of 16 rows (0 to 15, 16 to 31, ...) at most 2 rows name the same one
- pair_coarse: int32 [256], P('wide'), may hold values from 0 to 15
- coarse_faces: int32 [256, 6], P('wide'), may hold values from 0 to 255, as said below
- coarse_inv_mass: float32 [256], P('wide'), may hold values from 0.5 to 2
- fine_inv_mass: float32 [128], P('wide'), may hold values from 0.5 to 2
Outputs:
- coarse_field: bfloat16 [256, 32, 512], P('wide', 'field')
- fine_field: bfloat16 [128, 32, 512], P('wide', 'field')
Inputs may be any that keep to these rules, and one draw needn't show every extreme that they name: `pair_fine`: within each aligned block of 16 pairs (one partition) every value 0 to 7 appears at least once. `pair_owner`: in each aligned block of 16 rows (one partition) no owner is named more than 2 times, a bound that some block reaches. `coarse_faces`: the owner of a neighbour (index // 16) differs from the element's own owner by at most one; a boundary face names the element itself.
All inputs are finite; a program needn't handle non-finite values.
Results may differ from a plain program's by a relative error of at most 0.007.
Values may be sent and summed in bfloat16 or wider, within the bound.
No kernel may reach another device: no remote copies, remote signals or barrier semaphores. Data moves between devices by JAX's collectives and lax.ppermute only.
A program may use at most 64 MiB of HBM per device.

v0:
```python
import math

import jax
import jax.numpy as jnp
from jax import lax
from jax.sharding import PartitionSpec as P

NB = 8
CAP = 2


DIFFUSE = 0.125


def with_halo(block, sides, width):
    for axis, dim in sides:
        count = lax.axis_size(axis)
        forward = [(i, i + 1) for i in range(count - 1)]
        backward = [(target, source) for source, target in forward]
        low = lax.ppermute(
            lax.slice_in_dim(block, block.shape[dim] - width, None, axis=dim), axis, forward
        )
        high = lax.ppermute(lax.slice_in_dim(block, 0, width, axis=dim), axis, backward)
        block = jnp.concatenate([low, block, high], axis=dim)
    return block


def legendre(points, count):
    values = [jnp.ones_like(points), points]
    for degree in range(1, count - 1):
        values.append(
            ((2 * degree + 1) * points * values[degree] - degree * values[degree - 1])
            / (degree + 1)
        )
    values = values[:count]
    return jnp.stack([values[n] * math.sqrt((2 * n + 1) / 2.0) for n in range(count)])


def basis(points, count):
    table = legendre(points, count)
    product = table[:, None, None, 0, :] * table[None, :, None, 1, :] * table[None, None, :, 2, :]
    return product.reshape(count * count * count, points.shape[-1])


def build_tile(fine_pts, coarse_pts, weights):
    left = (basis(coarse_pts, NB) * weights[None, :]).astype(jnp.bfloat16)
    right = basis(fine_pts, NB).astype(jnp.bfloat16)
    return lax.dot_general(
        left, right, (((1,), (1,)), ((), ())), preferred_element_type=jnp.float32
    ).astype(jnp.bfloat16)


def shards(
    fine_field_in,
    fine_points,
    coarse_points,
    quad_weights,
    pair_fine,
    pair_owner,
    pair_coarse,
    coarse_faces,
    coarse_inv_mass,
    fine_inv_mass,
):
    nwide = lax.axis_size("wide")
    wide_index = lax.axis_index("wide")
    grp_pairs = pair_fine.shape[0]
    block = fine_field_in.shape[1]
    basis_count = fine_field_in.shape[2]
    fine_count = fine_field_in.shape[0]
    coarse_count = coarse_inv_mass.shape[0]
    slots = nwide * CAP
    tiles = lax.map(
        lambda item: build_tile(item[0], item[1], item[2]),
        (fine_points, coarse_points, quad_weights),
    )
    picked = jnp.take(fine_field_in, pair_fine, axis=0)
    rows = lax.all_to_all(picked, "field", split_axis=0, concat_axis=1, tiled=True)
    contrib = jnp.einsum("pfj,pij->pfi", rows, tiles, preferred_element_type=jnp.float32).astype(
        jnp.bfloat16
    )
    blocked = lax.all_to_all(contrib, "field", split_axis=1, concat_axis=0, tiled=True)
    owner = pair_owner[:, 0]
    owner_hot = (owner[:, None] == jnp.arange(nwide, dtype=jnp.int32)[None, :]).astype(jnp.int32)
    before = jnp.cumsum(owner_hot, axis=0) - owner_hot
    slot = jnp.sum(before * owner_hot, axis=1)
    target = owner * CAP + slot
    place = jnp.arange(slots, dtype=jnp.int32)[:, None] == target[None, :]
    place_bf = place.astype(jnp.bfloat16)
    slot_ids = jnp.sum(jnp.where(place, (pair_coarse + 1)[None, :], 0), axis=1)
    outgoing = jnp.dot(
        place_bf,
        blocked.reshape(grp_pairs, block * basis_count),
        preferred_element_type=jnp.float32,
    ).astype(jnp.bfloat16)
    arrived, arrived_ids = (
        lax.all_to_all(outgoing, "wide", split_axis=0, concat_axis=0, tiled=True),
        lax.all_to_all(slot_ids, "wide", split_axis=0, concat_axis=0, tiled=True),
    )
    owned_hot = (
        jnp.arange(coarse_count, dtype=jnp.int32)[:, None] == (arrived_ids - 1)[None, :]
    ).astype(jnp.bfloat16)
    load = jnp.dot(owned_hot, arrived, preferred_element_type=jnp.float32)
    solved = coarse_inv_mass[:, None] * load
    table = with_halo(solved, (("wide", 0),), coarse_count)
    relative = coarse_faces - (wide_index - 1) * coarse_count
    face_hits = jnp.sum(
        (
            relative[:, :, None] == jnp.arange(3 * coarse_count, dtype=jnp.int32)[None, None, :]
        ).astype(jnp.float32),
        axis=1,
    )
    beside = jnp.dot(
        face_hits, table, precision=lax.Precision.HIGHEST, preferred_element_type=jnp.float32
    )
    smoothed = solved + DIFFUSE * (beside - 6.0 * solved)
    coarse_out = smoothed.astype(jnp.bfloat16)
    reply = lax.dot_general(
        owned_hot, coarse_out, (((0,), (0,)), ((), ())), preferred_element_type=jnp.float32
    ).astype(jnp.bfloat16)
    returned = lax.all_to_all(reply, "wide", split_axis=0, concat_axis=0, tiled=True)
    per_pair = lax.dot_general(
        place_bf, returned, (((0,), (0,)), ((), ())), preferred_element_type=jnp.float32
    ).astype(jnp.bfloat16)
    spread = lax.all_to_all(
        per_pair.reshape(grp_pairs, block, basis_count),
        "field",
        split_axis=0,
        concat_axis=1,
        tiled=True,
    )
    terms = jnp.einsum("pfj,pji->pfi", spread, tiles, preferred_element_type=jnp.float32).astype(
        jnp.bfloat16
    )
    collected = lax.all_to_all(terms, "field", split_axis=1, concat_axis=0, tiled=True)
    fine_hot = (jnp.arange(fine_count, dtype=jnp.int32)[:, None] == pair_fine[None, :]).astype(
        jnp.bfloat16
    )
    fine_sum = jnp.dot(
        fine_hot,
        collected.reshape(grp_pairs, block * basis_count),
        preferred_element_type=jnp.float32,
    )
    fine_out = (fine_inv_mass[:, None] * fine_sum).astype(jnp.bfloat16)
    return (
        coarse_out.reshape(coarse_count, block, basis_count),
        fine_out.reshape(fine_count, block, basis_count),
    )


def solution(mesh):
    placed = (
        P("wide", "field", None),
        P(("wide", "field"), None, None),
        P(("wide", "field"), None, None),
        P(("wide", "field"), None),
        P("wide"),
        P("wide", None),
        P("wide"),
        P("wide", None),
        P("wide"),
        P("wide"),
    )
    return jax.shard_map(
        shards,
        mesh=mesh,
        in_specs=placed,
        out_specs=(P("wide", "field", None), P("wide", "field", None)),
        check_vma=False,
    )
```

profile of v0, /device:TPU:0, one launch (start us, length us, event | category | flops | bytes accessed | tf_op | source)
XLA Modules:
  0.0 147.1 jit_solution(11060210914114905766)
XLA Ops:
  0.6 0.7 compare_select_fusion
  1.3 0.7 compare_and_fusion
  2.0 0.6 gather_fusion
  2.6 0.8 broadcast_select_fusion
  3.4 4.2 %all-to-all-start.1 = ((bf16[16,16,512]{2,1,0:T(8,128)(2,1)}), bf16[16,16,512]{2,1,0:T(8,128)(2,1)S(1)}, u32[]{:S(2)}, u32[]{:S(2)}) async-start(bf16[16,16,512]{2,1,0:T(8,128)(2,1)} %broadcast_select_fusion), calls=%async_computation.1 | async-start | bytes 524288 | tf_op jit(solution)/shard_map/all_to_all | solution.py:78
  7.6 36.4 %while.13 = (s32[]{:T(128)}, bf16[8,512,512]{2,1,0:T(8,128)(2,1)}, f32[8,3,1024]{2,0,1:T(8,128)}, f32[8,1024]{1,0:T(8,128)}, f32[8,3,1024]{2,0,1:T(8,128)}, /*index=5*/s32[]{:T(128)}, f32[]{:T(128)}) while((s32[]{:T(128)}, bf16[8,512,512]{2,1,0:T(8,128)(2,1)}, f32[8,3,1024]{2,0,1:T(8,128)}, f32[8,1024]{1,0:T(8,128)}, f32[8,3,1024]{2,0,1:T(8,128)}, ...), condition=%wide.region_4.5_spmd, body=%wide.region_3.4_spmd.sunk | while | flops 540100608 | bytes 7365209 | solution.py:73
  7.6 1.0 constant_dynamic-slice_fusion.6
  9.6 0.8 constant_dynamic-slice_fusion.5
  10.4 0.2 multiply_convert_fusion.4
  10.6 1.5 %fusion.63 = bf16[8,512,512]{2,1,0:T(8,128)(2,1)} fusion(bf16[8,512,512]{2,1,0:T(8,128)(2,1)} %get-tuple-element.290, s32[]{:T(128)} %get-tuple-element.289, bf16[512,1024]{1,0:T(8,128)(2,1)S(1)} %bitcast.78, bf16[512,1024]{1,0:T(8,128)(2,1)S(1)} %bitcast.77), kind=kOutput, calls=%fused_computation.5.clone.1 | convolution fusion | flops 537133056 | bytes 2621952 | tf_op jit(solution)/shard_map/while/body/eval_jaxpr/dot_general | solution.py:48
  12.1 1.0 constant_dynamic-slice_fusion.6
  14.1 0.8 constant_dynamic-slice_fusion.5
  14.9 0.2 multiply_convert_fusion.4
  15.2 1.5 %fusion.63 = bf16[8,512,512]{2,1,0:T(8,128)(2,1)} fusion(bf16[8,512,512]{2,1,0:T(8,128)(2,1)} %get-tuple-element.290, s32[]{:T(128)} %get-tuple-element.289, bf16[512,1024]{1,0:T(8,128)(2,1)S(1)} %bitcast.78, bf16[512,1024]{1,0:T(8,128)(2,1)S(1)} %bitcast.77), kind=kOutput, calls=%fused_computation.5.clone.1 | convolution fusion | flops 537133056 | bytes 2621952 | tf_op jit(solution)/shard_map/while/body/eval_jaxpr/dot_general | solution.py:48
  16.7 1.0 constant_dynamic-slice_fusion.6
  18.7 0.8 constant_dynamic-slice_fusion.5
  19.5 0.2 multiply_convert_fusion.4
  19.7 1.6 %fusion.63 = bf16[8,512,512]{2,1,0:T(8,128)(2,1)} fusion(bf16[8,512,512]{2,1,0:T(8,128)(2,1)} %get-tuple-element.290, s32[]{:T(128)} %get-tuple-element.289, bf16[512,1024]{1,0:T(8,128)(2,1)S(1)} %bitcast.78, bf16[512,1024]{1,0:T(8,128)(2,1)S(1)} %bitcast.77), kind=kOutput, calls=%fused_computation.5.clone.1 | convolution fusion | flops 537133056 | bytes 2621952 | tf_op jit(solution)/shard_map/while/body/eval_jaxpr/dot_general | solution.py:48
  21.2 1.0 constant_dynamic-slice_fusion.6
  23.2 0.8 constant_dynamic-slice_fusion.5
  24.0 0.2 multiply_convert_fusion.4
  24.3 1.5 %fusion.63 = bf16[8,512,512]{2,1,0:T(8,128)(2,1)} fusion(bf16[8,512,512]{2,1,0:T(8,128)(2,1)} %get-tuple-element.290, s32[]{:T(128)} %get-tuple-element.289, bf16[512,1024]{1,0:T(8,128)(2,1)S(1)} %bitcast.78, bf16[512,1024]{1,0:T(8,128)(2,1)S(1)} %bitcast.77), kind=kOutput, calls=%fused_computation.5.clone.1 | convolution fusion | flops 537133056 | bytes 2621952 | tf_op jit(solution)/shard_map/while/body/eval_jaxpr/dot_general | solution.py:48
  25.8 1.0 constant_dynamic-slice_fusion.6
  27.8 0.8 constant_dynamic-slice_fusion.5
  28.6 0.2 multiply_convert_fusion.4
  28.8 1.5 %fusion.63 = bf16[8,512,512]{2,1,0:T(8,128)(2,1)} fusion(bf16[8,512,512]{2,1,0:T(8,128)(2,1)} %get-tuple-element.290, s32[]{:T(128)} %get-tuple-element.289, bf16[512,1024]{1,0:T(8,128)(2,1)S(1)} %bitcast.78, bf16[512,1024]{1,0:T(8,128)(2,1)S(1)} %bitcast.77), kind=kOutput, calls=%fused_computation.5.clone.1 | convolution fusion | flops 537133056 | bytes 2621952 | tf_op jit(solution)/shard_map/while/body/eval_jaxpr/dot_general | solution.py:48
  30.3 1.0 constant_dynamic-slice_fusion.6
  32.3 0.8 constant_dynamic-slice_fusion.5
  33.1 0.2 multiply_convert_fusion.4
  33.3 1.6 %fusion.63 = bf16[8,512,512]{2,1,0:T(8,128)(2,1)} fusion(bf16[8,512,512]{2,1,0:T(8,128)(2,1)} %get-tuple-element.290, s32[]{:T(128)} %get-tuple-element.289, bf16[512,1024]{1,0:T(8,128)(2,1)S(1)} %bitcast.78, bf16[512,1024]{1,0:T(8,128)(2,1)S(1)} %bitcast.77), kind=kOutput, calls=%fused_computation.5.clone.1 | convolution fusion | flops 537133056 | bytes 2621952 | tf_op jit(solution)/shard_map/while/body/eval_jaxpr/dot_general | solution.py:48
  34.9 1.0 constant_dynamic-slice_fusion.6
  36.9 0.8 constant_dynamic-slice_fusion.5
  37.7 0.2 multiply_convert_fusion.4
  37.9 1.6 %fusion.63 = bf16[8,512,512]{2,1,0:T(8,128)(2,1)} fusion(bf16[8,512,512]{2,1,0:T(8,128)(2,1)} %get-tuple-element.290, s32[]{:T(128)} %get-tuple-element.289, bf16[512,1024]{1,0:T(8,128)(2,1)S(1)} %bitcast.78, bf16[512,1024]{1,0:T(8,128)(2,1)S(1)} %bitcast.77), kind=kOutput, calls=%fused_computation.5.clone.1 | convolution fusion | flops 537133056 | bytes 2621952 | tf_op jit(solution)/shard_map/while/body/eval_jaxpr/dot_general | solution.py:48
  39.5 1.0 constant_dynamic-slice_fusion.6
  41.5 0.8 constant_dynamic-slice_fusion.5
  42.2 0.2 multiply_convert_fusion.4
  42.5 1.5 %fusion.63 = bf16[8,512,512]{2,1,0:T(8,128)(2,1)} fusion(bf16[8,512,512]{2,1,0:T(8,128)(2,1)} %get-tuple-element.290, s32[]{:T(128)} %get-tuple-element.289, bf16[512,1024]{1,0:T(8,128)(2,1)S(1)} %bitcast.78, bf16[512,1024]{1,0:T(8,128)(2,1)S(1)} %bitcast.77), kind=kOutput, calls=%fused_computation.5.clone.1 | convolution fusion | flops 537133056 | bytes 2621952 | tf_op jit(solution)/shard_map/while/body/eval_jaxpr/dot_general | solution.py:48
  44.4 3.5 %convolution_convert_fusion.5 = bf16[8,32,512]{2,1,0:T(8,128)(2,1)S(1)} fusion(bf16[8,32,512]{2,1,0:T(8,128)(2,1)S(1)} %bitcast.79, bf16[8,512,512]{2,1,0:T(8,128)(2,1)} %get-tuple-element.143), kind=kOutput, calls=%fused_computation.83 | convolution fusion | flops 134348800 | bytes 4718592 | tf_op jit(solution)/shard_map/pfj,pij->pfi/dot_general | solution.py:79
  47.9 0.9 copy.77
  48.7 3.5 %all-to-all-start.2 = ((bf16[8,32,512]{2,0,1:T(8,128)(2,1)}), bf16[8,32,512]{2,0,1:T(8,128)(2,1)S(1)}, u32[]{:S(2)}, u32[]{:S(2)}) async-start(bf16[8,32,512]{2,0,1:T(8,128)(2,1)} %copy.77), calls=%async_computation.2 | async-start | bytes 524288 | tf_op jit(solution)/shard_map/all_to_all | solution.py:82
  52.3 0.7 all_to_all.70
  53.0 5.1 %all-to-all-done.2 = bf16[8,32,512]{2,0,1:T(8,128)(2,1)S(1)} async-done(((bf16[8,32,512]{2,0,1:T(8,128)(2,1)}), bf16[8,32,512]{2,0,1:T(8,128)(2,1)S(1)}, u32[]{:S(2)}, u32[]{:S(2)}) %all-to-all-start.2) | async-done | bytes 262176 | tf_op jit(solution)/shard_map/all_to_all | solution.py:82
  58.1 6.2 %all-to-all-start = ((s32[16,2,1]{1,2,0:T(1,128)}), s32[16,2,1]{1,2,0:T(1,128)S(1)}, u32[]{:S(2)}, u32[]{:S(2)}) async-start(s32[16,2,1]{1,2,0:T(1,128)} %bitcast.11), calls=%async_computation | async-start | bytes 16384 | tf_op jit(solution)/shard_map/all_to_all | solution.py:98
  64.5 0.4 convolution_convert_fusion.2
  65.0 1.1 all_to_all.79
  66.1 4.5 %all-to-all-done = s32[16,2,1]{1,2,0:T(1,128)S(1)} async-done(((s32[16,2,1]{1,2,0:T(1,128)}), s32[16,2,1]{1,2,0:T(1,128)S(1)}, u32[]{:S(2)}, u32[]{:S(2)}) %all-to-all-start) | async-done | bytes 160 | tf_op jit(solution)/shard_map/all_to_all | solution.py:98
  70.6 3.6 %all-to-all-start.3 = ((bf16[16,2,8192]{2,1,0:T(2,128)(2,1)}), bf16[16,2,8192]{2,1,0:T(2,128)(2,1)S(1)}, u32[]{:S(2)}, u32[]{:S(2)}) async-start(bf16[16,2,8192]{2,1,0:T(2,128)(2,1)} %all_to_all.79), calls=%async_computation.3 | async-start | bytes 1048576 | tf_op jit(solution)/shard_map/all_to_all | solution.py:97
  74.3 14.3 %all-to-all-done.3 = bf16[16,2,8192]{2,1,0:T(2,128)(2,1)S(1)} async-done(((bf16[16,2,8192]{2,1,0:T(2,128)(2,1)}), bf16[16,2,8192]{2,1,0:T(2,128)(2,1)S(1)}, u32[]{:S(2)}, u32[]{:S(2)}) %all-to-all-start.3) | async-done | bytes 524320 | tf_op jit(solution)/shard_map/all_to_all | solution.py:97
  89.0 2.0 %collective-permute-start = (f32[16,8192]{1,0:T(8,128)S(1)}, f32[16,8192]{1,0:T(8,128)S(1)}, u32[]{:S(2)}, u32[]{:S(2)}) collective-permute-start(f32[16,8192]{1,0:T(8,128)S(1)} %convolution_multiply_fusion), channel_id=1, source_target_pairs={{0,2},{2,4},{4,6},{6,8},{8,10},{10,12},{12,14},{14,16},{16,18},{18... | collective-permute-start | bytes 1572872 | tf_op jit(solution)/shard_map/ppermute | solution.py:20
  91.0 1.3 collective-permute-start.1
  92.5 2.3 %collective-permute-done.1 = f32[16,8192]{1,0:T(8,128)S(1)} collective-permute-done((f32[16,8192]{1,0:T(8,128)S(1)}, f32[16,8192]{1,0:T(8,128)S(1)}, u32[]{:S(2)}, u32[]{:S(2)}) %collective-permute-start.1) | collective-permute-done | bytes 524320 | tf_op jit(solution)/shard_map/ppermute | solution.py:23
  94.8 0.9 fusion.28
  95.7 0.3 convolution_convert_fusion.1
  96.0 0.3 all_to_all.82
  96.4 28.5 %all_to_all.99 = bf16[16,2,8192]{2,1,0:T(2,128)(2,1)S(1)} all-to-all(bf16[16,2,8192]{2,1,0:T(2,128)(2,1)S(1)} %all_to_all.82), channel_id=1, replica_groups=mesh['wide'=16,'field'=2] {'wide'}, dimensions={0} | all-to-all | bytes 1048576 | tf_op jit(solution)/shard_map/all_to_all | solution.py:121
  125.1 0.3 convolution_convert_fusion.3
  125.5 8.0 %all_to_all.100 = bf16[16,16,512]{2,1,0:T(8,128)(2,1)S(1)} all-to-all(bf16[16,16,512]{2,1,0:T(8,128)(2,1)S(1)} %bitcast.85), channel_id=1, replica_groups=mesh['wide'=16,'field'=2] {'field'}, dimensions={0} | all-to-all | bytes 524288 | tf_op jit(solution)/shard_map/all_to_all | solution.py:125
  133.5 3.0 %convolution_convert_fusion.4 = bf16[8,32,512]{2,1,0:T(8,128)(2,1)S(1)} fusion(bf16[8,32,512]{2,1,0:T(8,128)(2,1)S(1)} %bitcast.80, bf16[8,512,512]{2,1,0:T(8,128)(2,1)} %get-tuple-element.143), kind=kOutput, calls=%fused_computation.82 | convolution fusion | flops 134348800 | bytes 4718592 | tf_op jit(solution)/shard_map/pfj,pji->pfi/dot_general | solution.py:132
  136.5 0.9 copy.80
  137.4 3.4 %all-to-all-start.6 = ((bf16[8,32,512]{2,0,1:T(8,128)(2,1)}), bf16[8,32,512]{2,0,1:T(8,128)(2,1)S(1)}, u32[]{:S(2)}, u32[]{:S(2)}) async-start(bf16[8,32,512]{2,0,1:T(8,128)(2,1)} %copy.80), calls=%async_computation.6 | async-start | bytes 524288 | tf_op jit(solution)/shard_map/all_to_all | solution.py:135
  140.8 0.8 copy.86
  141.6 4.4 %all-to-all-done.6 = bf16[8,32,512]{2,0,1:T(8,128)(2,1)S(1)} async-done(((bf16[8,32,512]{2,0,1:T(8,128)(2,1)}), bf16[8,32,512]{2,0,1:T(8,128)(2,1)S(1)}, u32[]{:S(2)}, u32[]{:S(2)}) %all-to-all-start.6) | async-done | bytes 262176 | tf_op jit(solution)/shard_map/all_to_all | solution.py:135
  146.4 0.7 copy.82
  (230 shorter events, 8.9 us)
Async XLA Ops:
  0.6 1.4 copy-start
  3.4 40.9 %all-to-all-start.1 = ((bf16[16,16,512]{2,1,0:T(8,128)(2,1)}), bf16[16,16,512]{2,1,0:T(8,128)(2,1)S(1)}, u32[]{:S(2)}, u32[]{:S(2)}) async-start(bf16[16,16,512]{2,1,0:T(8,128)(2,1)} %broadcast_select_fusion), calls=%async_computation.1 | async-start | bytes 524288 | tf_op jit(solution)/shard_map/all_to_all | solution.py:78
  7.6 36.4 %copy-start.1 = (s32[16,1]{0,1:T(1,128)S(1)}, s32[16,1]{0,1:T(1,128)}, u32[]{:S(2)}) copy-start(s32[16,1]{0,1:T(1,128)} %param.17) | copy-start | bytes 196
  44.3 7.9 %copy-start.6 = (s32[16]{0:T(128)S(1)}, s32[16]{0:T(128)}, u32[]{:S(2)}) copy-start(s32[16]{0:T(128)} %param.18) | copy-start | bytes 196
  48.7 9.3 %all-to-all-start.2 = ((bf16[8,32,512]{2,0,1:T(8,128)(2,1)}), bf16[8,32,512]{2,0,1:T(8,128)(2,1)S(1)}, u32[]{:S(2)}, u32[]{:S(2)}) async-start(bf16[8,32,512]{2,0,1:T(8,128)(2,1)} %copy.77), calls=%async_computation.2 | async-start | bytes 524288 | tf_op jit(solution)/shard_map/all_to_all | solution.py:82
  58.1 12.5 %all-to-all-start = ((s32[16,2,1]{1,2,0:T(1,128)}), s32[16,2,1]{1,2,0:T(1,128)S(1)}, u32[]{:S(2)}, u32[]{:S(2)}) async-start(s32[16,2,1]{1,2,0:T(1,128)} %bitcast.11), calls=%async_computation | async-start | bytes 16384 | tf_op jit(solution)/shard_map/all_to_all | solution.py:98
  64.5 24.3 %copy-start.3 = (f32[16]{0:T(128)S(1)}, f32[16]{0:T(128)}, u32[]{:S(2)}) copy-start(f32[16]{0:T(128)} %param.20) | copy-start | bytes 196
  64.9 27.4 %copy-start.2 = (s32[16,6]{0,1:T(8,128)S(1)}, s32[16,6]{0,1:T(8,128)}, u32[]{:S(2)}) copy-start(s32[16,6]{0,1:T(8,128)} %param.19) | copy-start | bytes 1156
  70.6 18.0 %all-to-all-start.3 = ((bf16[16,2,8192]{2,1,0:T(2,128)(2,1)}), bf16[16,2,8192]{2,1,0:T(2,128)(2,1)S(1)}, u32[]{:S(2)}, u32[]{:S(2)}) async-start(bf16[16,2,8192]{2,1,0:T(2,128)(2,1)} %all_to_all.79), calls=%async_computation.3 | async-start | bytes 1048576 | tf_op jit(solution)/shard_map/all_to_all | solution.py:97
  89.0 3.4 %collective-permute-start = (f32[16,8192]{1,0:T(8,128)S(1)}, f32[16,8192]{1,0:T(8,128)S(1)}, u32[]{:S(2)}, u32[]{:S(2)}) collective-permute-start(f32[16,8192]{1,0:T(8,128)S(1)} %convolution_multiply_fusion), channel_id=1, source_target_pairs={{0,2},{2,4},{4,6},{6,8},{8,10},{10,12},{12,14},{14,16},{16,18},{18... | collective-permute-start | bytes 1572872 | tf_op jit(solution)/shard_map/ppermute | solution.py:20
  91.0 3.8 %collective-permute-start.1 = (f32[16,8192]{1,0:T(8,128)S(1)}, f32[16,8192]{1,0:T(8,128)S(1)}, u32[]{:S(2)}, u32[]{:S(2)}) collective-permute-start(f32[16,8192]{1,0:T(8,128)S(1)} %convolution_multiply_fusion), channel_id=1, source_target_pairs={{2,0},{4,2},{6,4},{8,6},{10,8},{12,10},{14,12},{16,14},{18,16},{20... | collective-permute-start | bytes 1572872 | tf_op jit(solution)/shard_map/ppermute | solution.py:23
  136.5 9.7 %copy-start.4 = (s32[16]{0:T(128)S(1)}, s32[16]{0:T(128)}, u32[]{:S(2)}) copy-start(s32[16]{0:T(128)} %param.16) | copy-start | bytes 196
  136.5 9.7 %copy-start.5 = (f32[8]{0:T(128)S(1)}, f32[8]{0:T(128)}, u32[]{:S(2)}) copy-start(f32[8]{0:T(128)} %param.21) | copy-start | bytes 100
  137.4 8.6 %all-to-all-start.6 = ((bf16[8,32,512]{2,0,1:T(8,128)(2,1)}), bf16[8,32,512]{2,0,1:T(8,128)(2,1)S(1)}, u32[]{:S(2)}, u32[]{:S(2)}) async-start(bf16[8,32,512]{2,0,1:T(8,128)(2,1)} %copy.80), calls=%async_computation.6 | async-start | bytes 524288 | tf_op jit(solution)/shard_map/all_to_all | solution.py:135
where the time goes:
time: 149 us; the launch traced here: 147 us
  blocking collectives  36.6 us (25%)
  waiting for transfers between devices  30.7 us (21%)
  local copies, waits for them, and re-layouts  25.1 us (17%)
  starting transfers between devices  24.1 us (16%)
  matrix products  21.1 us (14%)
  other arithmetic  7.08 us (5%)
  loops' own time  1.52 us (1%)
    all_to_all x1, blocking collectives, shards(): lax.all_to_all(reply, 'wide', split_axis=0, concat_axis=0, tiled=True)  28.5 us
    all_to_all x1, waiting for transfers between devices, shards(): lax.all_to_all(outgoing, 'wide', split_axis=0, concat_axis=0, tiled=True)  14.3 us
    dynamic_slice x16, local copies, waits for them, and re-layouts, shards(): lax.map(lambda item: build_tile(item[0], item[1], item[2]), (fine_points,...  13.8 us
    dot_general x8, matrix products, build_tile(): lax.dot_general(left, right, (((1,), (1,)), ((), ())), preferred_element_...  12.4 us
    all_to_all x1, blocking collectives, shards(): lax.all_to_all(per_pair.reshape(grp_pairs, block, basis_count), 'field',...  8.01 us
    all_to_all x1, starting transfers between devices, shards(): lax.all_to_all(slot_ids, 'wide', split_axis=0, concat_axis=0, tiled=True)  6.19 us
    all_to_all x1, waiting for transfers between devices, shards(): lax.all_to_all(contrib, 'field', split_axis=1, concat_axis=0, tiled=True)  5.09 us
    all_to_all x1, waiting for transfers between devices, shards(): lax.all_to_all(slot_ids, 'wide', split_axis=0, concat_axis=0, tiled=True)  4.52 us
  transfers between devices with their start and end apart: 7, of which 6 were waited for; matrix products, arithmetic and copies ran while one was open for 25% of the time, Pallas kernels for 0%

commit v1 on v0

v1 whole, which is shorter than its diff:
```python
import functools
import math

import jax
import jax.numpy as jnp
from jax import lax
from jax.experimental import pallas as pl
from jax.experimental.pallas import tpu as pltpu
from jax.sharding import PartitionSpec as P

NB = 8
DIFFUSE = 0.125
PACK = 16
LANES = 128

NT = (((1,), (1,)), ((), ()))
NN = (((1,), (0,)), ((), ()))


def legendre(points, count):
    values = [jnp.ones_like(points), points]
    for degree in range(1, count - 1):
        values.append(
            ((2 * degree + 1) * points * values[degree] - degree * values[degree - 1])
            / (degree + 1)
        )
    values = values[:count]
    return [values[n] * math.sqrt((2 * n + 1) / 2.0) for n in range(count)]


def fill_table(table_ref, rows_ref, legs, base, here):
    for lane in range(legs.shape[1]):
        cols = slice(lane * LANES, (lane + 1) * LANES)
        first = legs[base, lane, here, :]
        second = legs[base + 1, lane, here, :]
        third = legs[base + 2, lane, here, :]
        for a in range(NB):
            rows_ref[lane, a * NB : (a + 1) * NB, :] = first[a : a + 1, :] * second
        for ab in range(0, NB * NB, 2):
            low = rows_ref[lane, ab : ab + 1, :] * third
            high = rows_ref[lane, ab + 1 : ab + 2, :] * third
            table_ref[ab * NB : (ab + 2) * NB, cols] = jnp.concatenate(
                [low, high], axis=0
            ).astype(jnp.bfloat16)


def project_kernel(fine_ids, points_ref, field_ref, *refs):
    tile_ref, contrib_ref, legs, rows, left, right, sums = refs[-7:]
    pair = pl.program_id(0)
    pairs = points_ref.shape[1]
    block = field_ref.shape[1]

    @pl.when(pair == 0)
    def _():
        for lane in range(legs.shape[1]):
            cols = slice(lane * LANES, (lane + 1) * LANES)
            for coord in range(6):
                values = legendre(points_ref[coord, :, cols], NB)
                for n in range(NB):
                    value = values[n] * points_ref[6, :, cols] if coord == 3 else values[n]
                    legs[coord, lane, pl.ds(n, pairs, stride=NB), :] = value

    here = pl.ds(pl.multiple_of(pair * NB, NB), NB)
    fill_table(right, rows, legs, 0, here)
    fill_table(left, rows, legs, 3, here)
    tile = lax.dot_general(
        left[...], right[...], NT, preferred_element_type=jnp.float32
    ).astype(jnp.bfloat16)
    tile_ref[0] = tile
    contrib = lax.dot_general(
        field_ref[fine_ids[pair]], tile, NT, preferred_element_type=jnp.float32
    )
    for lane in range(sums.shape[0]):
        cols = slice(lane * LANES, (lane + 1) * LANES)
        sums[lane, pl.ds(pair, block, stride=pairs), :] = contrib[:, cols]

    @pl.when(pair == pairs - 1)
    def _():
        for lane in range(sums.shape[0]):
            cols = slice(lane * LANES, (lane + 1) * LANES)
            contrib_ref[:, cols] = sums[lane].astype(jnp.bfloat16)


def project(fine_ids, points, field, tiles, shift, shifts):
    _, pairs, quad = points.shape
    fine_count, block, basis = field.shape
    in_specs = [
        pl.BlockSpec((7, pairs, quad), lambda p, ids: (0, 0, 0)),
        pl.BlockSpec((fine_count, block, basis), lambda p, ids: (0, 0, 0)),
    ]
    operands = [fine_ids, points, field]
    aliases = {}
    if tiles is not None:
        in_specs.append(pl.BlockSpec(memory_space=pl.ANY))
        operands.append(tiles)
        aliases = {3: 0}
    grid_spec = pltpu.PrefetchScalarGridSpec(
        num_scalar_prefetch=1,
        grid=(pairs,),
        in_specs=in_specs,
        out_specs=[
            pl.BlockSpec((1, basis, basis), lambda p, ids: (shift * pairs + p, 0, 0)),
            pl.BlockSpec((block * pairs, basis), lambda p, ids: (0, 0)),
        ],
        scratch_shapes=[
            pltpu.VMEM((6, quad // LANES, pairs * NB, LANES), jnp.float32),
            pltpu.VMEM((quad // LANES, NB * NB, LANES), jnp.float32),
            pltpu.VMEM((basis, quad), jnp.bfloat16),
            pltpu.VMEM((basis, quad), jnp.bfloat16),
            pltpu.VMEM((basis // LANES, block * pairs, LANES), jnp.float32),
        ],
    )
    return pl.pallas_call(
        project_kernel,
        grid_spec=grid_spec,
        out_shape=[
            jax.ShapeDtypeStruct((shifts * pairs, basis, basis), jnp.bfloat16),
            jax.ShapeDtypeStruct((block * pairs, basis), jnp.bfloat16),
        ],
        input_output_aliases=aliases,
        compiler_params=pltpu.CompilerParams(vmem_limit_bytes=32 * 1024 * 1024),
        cost_estimate=pl.CostEstimate(
            flops=2 * pairs * basis * basis * (quad + block),
            bytes_accessed=2 * pairs * basis * basis,
            transcendentals=0,
        ),
        name="project",
    )(*operands)


def combine_kernel(weight_ref, gathered_ref, *refs):
    out_ref = refs[-1]
    weight = weight_ref[...]
    high = weight.astype(jnp.bfloat16)
    low = (weight - high.astype(jnp.float32)).astype(jnp.bfloat16)
    wide, span, basis = gathered_ref.shape
    values = gathered_ref[...].reshape(wide * span, basis)
    total = lax.dot_general(high, values, NN, preferred_element_type=jnp.float32)
    total = total + lax.dot_general(low, values, NN, preferred_element_type=jnp.float32)
    for lane in range(out_ref.shape[0]):
        part = total[:, lane * LANES : (lane + 1) * LANES]
        if len(refs) > 1:
            part = part + refs[0][lane]
        out_ref[lane] = part


def combine(weight, gathered, before):
    wide, rows, basis = gathered.shape
    group, depth = weight.shape
    span = depth // wide
    steps = rows // span
    in_specs = [
        pl.BlockSpec((group, depth), lambda j: (0, 0)),
        pl.BlockSpec((wide, span, basis), lambda j: (0, j, 0)),
    ]
    operands = [weight, gathered]
    if before is not None:
        in_specs.append(pl.BlockSpec((basis // LANES, group, LANES), lambda j: (0, j, 0)))
        operands.append(before)
    return pl.pallas_call(
        combine_kernel,
        grid=(steps,),
        in_specs=in_specs,
        out_specs=pl.BlockSpec((basis // LANES, group, LANES), lambda j: (0, j, 0)),
        out_shape=jax.ShapeDtypeStruct((basis // LANES, steps * group, LANES), jnp.float32),
        compiler_params=pltpu.CompilerParams(vmem_limit_bytes=32 * 1024 * 1024),
        cost_estimate=pl.CostEstimate(
            flops=4 * steps * group * depth * basis,
            bytes_accessed=2 * wide * rows * basis,
            transcendentals=0,
        ),
        name="combine",
    )(*operands)


def restrict_kernel(fine_ids, inverse, smooth_ref, tile_ref, coarse_ref, fine_ref, sums):
    pair = pl.program_id(0)
    coarse_count, block, _ = coarse_ref.shape
    fine_count = fine_ref.shape[0]
    targets = smooth_ref.shape[1] // block

    def picked(target):
        parts = [
            smooth_ref[lane, pl.ds(target, block, stride=targets), :]
            for lane in range(smooth_ref.shape[0])
        ]
        return jnp.concatenate(parts, axis=1).astype(jnp.bfloat16)

    @pl.when(pair == 0)
    def _():
        sums[...] = jnp.zeros_like(sums)
        for c in range(coarse_count):
            coarse_ref[c] = picked(c)

    term = lax.dot_general(picked(coarse_count + pair), tile_ref[0], NN, preferred_element_type=jnp.float32)
    sums[fine_ids[pair]] += term.astype(jnp.bfloat16).astype(jnp.float32)

    @pl.when(pair == pl.num_programs(0) - 1)
    def _():
        for e in range(fine_count):
            fine_ref[e] = (inverse[e] * sums[e]).astype(jnp.bfloat16)


def restrict(fine_ids, inverse, smooth, tiles, coarse_count, block):
    pairs, basis, _ = tiles.shape
    fine_count = inverse.shape[0]
    grid_spec = pltpu.PrefetchScalarGridSpec(
        num_scalar_prefetch=2,
        grid=(pairs,),
        in_specs=[
            pl.BlockSpec(smooth.shape, lambda p, ids, inv: (0, 0, 0)),
            pl.BlockSpec((1, basis, basis), lambda p, ids, inv: (p, 0, 0)),
        ],
        out_specs=[
            pl.BlockSpec((coarse_count, block, basis), lambda p, ids, inv: (0, 0, 0)),
            pl.BlockSpec((fine_count, block, basis), lambda p, ids, inv: (0, 0, 0)),
        ],
        scratch_shapes=[pltpu.VMEM((fine_count, block, basis), jnp.float32)],
    )
    return pl.pallas_call(
        restrict_kernel,
        grid_spec=grid_spec,
        out_shape=[
            jax.ShapeDtypeStruct((coarse_count, block, basis), jnp.bfloat16),
            jax.ShapeDtypeStruct((fine_count, block, basis), jnp.bfloat16),
        ],
        compiler_params=pltpu.CompilerParams(vmem_limit_bytes=32 * 1024 * 1024),
        cost_estimate=pl.CostEstimate(
            flops=2 * pairs * basis * basis * block,
            bytes_accessed=2 * pairs * basis * basis,
            transcendentals=0,
        ),
        name="restrict",
    )(fine_ids, inverse, smooth, tiles)


def shards(
    fine_field_in,
    fine_points,
    coarse_points,
    quad_weights,
    pair_fine,
    pair_owner,
    pair_coarse,
    coarse_faces,
    coarse_inv_mass,
    fine_inv_mass,
):
    nwide = lax.axis_size("wide")
    nfield = lax.axis_size("field")
    wide_index = lax.axis_index("wide")
    field_index = lax.axis_index("field")
    pairs = fine_points.shape[0]
    block = fine_field_in.shape[1]
    coarse_count = coarse_inv_mass.shape[0]
    faces = coarse_faces.shape[1]
    all_coarse = nwide * coarse_count

    own = jnp.concatenate(
        [
            jnp.swapaxes(fine_points, 0, 1),
            jnp.swapaxes(coarse_points, 0, 1),
            quad_weights[None],
        ],
        axis=0,
    )
    points = [own]
    for shift in range(1, nfield):
        perm = [((i + shift) % nfield, i) for i in range(nfield)]
        points.append(lax.ppermute(own, "field", perm))

    def rolled(ids):
        return jnp.roll(ids.reshape(nfield, pairs), -field_index, axis=0)

    fine_ids = rolled(pair_fine)
    coarse_ids = rolled(pair_owner[:, 0] * coarse_count + pair_coarse)
    facts = jnp.concatenate(
        [
            coarse_ids.reshape(-1).astype(jnp.float32),
            coarse_faces.reshape(-1).astype(jnp.float32),
            coarse_inv_mass,
        ]
    )
    facts = lax.all_gather(facts, "wide", axis=0)
    count = nfield * pairs
    every_pair = facts[:, :count].astype(jnp.int32)
    every_face = facts[:, count : count + coarse_count * faces].astype(jnp.int32)
    every_face = every_face.reshape(all_coarse, faces)
    every_mass = facts[:, count + coarse_count * faces :].reshape(all_coarse)

    names = jnp.arange(all_coarse, dtype=jnp.int32)
    pair_mass = jnp.sum(
        jnp.where(every_pair[:, :, None] == names[None, None, :], every_mass[None, None, :], 0.0),
        axis=2,
    )
    pair_faces = jnp.sum(
        jnp.where(
            coarse_ids.reshape(-1)[:, None, None] == names[None, :, None], every_face[None], 0
        ),
        axis=1,
    )
    target = jnp.concatenate([names[:coarse_count] + wide_index * coarse_count, coarse_ids.reshape(-1)])
    target_faces = jnp.concatenate([coarse_faces, pair_faces], axis=0)
    hits = (1.0 - faces * DIFFUSE) * (
        target[:, None, None] == every_pair[None]
    ).astype(jnp.float32)
    for face in range(faces):
        hits = hits + DIFFUSE * (target_faces[:, face, None, None] == every_pair[None]).astype(
            jnp.float32
        )
    weight = hits * pair_mass[None]
    targets = coarse_count + count
    fold = max(1, PACK // pairs)
    weight = weight.reshape(targets, nwide, nfield, pairs)
    same = jnp.eye(fold, dtype=jnp.float32)
    weights = [
        (same[:, None, None, :, None] * weight[None, :, :, shift, None, :]).reshape(
            fold * targets, nwide * fold * pairs
        )
        for shift in range(nfield)
    ]

    tiles = None
    totals = []
    total = None
    for shift in range(nfield):
        tiles, contrib = project(
            fine_ids[shift], points[shift], fine_field_in, tiles, shift, nfield
        )
        if shift >= 2:
            contrib, _ = lax.optimization_barrier((contrib, totals[shift - 2]))
        gathered = lax.all_gather(contrib, "wide", axis=0)
        total = combine(weights[shift], gathered, total)
        totals.append(total)
    return restrict(
        fine_ids.reshape(-1),
        fine_inv_mass,
        total,
        tiles,
        coarse_count,
        block,
    )


def solution(mesh):
    placed = (
        P("wide", "field", None),
        P(("wide", "field"), None, None),
        P(("wide", "field"), None, None),
        P(("wide", "field"), None),
        P("wide"),
        P("wide", None),
        P("wide"),
        P("wide", None),
        P("wide"),
        P("wide"),
    )
    return jax.shard_map(
        shards,
        mesh=mesh,
        in_specs=placed,
        out_specs=(P("wide", "field", None), P("wide", "field", None)),
        check_vma=False,
    )
```

time: 149 us -> 130 us (0.87)
  Pallas kernels: 0 us -> 29.1 us
  matrix products: 21.1 us -> 0 us
  starting transfers between devices: 24.1 us -> 3.1 us
  blocking collectives: 36.6 us -> 21.8 us
  between operations: 0.9 us -> 14.2 us
  waiting for transfers between devices: 30.7 us -> 38.9 us
  local copies, waits for them, and re-layouts: 25.1 us -> 19.8 us
  other arithmetic: 7.08 us -> 2.33 us
  loops' own time: 1.52 us -> 0 us
    all_to_all x2 -> x0, blocking collectives: 36.6 us -> none  [the longest x1 28.5 us: shards(): lax.all_to_all(reply, 'wide', split_axis=0, concat_axis=0, tiled=True)]
    all_gather x0 -> x2, waiting for transfers between devices: none -> 33.2 us  [shards(): gathered = lax.all_gather(contrib, 'wide', axis=0)]
    pallas_call x0 -> x5, Pallas kernels: none -> 29.1 us  [the longest x2 20.3 us: project(): pl.pallas_call(project_kernel, grid_spec=grid_spec, out_shape=[jax.ShapeD...]
    all_to_all x5 -> x0, waiting for transfers between devices: 28.3 us -> none  [the longest x1 14.3 us: shards(): lax.all_to_all(outgoing, 'wide', split_axis=0, concat_axis=0, tiled=True)]
    all_gather x0 -> x1, blocking collectives: none -> 21.8 us  [shards(): facts = lax.all_gather(facts, 'wide', axis=0)]
    dot_general x16 -> x0, matrix products: 21.1 us -> none  [the longest x8 12.4 us: build_tile(): lax.dot_general(left, right, (((1,), (1,)), ((), ())), preferred_element_...]
    all_to_all x5 -> x0, starting transfers between devices: 20.9 us -> none  [the longest x1 6.19 us: shards(): lax.all_to_all(slot_ids, 'wide', split_axis=0, concat_axis=0, tiled=True)]
    unnamed x19 -> x26, local copies, waits for them, and re-layouts: 1.92 us -> 17.5 us
  transfers between devices with their start and end apart: 7 -> 3, of which waited for: 6 -> 2; matrix products, arithmetic and copies ran while one was open for 25% -> 2% of each run, Pallas kernels for 0% -> 9%
where the time goes in v1:
time: 130 us; the launch traced here: 129 us
  waiting for transfers between devices  38.9 us (30%)
  Pallas kernels  29.1 us (22%)
  blocking collectives  21.8 us (17%)
  local copies, waits for them, and re-layouts  19.8 us (15%)
  between operations  14.2 us (11%)
  starting transfers between devices  3.1 us (2%)
  other arithmetic  2.33 us (2%)
    all_gather x2, waiting for transfers between devices, shards(): gathered = lax.all_gather(contrib, 'wide', axis=0)  33.2 us
    all_gather x1, blocking collectives, shards(): facts = lax.all_gather(facts, 'wide', axis=0)  21.8 us
    pallas_call x2, Pallas kernels, project(): pl.pallas_call(project_kernel, grid_spec=grid_spec, out_shape=[jax.ShapeD...  20.3 us
    unnamed x26, local copies, waits for them, and re-layouts  17.5 us
    ppermute x1, waiting for transfers between devices, shards(): points.append(lax.ppermute(own, 'field', perm))  5.59 us
    pallas_call x1, Pallas kernels, restrict(): pl.pallas_call(restrict_kernel, grid_spec=grid_spec, out_shape=[jax.Shape...  4.7 us
    pallas_call x2, Pallas kernels, combine(): pl.pallas_call(combine_kernel, grid=(steps,), in_specs=in_specs, out_spec...  4.08 us
    ppermute x1, starting transfers between devices, shards(): points.append(lax.ppermute(own, 'field', perm))  3.02 us
  transfers between devices with their start and end apart: 3, of which 2 were waited for; matrix products, arithmetic and copies ran while one was open for 2% of the time, Pallas kernels for 9%

profile of v1, /device:TPU:0, one launch (start us, length us, event | category | flops | bytes accessed | tf_op | source)
XLA Modules:
  0.0 129.3 jit_solution(9644321493811515801)
XLA Ops:
  7.2 0.0 all-gather.9.cloned.1.call-start
  7.2 0.0 copy-start.8
  7.2 0.8 reshape.90
  8.1 1.0 pad_maximum_fusion.points_ref
  9.0 0.0 copy-start.7
  9.1 0.9 copy-done.7
  9.9 10.2 %project.2 = (bf16[16,512,512]{2,1,0:T(8,128)(2,1)S(1)}, bf16[128,512]{1,0:T(8,128)(2,1)}) custom-call(s32[8]{0:T(128)S(1)} %get-tuple-element.23.fine_ids, f32[7,8,1024]{2,1,0:T(8,128)S(1)} %pad_maximum_fusion.points_ref, bf16[8,16,512]{2,1,0:T(8,128)(2,1)S(1)} %copy-done.7), custom_call_target="tpu_custom_call" | custom-call | flops 4362076160 | bytes 4194304 | tf_op jit(solution)/shard_map/project/pallas_call | solution.py:113
  20.1 0.0 copy-start
  20.1 3.2 %copy-done = bf16[16,512,512]{2,1,0:T(8,128)(2,1)} copy-done((bf16[16,512,512]{2,1,0:T(8,128)(2,1)}, bf16[16,512,512]{2,1,0:T(8,128)(2,1)S(1)}, u32[]{:S(2)}) %copy-start) | copy-done | bytes 8388632
  23.4 0.0 copy-start.11
  23.4 0.0 copy-start.12
  23.4 0.0 copy-start.9
  23.4 0.0 copy-start.10
  23.4 0.0 all-gather.9.cloned.1.call-update
  23.4 0.0 all-gather.7.cloned.1.call-start
  23.4 3.0 %collective-permute-start = (f32[7,8,1024]{2,1,0:T(8,128)S(1)}, f32[7,8,1024]{2,1,0:T(8,128)S(1)}, u32[]{:S(2)}, u32[]{:S(2)}) collective-permute-start(f32[7,8,1024]{2,1,0:T(8,128)S(1)} %pad_maximum_fusion.points_ref), channel_id=1, source_target_pairs={{1,0},{0,1},{3,2},{2,3},{5,4},{4,5},{7,6},{6,7},{9,8},{8,9},{11,10... | collective-permute-start | bytes 688136 | tf_op jit(solution)/shard_map/ppermute | solution.py:270
  26.5 5.6 %collective-permute-done.points_ref = f32[7,8,1024]{2,1,0:T(8,128)S(1)} collective-permute-done((f32[7,8,1024]{2,1,0:T(8,128)S(1)}, f32[7,8,1024]{2,1,0:T(8,128)S(1)}, u32[]{:S(2)}, u32[]{:S(2)}) %collective-permute-start) | collective-permute-done | bytes 229408 | tf_op jit(solution)/shard_map/ppermute | solution.py:270
  32.1 0.0 copy-done.8
  32.1 3.5 %copy-done.1 = bf16[16,512,512]{2,1,0:T(8,128)(2,1)S(1)} copy-done((bf16[16,512,512]{2,1,0:T(8,128)(2,1)S(1)}, bf16[16,512,512]{2,1,0:T(8,128)(2,1)}, u32[]{:S(2)}) %copy-start.1) | copy-done | bytes 8388632
  35.6 10.2 %project.3 = (bf16[16,512,512]{2,1,0:T(8,128)(2,1)S(1)}, bf16[128,512]{1,0:T(8,128)(2,1)}) custom-call(s32[8]{0:T(128)S(1)} %get-tuple-element.24.fine_ids, f32[7,8,1024]{2,1,0:T(8,128)S(1)} %collective-permute-done.points_ref, bf16[8,16,512]{2,1,0:T(8,128)(2,1)S(1)} %copy-done.8, bf16[16,512,512]{2,1,0:T(8,128)(2,1)S(1)} %copy-done.1), custom_call_target="tpu_custom_call", output_to_operand_aliasing={{0}: (3, {})} | custom-call | flops 4362076160 | bytes 4194304 | tf_op jit(solution)/shard_map/project/pallas_call | solution.py:113
  45.8 3.2 %copy-done.2 = bf16[16,512,512]{2,1,0:T(8,128)(2,1)} copy-done((bf16[16,512,512]{2,1,0:T(8,128)(2,1)}, bf16[16,512,512]{2,1,0:T(8,128)(2,1)S(1)}, u32[]{:S(2)}) %copy-start.2) | copy-done | bytes 8388632
  49.0 0.0 all-gather.7.cloned.1.call-update
  49.0 0.1 reshape.91.fine_ids
  49.1 0.0 copy-done.11
  49.1 0.0 copy-done.12
  49.1 0.1 reshape.92
  49.2 0.1 reshape.93
  49.3 0.0 copy-done.9
  49.3 0.1 copy.49
  49.4 0.1 convert_element_type.34
  49.5 0.0 copy-done.10
  49.5 0.1 maximum_bitcast_fusion
  49.6 21.8 %all-gather.3 = f32[16,1,128]{2,1,0:T(1,128)S(1)} all-gather(f32[1,1,128]{2,1,0:T(1,128)S(1)} %maximum_bitcast_fusion), channel_id=2, replica_groups=mesh['wide'=16,'field'=2] {'wide'}, dimensions={0}, use_global_device_ids=true | all-gather | bytes 8704 | tf_op jit(solution)/shard_map/all_gather | solution.py:284
  71.4 0.1 slice_convert_fusion
  71.5 0.1 broadcast_in_dim.54
  71.6 0.1 copy.52
  71.7 0.1 slice_convert_fusion.1
  71.7 0.1 broadcast_in_dim.57
  71.8 0.1 copy.50
  71.9 0.2 select_reduce_fusion
  72.1 0.1 copy.53
  72.2 0.1 copy.54
  72.2 0.1 copy.51
  72.3 0.1 pad_add_fusion.3
  72.4 0.1 iota_compare_fusion.1
  72.5 0.2 select_reduce_fusion.1
  72.7 0.1 pad_add_fusion
  72.8 0.2 add_multiply_fusion
  73.0 0.3 broadcast_multiply_fusion
  73.3 0.2 mul.104
  73.5 0.1 copy.55.weight_ref
  73.5 0.2 mul.100
  73.7 0.1 copy.56.weight_ref
  73.8 0.0 all-gather.9.cloned.1.call-done
  73.8 0.0 copy-start.4
  73.8 1.6 %copy-done.4 = bf16[2048,512]{1,0:T(8,128)(2,1)S(1)} copy-done((bf16[2048,512]{1,0:T(8,128)(2,1)S(1)}, bf16[2048,512]{1,0:T(8,128)(2,1)}, u32[]{:S(2)}) %copy-start.4) | copy-done | bytes 2097176
  75.4 2.0 %combine.2.refs_0_ = f32[4,512,128]{2,1,0:T(8,128)S(1)} custom-call(f32[64,256]{1,0:T(8,128)S(1)} %copy.55.weight_ref, bf16[16,128,512]{2,1,0:T(8,128)(2,1)S(1)} %bitcast.36), custom_call_target="tpu_custom_call" | custom-call | flops 268435456 | bytes 2097152 | tf_op jit(solution)/shard_map/combine/pallas_call | solution.py:160
  77.4 33.2 %all-gather.7.cloned.1.call-done = bf16[2048,512]{1,0:T(8,128)(2,1)} async-done(((bf16[128,512]{1,0:T(8,128)(2,1)}), bf16[2048,512]{1,0:T(8,128)(2,1)}) %all-gather.7.cloned.1.call-update) | async-done | bytes 2097168 | tf_op jit(solution)/shard_map/all_gather | solution.py:332
  110.7 1.6 %copy-done.5 = bf16[2048,512]{1,0:T(8,128)(2,1)S(1)} copy-done((bf16[2048,512]{1,0:T(8,128)(2,1)S(1)}, bf16[2048,512]{1,0:T(8,128)(2,1)}, u32[]{:S(2)}) %copy-start.5) | copy-done | bytes 2097176
  112.3 2.1 %combine.3.smooth_ref = f32[4,512,128]{2,1,0:T(8,128)S(1)} custom-call(f32[64,256]{1,0:T(8,128)S(1)} %copy.56.weight_ref, bf16[16,128,512]{2,1,0:T(8,128)(2,1)S(1)} %bitcast.37, f32[4,512,128]{2,1,0:T(8,128)S(1)} %combine.2.refs_0_), custom_call_target="tpu_custom_call" | custom-call | flops 268435456 | bytes 2097152 | tf_op jit(solution)/shard_map/combine/pallas_call | solution.py:160
  114.3 0.0 copy-done.6
  114.4 0.0 copy-start.3
  114.4 3.4 %copy-done.3 = bf16[16,512,512]{2,1,0:T(8,128)(2,1)S(1)} copy-done((bf16[16,512,512]{2,1,0:T(8,128)(2,1)S(1)}, bf16[16,512,512]{2,1,0:T(8,128)(2,1)}, u32[]{:S(2)}) %copy-start.3) | copy-done | bytes 8388632
  117.7 4.7 %restrict.1 = (bf16[16,16,512]{2,1,0:T(8,128)(2,1)}, bf16[8,16,512]{2,1,0:T(8,128)(2,1)}) custom-call(s32[16]{0:T(128)S(1)} %reshape.91.fine_ids, f32[8]{0:T(128)S(1)} %copy-done.6, f32[4,512,128]{2,1,0:T(8,128)S(1)} %combine.3.smooth_ref, bf16[16,512,512]{2,1,0:T(8,128)(2,1)S(1)} %copy-done.3), custom_call_target="tpu_custom_call" | custom-call | flops 134217728 | bytes 8388608 | tf_op jit(solution)/shard_map/restrict/pallas_call | solution.py:220
  (17 shorter events, 0.1 us)
Async XLA Ops:
  7.2 66.7 %all-gather.9.cloned.1.call-start = ((), (), s32[]{:S(2)}) async-start(), calls=%async_computation.1 | async-start | bytes 2228224 | tf_op jit(solution)/shard_map/all_gather | solution.py:332
  7.2 24.8 %copy-start.8 = (bf16[8,16,512]{2,1,0:T(8,128)(2,1)S(1)}, bf16[8,16,512]{2,1,0:T(8,128)(2,1)}, u32[]{:S(2)}) copy-start(bf16[8,16,512]{2,1,0:T(8,128)(2,1)} %field_ref.3) | copy-start | bytes 393220
  9.0 0.9 copy-start.7
  20.1 3.2 %copy-start = (bf16[16,512,512]{2,1,0:T(8,128)(2,1)}, bf16[16,512,512]{2,1,0:T(8,128)(2,1)S(1)}, u32[]{:S(2)}) copy-start(bf16[16,512,512]{2,1,0:T(8,128)(2,1)S(1)} %get-tuple-element.7.refs_0_) | copy-start | bytes 25165828
  23.4 25.8 %copy-start.11 = (s32[16]{0:T(128)S(1)}, s32[16]{0:T(128)}, u32[]{:S(2)}) copy-start(s32[16]{0:T(128)} %param.18) | copy-start | bytes 196
  23.4 25.8 %copy-start.12 = (s32[16,1]{0,1:T(1,128)S(1)}, s32[16,1]{0,1:T(1,128)}, u32[]{:S(2)}) copy-start(s32[16,1]{0,1:T(1,128)} %param.17) | copy-start | bytes 196
  23.4 26.0 %copy-start.9 = (s32[16,6]{0,1:T(8,128)S(1)}, s32[16,6]{0,1:T(8,128)}, u32[]{:S(2)}) copy-start(s32[16,6]{0,1:T(8,128)} %param.19) | copy-start | bytes 1156
  23.4 26.1 %copy-start.10 = (f32[16]{0:T(128)S(1)}, f32[16]{0:T(128)}, u32[]{:S(2)}) copy-start(f32[16]{0:T(128)} %param.20) | copy-start | bytes 196
  23.4 87.3 %all-gather.7.cloned.1.call-start = ((), (), s32[]{:S(2)}) async-start(), calls=%async_computation | async-start | bytes 2228224 | tf_op jit(solution)/shard_map/all_gather | solution.py:332
  23.4 8.6 %collective-permute-start = (f32[7,8,1024]{2,1,0:T(8,128)S(1)}, f32[7,8,1024]{2,1,0:T(8,128)S(1)}, u32[]{:S(2)}, u32[]{:S(2)}) collective-permute-start(f32[7,8,1024]{2,1,0:T(8,128)S(1)} %pad_maximum_fusion.points_ref), channel_id=1, source_target_pairs={{1,0},{0,1},{3,2},{2,3},{5,4},{4,5},{7,6},{6,7},{9,8},{8,9},{11,10... | collective-permute-start | bytes 688136 | tf_op jit(solution)/shard_map/ppermute | solution.py:270
  32.1 3.5 %copy-start.1 = (bf16[16,512,512]{2,1,0:T(8,128)(2,1)S(1)}, bf16[16,512,512]{2,1,0:T(8,128)(2,1)}, u32[]{:S(2)}) copy-start(bf16[16,512,512]{2,1,0:T(8,128)(2,1)} %copy-done) | copy-start | bytes 25165828
  45.8 3.2 %copy-start.2 = (bf16[16,512,512]{2,1,0:T(8,128)(2,1)}, bf16[16,512,512]{2,1,0:T(8,128)(2,1)S(1)}, u32[]{:S(2)}) copy-start(bf16[16,512,512]{2,1,0:T(8,128)(2,1)S(1)} %get-tuple-element.10.tile_ref) | copy-start | bytes 25165828
  49.0 65.3 %copy-start.6 = (f32[8]{0:T(128)S(1)}, f32[8]{0:T(128)}, u32[]{:S(2)}) copy-start(f32[8]{0:T(128)} %inverse.1) | copy-start | bytes 100
  73.8 1.6 %copy-start.4 = (bf16[2048,512]{1,0:T(8,128)(2,1)S(1)}, bf16[2048,512]{1,0:T(8,128)(2,1)}, u32[]{:S(2)}) copy-start(bf16[2048,512]{1,0:T(8,128)(2,1)} %all-gather.9.cloned.1.call-done) | copy-start | bytes 6291460
  110.7 1.6 %copy-start.5 = (bf16[2048,512]{1,0:T(8,128)(2,1)S(1)}, bf16[2048,512]{1,0:T(8,128)(2,1)}, u32[]{:S(2)}) copy-start(bf16[2048,512]{1,0:T(8,128)(2,1)} %all-gather.7.cloned.1.call-done) | copy-start | bytes 6291460
  114.4 3.4 %copy-start.3 = (bf16[16,512,512]{2,1,0:T(8,128)(2,1)S(1)}, bf16[16,512,512]{2,1,0:T(8,128)(2,1)}, u32[]{:S(2)}) copy-start(bf16[16,512,512]{2,1,0:T(8,128)(2,1)} %copy-done.2) | copy-start | bytes 25165828
Sparse Core Ops, SparseCore 0:
  23.5 44.1 all-gather.8
  70.4 40.2 all-gather.6

commit v2 on v0

v2 whole, which is shorter than its diff:
```python
import functools
import math

import jax
import jax.numpy as jnp
from jax import lax
from jax.experimental import pallas as pl
from jax.experimental.pallas import tpu as pltpu
from jax.sharding import PartitionSpec as P

NB = 8
DIFFUSE = 0.125
LANES = 128

NT = (((1,), (1,)), ((), ()))
NN = (((1,), (0,)), ((), ()))
TN = (((0,), (0,)), ((), ()))

SCALAR = pl.BlockSpec(memory_space=pltpu.SMEM)
VECTOR = pl.BlockSpec(memory_space=pltpu.VMEM)


def legendre(points, count):
    values = [jnp.ones_like(points), points]
    for degree in range(1, count - 1):
        values.append(
            ((2 * degree + 1) * points * values[degree] - degree * values[degree - 1])
            / (degree + 1)
        )
    values = values[:count]
    return [values[n] * math.sqrt((2 * n + 1) / 2.0) for n in range(count)]


def lanes(index):
    return slice(index * LANES, (index + 1) * LANES)


def fill_table(table_ref, rows_ref, legs, base, pair):
    here = pl.ds(pl.multiple_of(pair * NB, NB), NB)
    for lane in range(legs.shape[1]):
        first = legs[base, lane, here, :]
        second = legs[base + 1, lane, here, :]
        third = legs[base + 2, lane, here, :]
        for a in range(NB):
            rows_ref[lane, a * NB : (a + 1) * NB, :] = first[a : a + 1, :] * second
        for ab in range(0, NB * NB, 2):
            low = rows_ref[lane, ab : ab + 1, :] * third
            high = rows_ref[lane, ab + 1 : ab + 2, :] * third
            table_ref[ab * NB : (ab + 2) * NB, lanes(lane)] = jnp.concatenate(
                [low, high], axis=0
            ).astype(jnp.bfloat16)


def facts(owner_ref, coarse_ref, faces_ref, inverse_ref, rows, pair_at):
    elements, faces = faces_ref.shape
    lane = lax.broadcasted_iota(jnp.int32, (1, LANES), 1)
    lines = []
    for row in range(rows):
        line = jnp.zeros((1, LANES), jnp.float32)
        if row < coarse_ref.shape[0]:
            pair = pair_at(row)
            line = jnp.where(lane == 0, owner_ref[pair, 0].astype(jnp.float32), line)
            line = jnp.where(lane == 1, coarse_ref[pair].astype(jnp.float32), line)
        if row < elements:
            for face in range(faces):
                name = faces_ref[row, face]
                outer = lax.div(name, jnp.int32(elements))
                inner = name - outer * elements
                line = jnp.where(lane == 2 + 2 * face, outer.astype(jnp.float32), line)
                line = jnp.where(lane == 3 + 2 * face, inner.astype(jnp.float32), line)
            rest = jnp.full((1, LANES), inverse_ref[row], jnp.float32)
            for part in range(3):
                head = rest.astype(jnp.bfloat16).astype(jnp.float32)
                line = jnp.where(lane == 2 + 2 * faces + part, head, line)
                rest = rest - head
        lines.append(line)
    return jnp.concatenate(lines, axis=0).astype(jnp.bfloat16)


def project_kernel(shift, shifts, last, place_ref, fine_ref, *refs):
    if last:
        owner_ref, coarse_ref, faces_ref, inverse_ref = refs[:4]
        refs = refs[4:]
    points_ref, field_ref = refs[:2]
    before = refs[2 : len(refs) - 12]
    tile_ref, out_ref, legs, sums = refs[-12:-8]
    rows, tables = refs[-8:-4], refs[-4:]
    pairs = points_ref.shape[1]
    block = field_ref.shape[1]

    def pair_at(step, pair):
        part = place_ref[0] + step
        return jnp.where(part >= shifts, part - shifts, part) * pairs + pair

    for lane in range(legs.shape[1]):
        for coord in range(6):
            values = legendre(points_ref[coord, :, lanes(lane)], NB)
            for n in range(NB):
                value = values[n] * points_ref[6, :, lanes(lane)] if coord == 3 else values[n]
                legs[coord, lane, pl.ds(n, pairs, stride=NB), :] = value

    def fill(pair, slot):
        fill_table(tables[2 * slot], rows[2 * slot], legs, 0, pair)
        fill_table(tables[2 * slot + 1], rows[2 * slot + 1], legs, 3, pair)

    def apply(pair, slot):
        tile = lax.dot_general(
            tables[2 * slot + 1][...], tables[2 * slot][...], NT, preferred_element_type=jnp.float32
        ).astype(jnp.bfloat16)
        tile_ref[pair] = tile
        contrib = lax.dot_general(
            field_ref[fine_ref[pair_at(shift, pair)]], tile, NT, preferred_element_type=jnp.float32
        )
        for lane in range(sums.shape[0]):
            sums[lane, pl.ds(pair, block, stride=pairs), :] = contrib[:, lanes(lane)]

    fill(0, 0)

    @pl.loop(0, pairs // 2)
    def _(step):
        pair = 2 * step
        fill(pair + 1, 1)
        apply(pair, 0)
        fill(jnp.minimum(pair + 2, pairs - 1), 0)
        apply(pair + 1, 1)

    if not last:
        out_ref[...] = sums[...]
        return
    wide, total, span = out_ref.shape
    width = span - LANES
    across = sums.shape[0]
    extra = facts(
        owner_ref,
        coarse_ref,
        faces_ref,
        inverse_ref,
        total,
        lambda row: pair_at(row // pairs, row % pairs),
    )
    sources = list(before) + [sums]
    for dest in range(wide):
        for piece in range(width // LANES):
            column = dest * (width // LANES) + piece
            row, lane = divmod(column, across)
            parts = [s[lane, row * pairs : (row + 1) * pairs, :] for s in sources]
            out_ref[dest, :, lanes(piece)] = jnp.concatenate(parts, axis=0).astype(jnp.bfloat16)
        out_ref[dest, :, lanes(width // LANES)] = extra


def project(place, fine_ids, scalars, points, field, before, shift, shifts, wide):
    _, pairs, quad = points.shape
    fine_count, block, basis = field.shape
    last = shift == shifts - 1
    across = basis // LANES
    if last:
        out = jax.ShapeDtypeStruct(
            (wide, shifts * pairs, block * basis // wide + LANES), jnp.bfloat16
        )
    else:
        out = jax.ShapeDtypeStruct((across, block * pairs, LANES), jnp.float32)
    operands = [place, fine_ids]
    if last:
        operands += scalars
    specs = [SCALAR] * len(operands)
    vectors = [points, field] + (before if last else [])
    return pl.pallas_call(
        functools.partial(project_kernel, shift, shifts, last),
        in_specs=specs + [VECTOR] * len(vectors),
        out_specs=[VECTOR, VECTOR],
        out_shape=[jax.ShapeDtypeStruct((pairs, basis, basis), jnp.bfloat16), out],
        scratch_shapes=[
            pltpu.VMEM((6, quad // LANES, pairs * NB, LANES), jnp.float32),
            pltpu.VMEM((across, block * pairs, LANES), jnp.float32),
        ]
        + [pltpu.VMEM((quad // LANES, NB * NB, LANES), jnp.float32)] * 4
        + [pltpu.VMEM((basis, quad), jnp.bfloat16)] * 4,
        compiler_params=pltpu.CompilerParams(vmem_limit_bytes=24 * 1024 * 1024),
        cost_estimate=pl.CostEstimate(
            flops=2 * pairs * basis * basis * (quad + block),
            bytes_accessed=2 * pairs * basis * basis,
            transcendentals=0,
        ),
        name="project",
    )(*operands, *vectors)


def coarse_kernel(faces, elements, arrived_ref, out_ref, pick, near, moved):
    wide, rows, span = arrived_ref.shape
    width = span - LANES
    count = wide * elements
    name = lax.broadcasted_iota(jnp.int32, (rows, count), 1).astype(jnp.float32)
    inverse = []
    for source in range(wide):
        fact = arrived_ref[source, :, width:].astype(jnp.float32)
        moved[source * rows : (source + 1) * rows, :] = arrived_ref[source, :, :width]
        index = fact[:, 0:1] * elements + fact[:, 1:2]
        pick[source * rows : (source + 1) * rows, :] = (index == name).astype(jnp.float32).astype(
            jnp.bfloat16
        )
        hits = jnp.zeros((elements, count), jnp.float32)
        for face in range(faces):
            index = fact[:elements, 2 + 2 * face : 3 + 2 * face] * elements
            index = index + fact[:elements, 3 + 2 * face : 4 + 2 * face]
            hits = hits + (index == name[:elements]).astype(jnp.float32)
        near[source * elements : (source + 1) * elements, :] = hits.astype(jnp.bfloat16)
        first = 2 + 2 * faces
        inverse.append(
            fact[:elements, first : first + 1]
            + fact[:elements, first + 1 : first + 2]
            + fact[:elements, first + 2 : first + 3]
        )
    load = lax.dot_general(pick[...], moved[...], TN, preferred_element_type=jnp.float32)
    solved = jnp.concatenate(inverse, axis=0) * load
    high = solved.astype(jnp.bfloat16)
    low = (solved - high.astype(jnp.float32)).astype(jnp.bfloat16)
    beside = lax.dot_general(near[...], high, NN, preferred_element_type=jnp.float32)
    beside = beside + lax.dot_general(near[...], low, NN, preferred_element_type=jnp.float32)
    smooth = (solved + DIFFUSE * (beside - float(faces) * solved)).astype(jnp.bfloat16)
    reply = lax.dot_general(pick[...], smooth, NN, preferred_element_type=jnp.float32).astype(
        jnp.bfloat16
    )
    for dest in range(wide):
        out_ref[dest, :elements, :] = smooth[dest * elements : (dest + 1) * elements, :]
        out_ref[dest, elements:, :] = reply[dest * rows : (dest + 1) * rows, :]


def coarse_stage(arrived, elements, faces):
    wide, rows, span = arrived.shape
    width = span - LANES
    count = wide * elements
    return pl.pallas_call(
        functools.partial(coarse_kernel, faces, elements),
        in_specs=[VECTOR],
        out_specs=VECTOR,
        out_shape=jax.ShapeDtypeStruct((wide, elements + rows, width), jnp.bfloat16),
        scratch_shapes=[
            pltpu.VMEM((wide * rows, count), jnp.bfloat16),
            pltpu.VMEM((count, count), jnp.bfloat16),
            pltpu.VMEM((wide * rows, width), jnp.bfloat16),
        ],
        compiler_params=pltpu.CompilerParams(vmem_limit_bytes=48 * 1024 * 1024),
        cost_estimate=pl.CostEstimate(
            flops=8 * count * wide * rows * width,
            bytes_accessed=4 * wide * rows * width,
            transcendentals=0,
        ),
        name="coarse_stage",
    )(arrived)


def restrict_kernel(shifts, place_ref, fine_ids, inverse_ref, back_ref, *refs):
    tiles = refs[:shifts]
    coarse_ref, fine_ref, rows, sums = refs[shifts:]
    wide, targets, width = back_ref.shape
    elements, block, _ = coarse_ref.shape
    fine_count = fine_ref.shape[0]
    across = rows.shape[0]
    for source in range(wide):
        for piece in range(width // LANES):
            row, lane = divmod(source * (width // LANES) + piece, across)
            rows[lane, row * targets : (row + 1) * targets, :] = back_ref[
                source, :, lanes(piece)
            ].astype(jnp.float32)

    def picked(target):
        parts = [rows[lane, pl.ds(target, block, stride=targets), :] for lane in range(across)]
        return jnp.concatenate(parts, axis=1).astype(jnp.bfloat16)

    sums[...] = jnp.zeros_like(sums)
    for shift in range(shifts):
        part = place_ref[0] + shift
        part = jnp.where(part >= shifts, part - shifts, part)
        pairs = tiles[shift].shape[0]
        for pair in range(pairs):
            term = lax.dot_general(
                picked(elements + shift * pairs + pair),
                tiles[shift][pair],
                NN,
                preferred_element_type=jnp.float32,
            )
            fine = fine_ids[part * pairs + pair]
            sums[fine] += term.astype(jnp.bfloat16).astype(jnp.float32)
    for element in range(elements):
        coarse_ref[element] = picked(element)
    for fine in range(fine_count):
        fine_ref[fine] = (inverse_ref[fine] * sums[fine]).astype(jnp.bfloat16)


def restrict(place, fine_ids, inverse, back, tiles, elements, block):
    pairs, basis, _ = tiles[0].shape
    fine_count = inverse.shape[0]
    targets = back.shape[1]
    return pl.pallas_call(
        functools.partial(restrict_kernel, len(tiles)),
        in_specs=[SCALAR] * 3 + [VECTOR] * (1 + len(tiles)),
        out_specs=[VECTOR, VECTOR],
        out_shape=[
            jax.ShapeDtypeStruct((elements, block, basis), jnp.bfloat16),
            jax.ShapeDtypeStruct((fine_count, block, basis), jnp.bfloat16),
        ],
        scratch_shapes=[
            pltpu.VMEM((basis // LANES, block * targets, LANES), jnp.float32),
            pltpu.VMEM((fine_count, block, basis), jnp.float32),
        ],
        compiler_params=pltpu.CompilerParams(
            vmem_limit_bytes=(16 if len(tiles) <= 2 else 56) * 1024 * 1024
        ),
        cost_estimate=pl.CostEstimate(
            flops=2 * len(tiles) * pairs * basis * basis * block,
            bytes_accessed=2 * len(tiles) * pairs * basis * basis,
            transcendentals=0,
        ),
        name="restrict",
    )(place, fine_ids, inverse, back, *tiles)


def shards(
    fine_field_in,
    fine_points,
    coarse_points,
    quad_weights,
    pair_fine,
    pair_owner,
    pair_coarse,
    coarse_faces,
    coarse_inv_mass,
    fine_inv_mass,
):
    nwide = lax.axis_size("wide")
    nfield = lax.axis_size("field")
    place = lax.axis_index("field").astype(jnp.int32).reshape(1)
    block = fine_field_in.shape[1]
    elements, faces = coarse_faces.shape

    own = jnp.concatenate(
        [
            jnp.swapaxes(fine_points, 0, 1),
            jnp.swapaxes(coarse_points, 0, 1),
            quad_weights[None],
        ],
        axis=0,
    )
    points = [own]
    for shift in range(1, nfield):
        perm = [((i + shift) % nfield, i) for i in range(nfield)]
        points.append(lax.ppermute(own, "field", perm))

    scalars = [pair_owner, pair_coarse, coarse_faces, coarse_inv_mass]
    tiles = []
    outs = []
    for shift in range(nfield):
        tile, out = project(
            place, pair_fine, scalars, points[shift], fine_field_in, outs, shift, nfield, nwide
        )
        tiles.append(tile)
        outs.append(out)
    arrived = lax.all_to_all(outs[-1], "wide", split_axis=0, concat_axis=0, tiled=True)
    smooth = coarse_stage(arrived, elements, faces)
    back = lax.all_to_all(smooth, "wide", split_axis=0, concat_axis=0, tiled=True)
    return restrict(place, pair_fine, fine_inv_mass, back, tiles, elements, block)


def solution(mesh):
    placed = (
        P("wide", "field", None),
        P(("wide", "field"), None, None),
        P(("wide", "field"), None, None),
        P(("wide", "field"), None),
        P("wide"),
        P("wide", None),
        P("wide"),
        P("wide", None),
        P("wide"),
        P("wide"),
    )
    return jax.shard_map(
        shards,
        mesh=mesh,
        in_specs=placed,
        out_specs=(P("wide", "field", None), P("wide", "field", None)),
        check_vma=False,
    )
```

time: 149 us -> 65.5 us (0.44); the launches traced: 147 us -> 65.2 us
  waiting for transfers between devices: 30.7 us -> 0.01 us
  Pallas kernels: 0 us -> 23.1 us
  local copies, waits for them, and re-layouts: 25.1 us -> 3.07 us
  matrix products: 21.1 us -> 0 us
  starting transfers between devices: 24.1 us -> 3 us
  other arithmetic: 7.08 us -> 0.98 us
  blocking collectives: 36.6 us -> 34.3 us
  loops' own time: 1.52 us -> 0 us
    all_to_all x5 -> x0, waiting for transfers between devices: 28.3 us -> none  [the longest x1 14.3 us: shards(): lax.all_to_all(outgoing, 'wide', split_axis=0, concat_axis=0, tiled=True)]
    pallas_call x0 -> x4, Pallas kernels: none -> 23.1 us  [the longest x2 19.1 us: project(): pl.pallas_call(functools.partial(project_kernel, shift, shifts, last), in...]
    dot_general x16 -> x0, matrix products: 21.1 us -> none  [the longest x8 12.4 us: build_tile(): lax.dot_general(left, right, (((1,), (1,)), ((), ())), preferred_element_...]
    all_to_all x5 -> x0, starting transfers between devices: 20.9 us -> none  [the longest x1 6.19 us: shards(): lax.all_to_all(slot_ids, 'wide', split_axis=0, concat_axis=0, tiled=True)]
    dynamic_slice x16 -> x0, local copies, waits for them, and re-layouts: 13.8 us -> none  [shards(): lax.map(lambda item: build_tile(item[0], item[1], item[2]), (fine_points,...]
    convert_element_type x17 -> x0, other arithmetic: 3.35 us -> none  [the longest x8 1.8 us: build_tile(): left = (basis(coarse_pts, NB) * weights[None, :]).astype(jnp.bfloat16)]
    all_to_all x9 -> x0, local copies, waits for them, and re-layouts: 2.76 us -> none  [the longest x2 1.34 us: shards(): lax.all_to_all(outgoing, 'wide', split_axis=0, concat_axis=0, tiled=True)]
    another operation x24 -> x0, local copies, waits for them, and re-layouts: 2.5 us -> none  [the longest x16 2.43 us: legendre(): jnp.stack([values[n] * math.sqrt((2 * n + 1) / 2.0) for n in range(count)])]
  transfers between devices with their start and end apart: 7 -> 1, of which waited for: 6 -> 0; matrix products, arithmetic and copies ran while one was open for 25% -> 2% of each run, Pallas kernels for 0% -> 14%
where the time goes in v2:
time: 65.5 us; the launch traced here: 65.2 us
  blocking collectives  34.3 us (52%)
  Pallas kernels  23.1 us (35%)
  local copies, waits for them, and re-layouts  3.07 us (5%)
  starting transfers between devices  3 us (5%)
  other arithmetic  0.98 us (1%)
  between operations  0.7 us (1%)
    pallas_call x2, Pallas kernels, project(): pl.pallas_call(functools.partial(project_kernel, shift, shifts, last), in...  19.1 us
    all_to_all x1, blocking collectives, shards(): lax.all_to_all(smooth, 'wide', split_axis=0, concat_axis=0, tiled=True)  17.5 us
    all_to_all x1, blocking collectives, shards(): lax.all_to_all(outs[-1], 'wide', split_axis=0, concat_axis=0, tiled=True)  16.8 us
    unnamed x14, local copies, waits for them, and re-layouts  3.07 us
    ppermute x1, starting transfers between devices, shards(): points.append(lax.ppermute(own, 'field', perm))  3 us
    pallas_call x1, Pallas kernels, restrict(): pl.pallas_call(functools.partial(restrict_kernel, len(tiles)), in_specs=[...  2.8 us
  transfers between devices with their start and end apart: 1, of which 0 were waited for; matrix products, arithmetic and copies ran while one was open for 2% of the time, Pallas kernels for 14%

profile of v2, /device:TPU:0, one launch (start us, length us, event | category | flops | bytes accessed | tf_op | source)
XLA Modules:
  0.0 65.2 jit_solution(7521658460167478373)
XLA Ops:
  0.6 1.0 %pad_maximum_fusion.refs_0_ = f32[7,8,1024]{2,1,0:T(8,128)S(1)} fusion(f32[1,8,1024]{2,1,0:T(8,128)} %bitcast.6, f32[3,8,1024]{2,1,0:T(8,128)} %bitcast.4, f32[3,8,1024]{2,1,0:T(8,128)} %bitcast.5), kind=kLoop, calls=%fused_computation | loop fusion | flops 114688 | bytes 458752 | tf_op jit(solution)/shard_map/concatenate | solution.py:336
  1.6 3.0 %collective-permute-start = (f32[7,8,1024]{2,1,0:T(8,128)S(1)}, f32[7,8,1024]{2,1,0:T(8,128)S(1)}, u32[]{:S(2)}, u32[]{:S(2)}) collective-permute-start(f32[7,8,1024]{2,1,0:T(8,128)S(1)} %pad_maximum_fusion.refs_0_), channel_id=1, source_target_pairs={{1,0},{0,1},{3,2},{2,3},{5,4},{4,5},{7,6},{6,7},{9,8},{8,9},{11,10... | collective-permute-start | bytes 688136 | tf_op jit(solution)/shard_map/ppermute | solution.py:347
  4.6 0.7 %copy.12.refs_0_ = s32[16,1]{1,0:T(8,128)S(1)} copy(s32[16,1]{0,1:T(1,128)} %param.15) | data formatting | bytes 128 | tf_op args[5]
  5.3 0.8 %copy.13.refs_2_ = s32[16,6]{1,0:T(8,128)S(1)} copy(s32[16,6]{0,1:T(8,128)} %param.17) | data formatting | bytes 768 | tf_op args[7]
  6.1 0.0 copy-start
  6.1 0.7 %copy-done = s32[16]{0:T(128)S(1)} copy-done((s32[16]{0:T(128)S(1)}, s32[16]{0:T(128)}, u32[]{:S(2)}) %copy-start) | copy-done | bytes 88
  6.8 0.0 copy-start.3
  6.8 0.9 %copy-done.3 = bf16[8,16,512]{2,1,0:T(8,128)(2,1)S(1)} copy-done((bf16[8,16,512]{2,1,0:T(8,128)(2,1)S(1)}, bf16[8,16,512]{2,1,0:T(8,128)(2,1)}, u32[]{:S(2)}) %copy-start.3) | copy-done | bytes 131096
  7.7 0.0 copy-start.4
  7.7 0.0 copy-start.5
  7.7 9.2 %project.2 = (bf16[8,512,512]{2,1,0:T(8,128)(2,1)S(1)}, f32[4,128,128]{2,1,0:T(8,128)S(1)}) custom-call(s32[1]{0:T(128)} %bitcast.place_ref, s32[16]{0:T(128)S(1)} %copy-done, f32[7,8,1024]{2,1,0:T(8,128)S(1)} %pad_maximum_fusion.refs_0_, bf16[8,16,512]{2,1,0:T(8,128)(2,1)S(1)} %copy-done.3), custom_call_target="tpu_custom_call" | custom-call | flops 4362076160 | bytes 4194304 | tf_op jit(solution)/shard_map/project/pallas_call | solution.py:167
  16.9 0.0 collective-permute-done.refs_4_
  16.9 0.0 copy-done.4
  17.0 0.0 copy-done.5
  17.0 0.0 copy-start.1
  17.0 0.0 copy-start.2
  17.0 9.9 %project.3 = (bf16[8,512,512]{2,1,0:T(8,128)(2,1)S(1)}, bf16[16,16,640]{2,1,0:T(8,128)(2,1)S(1)}) custom-call(s32[1]{0:T(128)} %bitcast.place_ref, s32[16]{0:T(128)S(1)} %copy-done, s32[16,1]{1,0:T(8,128)S(1)} %copy.12.refs_0_, s32[16]{0:T(128)S(1)} %copy-done.4, s32[16,6]{1,0:T(8,128)S(1)} %copy.13.refs_2_, f32[16]{0:T(128)S(1)} %copy-done.5, ...), custom_call_target="tpu_custom_call" | custom-call | flops 4362076160 | bytes 4194304 | tf_op jit(solution)/shard_map/project/pallas_call | solution.py:167
  26.8 16.8 %all_to_all.10.arrived_ref = bf16[16,16,640]{2,1,0:T(8,128)(2,1)S(1)} all-to-all(bf16[16,16,640]{2,1,0:T(8,128)(2,1)S(1)} %get-tuple-element.7), channel_id=1, replica_groups=mesh['wide'=16,'field'=2] {'wide'}, dimensions={0} | all-to-all | bytes 655360 | tf_op jit(solution)/shard_map/all_to_all | solution.py:358
  43.7 1.2 %coarse_stage.1 = bf16[16,32,512]{2,1,0:T(8,128)(2,1)S(1)} custom-call(bf16[16,16,640]{2,1,0:T(8,128)(2,1)S(1)} %all_to_all.10.arrived_ref), custom_call_target="tpu_custom_call" | custom-call | flops 268435456 | bytes 524288 | tf_op jit(solution)/shard_map/coarse_stage/pallas_call | solution.py:232
  44.9 17.5 %all_to_all.11.back_ref = bf16[16,32,512]{2,1,0:T(8,128)(2,1)S(1)} all-to-all(bf16[16,32,512]{2,1,0:T(8,128)(2,1)S(1)} %coarse_stage.1), channel_id=1, replica_groups=mesh['wide'=16,'field'=2] {'wide'}, dimensions={0} | all-to-all | bytes 1048576 | tf_op jit(solution)/shard_map/all_to_all | solution.py:360
  62.4 0.0 copy-done.1
  62.4 0.0 copy-done.2
  62.4 2.8 %restrict.1 = (bf16[16,16,512]{2,1,0:T(8,128)(2,1)}, bf16[8,16,512]{2,1,0:T(8,128)(2,1)}) custom-call(s32[1]{0:T(128)} %bitcast.place_ref, s32[16]{0:T(128)S(1)} %copy-done.1, f32[8]{0:T(128)S(1)} %copy-done.2, bf16[16,32,512]{2,1,0:T(8,128)(2,1)S(1)} %all_to_all.11.back_ref, bf16[8,512,512]{2,1,0:T(8,128)(2,1)S(1)} %get-tuple-element.8.refs_0_, ...), custom_call_target="tpu_custom_call" | custom-call | flops 134217728 | bytes 8388608 | tf_op jit(solution)/shard_map/restrict/pallas_call | solution.py:294
Async XLA Ops:
  1.6 15.3 %collective-permute-start = (f32[7,8,1024]{2,1,0:T(8,128)S(1)}, f32[7,8,1024]{2,1,0:T(8,128)S(1)}, u32[]{:S(2)}, u32[]{:S(2)}) collective-permute-start(f32[7,8,1024]{2,1,0:T(8,128)S(1)} %pad_maximum_fusion.refs_0_), channel_id=1, source_target_pairs={{1,0},{0,1},{3,2},{2,3},{5,4},{4,5},{7,6},{6,7},{9,8},{8,9},{11,10... | collective-permute-start | bytes 688136 | tf_op jit(solution)/shard_map/ppermute | solution.py:347
  6.1 0.7 %copy-start = (s32[16]{0:T(128)S(1)}, s32[16]{0:T(128)}, u32[]{:S(2)}) copy-start(s32[16]{0:T(128)} %fine_ids.1) | copy-start | bytes 196
  6.8 0.9 %copy-start.3 = (bf16[8,16,512]{2,1,0:T(8,128)(2,1)S(1)}, bf16[8,16,512]{2,1,0:T(8,128)(2,1)}, u32[]{:S(2)}) copy-start(bf16[8,16,512]{2,1,0:T(8,128)(2,1)} %refs_5_.1) | copy-start | bytes 393220
  7.7 9.3 %copy-start.4 = (s32[16]{0:T(128)S(1)}, s32[16]{0:T(128)}, u32[]{:S(2)}) copy-start(s32[16]{0:T(128)} %refs_1_.3) | copy-start | bytes 196
  7.7 9.3 %copy-start.5 = (f32[16]{0:T(128)S(1)}, f32[16]{0:T(128)}, u32[]{:S(2)}) copy-start(f32[16]{0:T(128)} %refs_3_.1) | copy-start | bytes 196
  17.0 45.4 %copy-start.1 = (s32[16]{0:T(128)S(1)}, s32[16]{0:T(128)}, u32[]{:S(2)}) copy-start(s32[16]{0:T(128)} %fine_ids.1) | copy-start | bytes 196
  17.0 45.4 %copy-start.2 = (f32[8]{0:T(128)S(1)}, f32[8]{0:T(128)}, u32[]{:S(2)}) copy-start(f32[8]{0:T(128)} %inverse_ref.1) | copy-start | bytes 100

commit v3 on v2

--- a/solution.py
+++ b/solution.py
@@ -18,6 +18,7 @@
 
 SCALAR = pl.BlockSpec(memory_space=pltpu.SMEM)
 VECTOR = pl.BlockSpec(memory_space=pltpu.VMEM)
+DISTANT = pl.BlockSpec(memory_space=pltpu.HBM)
 
 
 def legendre(points, count):
@@ -35,35 +36,35 @@
     return slice(index * LANES, (index + 1) * LANES)
 
 
-def fill_table(table_ref, rows_ref, legs, base, pair):
-    here = pl.ds(pl.multiple_of(pair * NB, NB), NB)
+def fill_table(table_ref, legs, base, pair):
+    start = pl.multiple_of(pair * NB, NB)
     for lane in range(legs.shape[1]):
-        first = legs[base, lane, here, :]
-        second = legs[base + 1, lane, here, :]
-        third = legs[base + 2, lane, here, :]
+        third = legs[base + 2, lane, pl.ds(start, NB), :]
+        outer = [legs[base, lane, pl.ds(start + a, 1), :] * third for a in range(NB)]
+        inner = [
+            jnp.broadcast_to(legs[base + 1, lane, pl.ds(start + b, 1), :], (NB, LANES))
+            for b in range(NB)
+        ]
         for a in range(NB):
-            rows_ref[lane, a * NB : (a + 1) * NB, :] = first[a : a + 1, :] * second
-        for ab in range(0, NB * NB, 2):
-            low = rows_ref[lane, ab : ab + 1, :] * third
-            high = rows_ref[lane, ab + 1 : ab + 2, :] * third
-            table_ref[ab * NB : (ab + 2) * NB, lanes(lane)] = jnp.concatenate(
-                [low, high], axis=0
-            ).astype(jnp.bfloat16)
+            for b in range(0, NB, 2):
+                both = jnp.concatenate([outer[a] * inner[b], outer[a] * inner[b + 1]], axis=0)
+                row = (a * NB + b) * NB
+                table_ref[row : row + 2 * NB, lanes(lane)] = both.astype(jnp.bfloat16)
 
 
 def facts(owner_ref, coarse_ref, faces_ref, inverse_ref, rows, pair_at):
-    elements, faces = faces_ref.shape
+    faces, elements = faces_ref.shape
     lane = lax.broadcasted_iota(jnp.int32, (1, LANES), 1)
     lines = []
     for row in range(rows):
         line = jnp.zeros((1, LANES), jnp.float32)
         if row < coarse_ref.shape[0]:
             pair = pair_at(row)
-            line = jnp.where(lane == 0, owner_ref[pair, 0].astype(jnp.float32), line)
+            line = jnp.where(lane == 0, owner_ref[0, pair].astype(jnp.float32), line)
             line = jnp.where(lane == 1, coarse_ref[pair].astype(jnp.float32), line)
         if row < elements:
             for face in range(faces):
-                name = faces_ref[row, face]
+                name = faces_ref[face, row]
                 outer = lax.div(name, jnp.int32(elements))
                 inner = name - outer * elements
                 line = jnp.where(lane == 2 + 2 * face, outer.astype(jnp.float32), line)
@@ -77,14 +78,20 @@
     return jnp.concatenate(lines, axis=0).astype(jnp.bfloat16)
 
 
-def project_kernel(shift, shifts, last, place_ref, fine_ref, *refs):
+def project_kernel(shift, shifts, last, place_ref, *refs):
     if last:
         owner_ref, coarse_ref, faces_ref, inverse_ref = refs[:4]
         refs = refs[4:]
-    points_ref, field_ref = refs[:2]
-    before = refs[2 : len(refs) - 12]
-    tile_ref, out_ref, legs, sums = refs[-12:-8]
-    rows, tables = refs[-8:-4], refs[-4:]
+    points_ref, fine_hbm, field_hbm = refs[:3]
+    before = refs[3 : len(refs) - 11]
+    tile_ref, out_ref, legs, sums, fine_ref, field_ref, arrive = refs[-11:-4]
+    tables = refs[-4:]
+    fetches = [
+        pltpu.make_async_copy(fine_hbm, fine_ref, arrive.at[0]),
+        pltpu.make_async_copy(field_hbm, field_ref, arrive.at[1]),
+    ]
+    for fetch in fetches:
+        fetch.start()
     pairs = points_ref.shape[1]
     block = field_ref.shape[1]
 
@@ -100,8 +107,8 @@
                 legs[coord, lane, pl.ds(n, pairs, stride=NB), :] = value
 
     def fill(pair, slot):
-        fill_table(tables[2 * slot], rows[2 * slot], legs, 0, pair)
-        fill_table(tables[2 * slot + 1], rows[2 * slot + 1], legs, 3, pair)
+        fill_table(tables[2 * slot], legs, 0, pair)
+        fill_table(tables[2 * slot + 1], legs, 3, pair)
 
     def apply(pair, slot):
         tile = lax.dot_general(
@@ -115,6 +122,8 @@
             sums[lane, pl.ds(pair, block, stride=pairs), :] = contrib[:, lanes(lane)]
 
     fill(0, 0)
+    for fetch in fetches:
+        fetch.wait()
 
     @pl.loop(0, pairs // 2)
     def _(step):
@@ -159,11 +168,9 @@
         )
     else:
         out = jax.ShapeDtypeStruct((across, block * pairs, LANES), jnp.float32)
-    operands = [place, fine_ids]
-    if last:
-        operands += scalars
-    specs = [SCALAR] * len(operands)
-    vectors = [points, field] + (before if last else [])
+    operands = [place] + (scalars if last else [])
+    specs = [SCALAR] * len(operands) + [VECTOR, DISTANT, DISTANT]
+    vectors = before if last else []
     return pl.pallas_call(
         functools.partial(project_kernel, shift, shifts, last),
         in_specs=specs + [VECTOR] * len(vectors),
@@ -172,8 +179,10 @@
         scratch_shapes=[
             pltpu.VMEM((6, quad // LANES, pairs * NB, LANES), jnp.float32),
             pltpu.VMEM((across, block * pairs, LANES), jnp.float32),
+            pltpu.SMEM(fine_ids.shape, jnp.int32),
+            pltpu.VMEM(field.shape, field.dtype),
+            pltpu.SemaphoreType.DMA((2,)),
         ]
-        + [pltpu.VMEM((quad // LANES, NB * NB, LANES), jnp.float32)] * 4
         + [pltpu.VMEM((basis, quad), jnp.bfloat16)] * 4,
         compiler_params=pltpu.CompilerParams(vmem_limit_bytes=24 * 1024 * 1024),
         cost_estimate=pl.CostEstimate(
@@ -182,7 +191,7 @@
             transcendentals=0,
         ),
         name="project",
-    )(*operands, *vectors)
+    )(*operands, points, fine_ids, field, *vectors)
 
 
 def coarse_kernel(faces, elements, arrived_ref, out_ref, pick, near, moved):
@@ -346,7 +355,7 @@
         perm = [((i + shift) % nfield, i) for i in range(nfield)]
         points.append(lax.ppermute(own, "field", perm))
 
-    scalars = [pair_owner, pair_coarse, coarse_faces, coarse_inv_mass]
+    scalars = [pair_owner.T, pair_coarse, coarse_faces.T, coarse_inv_mass]
     tiles = []
     outs = []
     for shift in range(nfield):

time: 65.5 us -> 63.1 us (0.963)
  local copies, waits for them, and re-layouts: 3.07 us -> 1.59 us
  Pallas kernels: 23.1 us -> 22.2 us
    unnamed x14 -> x16, local copies, waits for them, and re-layouts: 3.07 us -> 1.59 us
    pallas_call x2, Pallas kernels: 19.1 us -> 18.2 us  [project(): pl.pallas_call(functools.partial(project_kernel, shift, shifts, last), in...]
  transfers between devices with their start and end apart: 1 -> 1, of which waited for: 0 -> 0; matrix products, arithmetic and copies ran while one was open for 2% -> 0% of each run, Pallas kernels for 14% -> 14%
where the time goes in v3:
time: 63.1 us; the launch traced here: 62.9 us
  blocking collectives  34.4 us (55%)
  Pallas kernels  22.2 us (35%)
  starting transfers between devices  3 us (5%)
  local copies, waits for them, and re-layouts  1.59 us (3%)
  other arithmetic  0.98 us (2%)
  between operations  0.72 us (1%)
    pallas_call x2, Pallas kernels, project(): pl.pallas_call(functools.partial(project_kernel, shift, shifts, last), in...  18.2 us
    all_to_all x1, blocking collectives, shards(): lax.all_to_all(smooth, 'wide', split_axis=0, concat_axis=0, tiled=True)  17.5 us
    all_to_all x1, blocking collectives, shards(): lax.all_to_all(outs[-1], 'wide', split_axis=0, concat_axis=0, tiled=True)  16.8 us
    ppermute x1, starting transfers between devices, shards(): points.append(lax.ppermute(own, 'field', perm))  3 us
    pallas_call x1, Pallas kernels, restrict(): pl.pallas_call(functools.partial(restrict_kernel, len(tiles)), in_specs=[...  2.8 us
    unnamed x16, local copies, waits for them, and re-layouts  1.59 us
  transfers between devices with their start and end apart: 1, of which 0 were waited for; matrix products, arithmetic and copies ran while one was open for 0% of the time, Pallas kernels for 14%

profile of v3, /device:TPU:0, one launch (start us, length us, event | category | flops | bytes accessed | tf_op | source)
XLA Modules:
  0.0 62.9 jit_solution(4551572124733401557)
XLA Ops:
  0.6 1.0 %pad_maximum_fusion.refs_0_ = f32[7,8,1024]{2,1,0:T(8,128)S(1)} fusion(f32[1,8,1024]{2,1,0:T(8,128)} %bitcast.10, f32[3,8,1024]{2,1,0:T(8,128)} %bitcast.8, f32[3,8,1024]{2,1,0:T(8,128)} %bitcast.9), kind=kLoop, calls=%fused_computation | loop fusion | flops 114688 | bytes 458752 | tf_op jit(solution)/shard_map/concatenate | solution.py:345
  1.6 3.0 %collective-permute-start = (f32[7,8,1024]{2,1,0:T(8,128)S(1)}, f32[7,8,1024]{2,1,0:T(8,128)S(1)}, u32[]{:S(2)}, u32[]{:S(2)}) collective-permute-start(f32[7,8,1024]{2,1,0:T(8,128)S(1)} %pad_maximum_fusion.refs_0_), channel_id=1, source_target_pairs={{1,0},{0,1},{3,2},{2,3},{5,4},{4,5},{7,6},{6,7},{9,8},{8,9},{11,10... | collective-permute-start | bytes 688136 | tf_op jit(solution)/shard_map/ppermute | solution.py:356
  4.6 0.0 copy-start
  4.6 0.7 %copy-done = s32[16]{0:T(128)S(1)} copy-done((s32[16]{0:T(128)S(1)}, s32[16]{0:T(128)}, u32[]{:S(2)}) %copy-start) | copy-done | bytes 88
  5.3 0.0 copy-start.3
  5.3 0.9 %copy-done.3 = bf16[8,16,512]{2,1,0:T(8,128)(2,1)S(1)} copy-done((bf16[8,16,512]{2,1,0:T(8,128)(2,1)S(1)}, bf16[8,16,512]{2,1,0:T(8,128)(2,1)}, u32[]{:S(2)}) %copy-start.3) | copy-done | bytes 131096
  6.2 0.0 copy-start.4
  6.2 0.0 copy-start.5
  6.2 0.0 copy-start.6
  6.2 0.0 copy-start.7
  6.2 8.7 %project.2 = (bf16[8,512,512]{2,1,0:T(8,128)(2,1)S(1)}, f32[4,128,128]{2,1,0:T(8,128)S(1)}) custom-call(s32[1]{0:T(128)} %bitcast.place_ref, f32[7,8,1024]{2,1,0:T(8,128)S(1)} %pad_maximum_fusion.refs_0_, s32[16]{0:T(128)S(1)} %copy-done, bf16[8,16,512]{2,1,0:T(8,128)(2,1)S(1)} %copy-done.3), custom_call_target="tpu_custom_call" | custom-call | flops 4362076160 | bytes 4194304 | tf_op jit(solution)/shard_map/project/pallas_call | solution.py:174
  14.8 0.0 collective-permute-done.refs_4_
  14.9 0.0 copy-done.4
  14.9 0.0 copy-done.5
  14.9 0.0 copy-done.6
  14.9 0.0 copy-done.7
  14.9 0.0 copy-start.1
  14.9 0.0 copy-start.2
  14.9 9.6 %project.3 = (bf16[8,512,512]{2,1,0:T(8,128)(2,1)S(1)}, bf16[16,16,640]{2,1,0:T(8,128)(2,1)S(1)}) custom-call(s32[1]{0:T(128)} %bitcast.place_ref, s32[1,16]{1,0:T(1,128)S(1)} %bitcast.7, s32[16]{0:T(128)S(1)} %copy-done.6, s32[6,16]{1,0:T(8,128)S(1)} %bitcast.6, f32[16]{0:T(128)S(1)} %copy-done.7, f32[7,8,1024]{2,1,0:T(8,128)S(1)} %collective-permute-done.refs_4_, ...), custom_call_target="tpu_custom_call" | custom-call | flops 4362076160 | bytes 4194304 | tf_op jit(solution)/shard_map/project/pallas_call | solution.py:174
  24.5 16.8 %all_to_all.10.arrived_ref = bf16[16,16,640]{2,1,0:T(8,128)(2,1)S(1)} all-to-all(bf16[16,16,640]{2,1,0:T(8,128)(2,1)S(1)} %get-tuple-element.7), channel_id=1, replica_groups=mesh['wide'=16,'field'=2] {'wide'}, dimensions={0} | all-to-all | bytes 655360 | tf_op jit(solution)/shard_map/all_to_all | solution.py:367
  41.4 1.2 %coarse_stage.1 = bf16[16,32,512]{2,1,0:T(8,128)(2,1)S(1)} custom-call(bf16[16,16,640]{2,1,0:T(8,128)(2,1)S(1)} %all_to_all.10.arrived_ref), custom_call_target="tpu_custom_call" | custom-call | flops 268435456 | bytes 524288 | tf_op jit(solution)/shard_map/coarse_stage/pallas_call | solution.py:241
  42.6 17.5 %all_to_all.11.back_ref = bf16[16,32,512]{2,1,0:T(8,128)(2,1)S(1)} all-to-all(bf16[16,32,512]{2,1,0:T(8,128)(2,1)S(1)} %coarse_stage.1), channel_id=1, replica_groups=mesh['wide'=16,'field'=2] {'wide'}, dimensions={0} | all-to-all | bytes 1048576 | tf_op jit(solution)/shard_map/all_to_all | solution.py:369
  60.1 0.0 copy-done.1
  60.1 0.0 copy-done.2
  60.1 2.8 %restrict.1 = (bf16[16,16,512]{2,1,0:T(8,128)(2,1)}, bf16[8,16,512]{2,1,0:T(8,128)(2,1)}) custom-call(s32[1]{0:T(128)} %bitcast.place_ref, s32[16]{0:T(128)S(1)} %copy-done.1, f32[8]{0:T(128)S(1)} %copy-done.2, bf16[16,32,512]{2,1,0:T(8,128)(2,1)S(1)} %all_to_all.11.back_ref, bf16[8,512,512]{2,1,0:T(8,128)(2,1)S(1)} %get-tuple-element.8.refs_0_, ...), custom_call_target="tpu_custom_call" | custom-call | flops 134217728 | bytes 8388608 | tf_op jit(solution)/shard_map/restrict/pallas_call | solution.py:303
Async XLA Ops:
  1.6 13.2 %collective-permute-start = (f32[7,8,1024]{2,1,0:T(8,128)S(1)}, f32[7,8,1024]{2,1,0:T(8,128)S(1)}, u32[]{:S(2)}, u32[]{:S(2)}) collective-permute-start(f32[7,8,1024]{2,1,0:T(8,128)S(1)} %pad_maximum_fusion.refs_0_), channel_id=1, source_target_pairs={{1,0},{0,1},{3,2},{2,3},{5,4},{4,5},{7,6},{6,7},{9,8},{8,9},{11,10... | collective-permute-start | bytes 688136 | tf_op jit(solution)/shard_map/ppermute | solution.py:356
  4.6 0.7 %copy-start = (s32[16]{0:T(128)S(1)}, s32[16]{0:T(128)}, u32[]{:S(2)}) copy-start(s32[16]{0:T(128)} %fine_ids.1) | copy-start | bytes 196
  5.3 0.9 %copy-start.3 = (bf16[8,16,512]{2,1,0:T(8,128)(2,1)S(1)}, bf16[8,16,512]{2,1,0:T(8,128)(2,1)}, u32[]{:S(2)}) copy-start(bf16[8,16,512]{2,1,0:T(8,128)(2,1)} %refs_6_.1) | copy-start | bytes 393220
  6.2 8.7 %copy-start.4 = (s32[16,6]{0,1:T(8,128)S(1)}, s32[16,6]{0,1:T(8,128)}, u32[]{:S(2)}) copy-start(s32[16,6]{0,1:T(8,128)} %param.17) | copy-start | bytes 1156
  6.2 8.7 %copy-start.5 = (s32[16,1]{0,1:T(1,128)S(1)}, s32[16,1]{0,1:T(1,128)}, u32[]{:S(2)}) copy-start(s32[16,1]{0,1:T(1,128)} %param.15) | copy-start | bytes 196
  6.2 8.7 %copy-start.6 = (s32[16]{0:T(128)S(1)}, s32[16]{0:T(128)}, u32[]{:S(2)}) copy-start(s32[16]{0:T(128)} %refs_1_.3) | copy-start | bytes 196
  6.2 8.7 %copy-start.7 = (f32[16]{0:T(128)S(1)}, f32[16]{0:T(128)}, u32[]{:S(2)}) copy-start(f32[16]{0:T(128)} %refs_3_.1) | copy-start | bytes 196
  14.9 45.2 %copy-start.1 = (s32[16]{0:T(128)S(1)}, s32[16]{0:T(128)}, u32[]{:S(2)}) copy-start(s32[16]{0:T(128)} %fine_ids.1) | copy-start | bytes 196
  14.9 45.2 %copy-start.2 = (f32[8]{0:T(128)S(1)}, f32[8]{0:T(128)}, u32[]{:S(2)}) copy-start(f32[8]{0:T(128)} %inverse_ref.1) | copy-start | bytes 100

commit v4 on v3

--- a/solution.py
+++ b/solution.py
@@ -11,6 +11,7 @@
 NB = 8
 DIFFUSE = 0.125
 LANES = 128
+DIGIT = 7
 
 NT = (((1,), (1,)), ((), ()))
 NN = (((1,), (0,)), ((), ()))
@@ -18,15 +19,14 @@
 
 SCALAR = pl.BlockSpec(memory_space=pltpu.SMEM)
 VECTOR = pl.BlockSpec(memory_space=pltpu.VMEM)
-DISTANT = pl.BlockSpec(memory_space=pltpu.HBM)
 
 
 def legendre(points, count):
     values = [jnp.ones_like(points), points]
     for degree in range(1, count - 1):
         values.append(
-            ((2 * degree + 1) * points * values[degree] - degree * values[degree - 1])
-            / (degree + 1)
+            ((2 * degree + 1) / (degree + 1)) * points * values[degree]
+            - (degree / (degree + 1)) * values[degree - 1]
         )
     values = values[:count]
     return [values[n] * math.sqrt((2 * n + 1) / 2.0) for n in range(count)]
@@ -36,20 +36,19 @@
     return slice(index * LANES, (index + 1) * LANES)
 
 
-def fill_table(table_ref, legs, base, pair):
+def fill_table(table_ref, legs, base, pair, lane):
     start = pl.multiple_of(pair * NB, NB)
-    for lane in range(legs.shape[1]):
-        third = legs[base + 2, lane, pl.ds(start, NB), :]
-        outer = [legs[base, lane, pl.ds(start + a, 1), :] * third for a in range(NB)]
-        inner = [
-            jnp.broadcast_to(legs[base + 1, lane, pl.ds(start + b, 1), :], (NB, LANES))
-            for b in range(NB)
-        ]
-        for a in range(NB):
-            for b in range(0, NB, 2):
-                both = jnp.concatenate([outer[a] * inner[b], outer[a] * inner[b + 1]], axis=0)
-                row = (a * NB + b) * NB
-                table_ref[row : row + 2 * NB, lanes(lane)] = both.astype(jnp.bfloat16)
+    third = legs[base + 2, lane, pl.ds(start, NB), :]
+    outer = [legs[base, lane, pl.ds(start + a, 1), :] * third for a in range(NB)]
+    inner = [
+        jnp.broadcast_to(legs[base + 1, lane, pl.ds(start + b, 1), :], (NB, LANES))
+        for b in range(NB)
+    ]
+    for a in range(NB):
+        for b in range(0, NB, 2):
+            both = jnp.concatenate([outer[a] * inner[b], outer[a] * inner[b + 1]], axis=0)
+            row = (a * NB + b) * NB
+            table_ref[row : row + 2 * NB, lanes(lane)] = both.astype(jnp.bfloat16)
 
 
 def facts(owner_ref, coarse_ref, faces_ref, inverse_ref, rows, pair_at):
@@ -65,8 +64,8 @@
         if row < elements:
             for face in range(faces):
                 name = faces_ref[face, row]
-                outer = lax.div(name, jnp.int32(elements))
-                inner = name - outer * elements
+                outer = lax.shift_right_logical(name, DIGIT)
+                inner = name - lax.shift_left(outer, DIGIT)
                 line = jnp.where(lane == 2 + 2 * face, outer.astype(jnp.float32), line)
                 line = jnp.where(lane == 3 + 2 * face, inner.astype(jnp.float32), line)
             rest = jnp.full((1, LANES), inverse_ref[row], jnp.float32)
@@ -78,22 +77,24 @@
     return jnp.concatenate(lines, axis=0).astype(jnp.bfloat16)
 
 
-def project_kernel(shift, shifts, last, place_ref, *refs):
+def project_kernel(shift, shifts, place_ref, *refs):
+    last = shift == shifts - 1
+    refs = list(refs)
+    points_ref = refs.pop(0)
+    if shift or last:
+        fine_ref, field_ref = refs.pop(0), refs.pop(0)
+    prior = [refs.pop(0)] if shift else []
     if last:
         owner_ref, coarse_ref, faces_ref, inverse_ref = refs[:4]
-        refs = refs[4:]
-    points_ref, fine_hbm, field_hbm = refs[:3]
-    before = refs[3 : len(refs) - 11]
-    tile_ref, out_ref, legs, sums, fine_ref, field_ref, arrive = refs[-11:-4]
-    tables = refs[-4:]
-    fetches = [
-        pltpu.make_async_copy(fine_hbm, fine_ref, arrive.at[0]),
-        pltpu.make_async_copy(field_hbm, field_ref, arrive.at[1]),
-    ]
-    for fetch in fetches:
-        fetch.start()
+        before = refs[4 : 4 + max(0, shifts - 2)]
+        refs = refs[4 + len(before) :]
+    tile_ref = refs.pop(0)
+    out_ref = refs.pop(0) if shift or last else None
+    legs, sums = refs[:2]
+    tables = refs[2:]
     pairs = points_ref.shape[1]
-    block = field_ref.shape[1]
+    half = tile_ref.shape[1] // 2
+    across = sums.shape[0]
 
     def pair_at(step, pair):
         part = place_ref[0] + step
@@ -106,39 +107,57 @@
                 value = values[n] * points_ref[6, :, lanes(lane)] if coord == 3 else values[n]
                 legs[coord, lane, pl.ds(n, pairs, stride=NB), :] = value
 
-    def fill(pair, slot):
-        fill_table(tables[2 * slot], legs, 0, pair)
-        fill_table(tables[2 * slot + 1], legs, 3, pair)
-
-    def apply(pair, slot):
-        tile = lax.dot_general(
-            tables[2 * slot + 1][...], tables[2 * slot][...], NT, preferred_element_type=jnp.float32
+    def fills(pair, slot):
+        return [
+            functools.partial(fill_table, tables[2 * slot + side], legs, 3 * side, pair, lane)
+            for lane in range(legs.shape[1])
+            for side in range(2)
+        ]
+
+    def quarter(pair, slot, up, across):
+        rows, columns = slice(up * half, (up + 1) * half), slice(across * half, (across + 1) * half)
+        tile_ref[pair, rows, columns] = lax.dot_general(
+            tables[2 * slot + 1][rows, :],
+            tables[2 * slot][columns, :],
+            NT,
+            preferred_element_type=jnp.float32,
         ).astype(jnp.bfloat16)
-        tile_ref[pair] = tile
-        contrib = lax.dot_general(
-            field_ref[fine_ref[pair_at(shift, pair)]], tile, NT, preferred_element_type=jnp.float32
-        )
-        for lane in range(sums.shape[0]):
-            sums[lane, pl.ds(pair, block, stride=pairs), :] = contrib[:, lanes(lane)]
-
-    fill(0, 0)
-    for fetch in fetches:
-        fetch.wait()
+
+    def contribute(source, step, base, pair):
+        field = field_ref[fine_ref[pair_at(step, pair)]]
+        block = field.shape[0]
+        total = sums.shape[1] // block
+        contrib = lax.dot_general(field, source[pair], NT, preferred_element_type=jnp.float32)
+        for lane in range(across):
+            sums[lane, pl.ds(base + pair, block, stride=total), :] = contrib[:, lanes(lane)]
+
+    def turn(pair, slot):
+        following = fills(jnp.minimum(pair + 1, pairs - 1), 1 - slot)
+        share = len(following) // 4
+        for part in range(4):
+            quarter(pair, slot, part % 2, part // 2)
+            for fill in following[part * share : (part + 1) * share]:
+                fill()
+        for source in prior:
+            contribute(source, shift - 1, 0, pair)
+
+    for fill in fills(0, 0):
+        fill()
 
     @pl.loop(0, pairs // 2)
     def _(step):
-        pair = 2 * step
-        fill(pair + 1, 1)
-        apply(pair, 0)
-        fill(jnp.minimum(pair + 2, pairs - 1), 0)
-        apply(pair + 1, 1)
+        turn(2 * step, 0)
+        turn(2 * step + 1, 1)
 
     if not last:
-        out_ref[...] = sums[...]
+        if shift:
+            out_ref[...] = sums[...]
         return
+    base = pairs if shift else 0
+    for pair in range(pairs):
+        contribute(tile_ref, shift, base, pair)
     wide, total, span = out_ref.shape
     width = span - LANES
-    across = sums.shape[0]
     extra = facts(
         owner_ref,
         coarse_ref,
@@ -147,41 +166,49 @@
         total,
         lambda row: pair_at(row // pairs, row % pairs),
     )
-    sources = list(before) + [sums]
+    held = base + pairs
     for dest in range(wide):
         for piece in range(width // LANES):
-            column = dest * (width // LANES) + piece
-            row, lane = divmod(column, across)
-            parts = [s[lane, row * pairs : (row + 1) * pairs, :] for s in sources]
+            row, lane = divmod(dest * (width // LANES) + piece, across)
+            parts = [b[lane, row * pairs : (row + 1) * pairs, :] for b in before]
+            parts.append(sums[lane, row * held : (row + 1) * held, :])
             out_ref[dest, :, lanes(piece)] = jnp.concatenate(parts, axis=0).astype(jnp.bfloat16)
         out_ref[dest, :, lanes(width // LANES)] = extra
 
 
-def project(place, fine_ids, scalars, points, field, before, shift, shifts, wide):
+def project(place, fine_ids, scalars, points, field, prior, before, shift, shifts, wide):
     _, pairs, quad = points.shape
-    fine_count, block, basis = field.shape
+    _, block, basis = field.shape
     last = shift == shifts - 1
     across = basis // LANES
+    operands, specs = [place, points], [SCALAR, VECTOR]
+    outs = [jax.ShapeDtypeStruct((pairs, basis, basis), jnp.bfloat16)]
+    held = pairs
+    if shift or last:
+        operands += [fine_ids, field]
+        specs += [SCALAR, VECTOR]
+    if shift:
+        operands.append(prior)
+        specs.append(VECTOR)
     if last:
-        out = jax.ShapeDtypeStruct(
-            (wide, shifts * pairs, block * basis // wide + LANES), jnp.bfloat16
+        operands += scalars + before
+        specs += [SCALAR] * len(scalars) + [VECTOR] * len(before)
+        held = pairs * min(2, shifts)
+        outs.append(
+            jax.ShapeDtypeStruct(
+                (wide, shifts * pairs, block * basis // wide + LANES), jnp.bfloat16
+            )
         )
-    else:
-        out = jax.ShapeDtypeStruct((across, block * pairs, LANES), jnp.float32)
-    operands = [place] + (scalars if last else [])
-    specs = [SCALAR] * len(operands) + [VECTOR, DISTANT, DISTANT]
-    vectors = before if last else []
+    elif shift:
+        outs.append(jax.ShapeDtypeStruct((across, block * pairs, LANES), jnp.float32))
     return pl.pallas_call(
-        functools.partial(project_kernel, shift, shifts, last),
-        in_specs=specs + [VECTOR] * len(vectors),
-        out_specs=[VECTOR, VECTOR],
-        out_shape=[jax.ShapeDtypeStruct((pairs, basis, basis), jnp.bfloat16), out],
+        functools.partial(project_kernel, shift, shifts),
+        in_specs=specs,
+        out_specs=[VECTOR] * len(outs),
+        out_shape=outs,
         scratch_shapes=[
             pltpu.VMEM((6, quad // LANES, pairs * NB, LANES), jnp.float32),
-            pltpu.VMEM((across, block * pairs, LANES), jnp.float32),
-            pltpu.SMEM(fine_ids.shape, jnp.int32),
-            pltpu.VMEM(field.shape, field.dtype),
-            pltpu.SemaphoreType.DMA((2,)),
+            pltpu.VMEM((across, block * held, LANES), jnp.float32),
         ]
         + [pltpu.VMEM((basis, quad), jnp.bfloat16)] * 4,
         compiler_params=pltpu.CompilerParams(vmem_limit_bytes=24 * 1024 * 1024),
@@ -191,7 +218,7 @@
             transcendentals=0,
         ),
         name="project",
-    )(*operands, points, fine_ids, field, *vectors)
+    )(*operands)
 
 
 def coarse_kernel(faces, elements, arrived_ref, out_ref, pick, near, moved):
@@ -209,7 +236,7 @@
         )
         hits = jnp.zeros((elements, count), jnp.float32)
         for face in range(faces):
-            index = fact[:elements, 2 + 2 * face : 3 + 2 * face] * elements
+            index = fact[:elements, 2 + 2 * face : 3 + 2 * face] * float(1 << DIGIT)
             index = index + fact[:elements, 3 + 2 * face : 4 + 2 * face]
             hits = hits + (index == name[:elements]).astype(jnp.float32)
         near[source * elements : (source + 1) * elements, :] = hits.astype(jnp.bfloat16)
@@ -359,11 +386,20 @@
     tiles = []
     outs = []
     for shift in range(nfield):
-        tile, out = project(
-            place, pair_fine, scalars, points[shift], fine_field_in, outs, shift, nfield, nwide
+        tile, *out = project(
+            place,
+            pair_fine,
+            scalars,
+            points[shift],
+            fine_field_in,
+            tiles[-1] if tiles else None,
+            outs,
+            shift,
+            nfield,
+            nwide,
         )
         tiles.append(tile)
-        outs.append(out)
+        outs += out
     arrived = lax.all_to_all(outs[-1], "wide", split_axis=0, concat_axis=0, tiled=True)
     smooth = coarse_stage(arrived, elements, faces)
     back = lax.all_to_all(smooth, "wide", split_axis=0, concat_axis=0, tiled=True)

time: 63.1 us -> 60.6 us (0.960)
  local copies, waits for them, and re-layouts: 1.59 us -> 0.03 us
  Pallas kernels: 22.2 us -> 21.3 us
    unnamed x16 -> x14, local copies, waits for them, and re-layouts: 1.59 us -> 0.03 us
    pallas_call x2, Pallas kernels: 18.2 us -> 17.3 us  [project(): pl.pallas_call(functools.partial(project_kernel, shift, shifts), in_specs...]
  transfers between devices with their start and end apart: 1 -> 1, of which waited for: 0 -> 0; matrix products, arithmetic and copies ran while one was open for 0% -> 0% of each run, Pallas kernels for 14% -> 12%
where the time goes in v4:
time: 60.6 us; the launch traced here: 60.4 us
  blocking collectives  34.3 us (57%)
  Pallas kernels  21.3 us (35%)
  starting transfers between devices  3 us (5%)
  other arithmetic  0.98 us (2%)
  between operations  0.74 us (1%)
    all_to_all x1, blocking collectives, shards(): lax.all_to_all(smooth, 'wide', split_axis=0, concat_axis=0, tiled=True)  17.5 us
    pallas_call x2, Pallas kernels, project(): pl.pallas_call(functools.partial(project_kernel, shift, shifts), in_specs...  17.3 us
    all_to_all x1, blocking collectives, shards(): lax.all_to_all(outs[-1], 'wide', split_axis=0, concat_axis=0, tiled=True)  16.8 us
    ppermute x1, starting transfers between devices, shards(): points.append(lax.ppermute(own, 'field', perm))  3 us
    pallas_call x1, Pallas kernels, restrict(): pl.pallas_call(functools.partial(restrict_kernel, len(tiles)), in_specs=[...  2.8 us
  transfers between devices with their start and end apart: 1, of which 0 were waited for; matrix products, arithmetic and copies ran while one was open for 0% of the time, Pallas kernels for 12%

profile of v4, /device:TPU:0, one launch (start us, length us, event | category | flops | bytes accessed | tf_op | source)
XLA Modules:
  0.0 60.4 jit_solution(9191588179652552717)
XLA Ops:
  0.6 1.0 %pad_maximum_fusion.refs_0_ = f32[7,8,1024]{2,1,0:T(8,128)S(1)} fusion(f32[1,8,1024]{2,1,0:T(8,128)} %bitcast.10, f32[3,8,1024]{2,1,0:T(8,128)} %bitcast.8, f32[3,8,1024]{2,1,0:T(8,128)} %bitcast.9), kind=kLoop, calls=%fused_computation | loop fusion | flops 114688 | bytes 458752 | tf_op jit(solution)/shard_map/concatenate | solution.py:372
  1.6 3.0 %collective-permute-start = (f32[7,8,1024]{2,1,0:T(8,128)S(1)}, f32[7,8,1024]{2,1,0:T(8,128)S(1)}, u32[]{:S(2)}, u32[]{:S(2)}) collective-permute-start(f32[7,8,1024]{2,1,0:T(8,128)S(1)} %pad_maximum_fusion.refs_0_), channel_id=1, source_target_pairs={{1,0},{0,1},{3,2},{2,3},{5,4},{4,5},{7,6},{6,7},{9,8},{8,9},{11,10... | collective-permute-start | bytes 688136 | tf_op jit(solution)/shard_map/ppermute | solution.py:383
  4.6 0.0 copy-start
  4.6 0.0 copy-start.2
  4.6 0.0 copy-start.3
  4.6 0.0 copy-start.4
  4.6 0.0 copy-start.5
  4.6 0.0 copy-start.6
  4.6 7.5 %project.2.refs_3_.refs_0_ = bf16[8,512,512]{2,1,0:T(8,128)(2,1)S(1)} custom-call(s32[1]{0:T(128)} %bitcast.place_ref, f32[7,8,1024]{2,1,0:T(8,128)S(1)} %pad_maximum_fusion.refs_0_), custom_call_target="tpu_custom_call" | custom-call | flops 4362076160 | bytes 4194304 | tf_op jit(solution)/shard_map/project/pallas_call | solution.py:204
  12.2 0.0 collective-permute-done.refs_0_
  12.2 0.0 copy-done
  12.2 0.0 copy-done.2
  12.2 0.0 copy-done.3
  12.2 0.0 copy-done.4
  12.2 0.0 copy-done.5
  12.3 0.0 copy-done.6
  12.3 0.0 copy-start.1
  12.3 9.8 %project.3 = (bf16[8,512,512]{2,1,0:T(8,128)(2,1)S(1)}, bf16[16,16,640]{2,1,0:T(8,128)(2,1)S(1)}) custom-call(s32[1]{0:T(128)} %bitcast.place_ref, f32[7,8,1024]{2,1,0:T(8,128)S(1)} %collective-permute-done.refs_0_, s32[16]{0:T(128)S(1)} %copy-done, bf16[8,16,512]{2,1,0:T(8,128)(2,1)S(1)} %copy-done.2, bf16[8,512,512]{2,1,0:T(8,128)(2,1)S(1)} %project.2.refs_3_.refs_0_, ...), custom_call_target="tpu_custom_call" | custom-call | flops 4362076160 | bytes 4194304 | tf_op jit(solution)/shard_map/project/pallas_call | solution.py:204
  22.1 16.8 %all_to_all.10.arrived_ref = bf16[16,16,640]{2,1,0:T(8,128)(2,1)S(1)} all-to-all(bf16[16,16,640]{2,1,0:T(8,128)(2,1)S(1)} %get-tuple-element.4), channel_id=1, replica_groups=mesh['wide'=16,'field'=2] {'wide'}, dimensions={0} | all-to-all | bytes 655360 | tf_op jit(solution)/shard_map/all_to_all | solution.py:403
  38.9 1.2 %coarse_stage.1 = bf16[16,32,512]{2,1,0:T(8,128)(2,1)S(1)} custom-call(bf16[16,16,640]{2,1,0:T(8,128)(2,1)S(1)} %all_to_all.10.arrived_ref), custom_call_target="tpu_custom_call" | custom-call | flops 268435456 | bytes 524288 | tf_op jit(solution)/shard_map/coarse_stage/pallas_call | solution.py:268
  40.1 17.5 %all_to_all.11.back_ref = bf16[16,32,512]{2,1,0:T(8,128)(2,1)S(1)} all-to-all(bf16[16,32,512]{2,1,0:T(8,128)(2,1)S(1)} %coarse_stage.1), channel_id=1, replica_groups=mesh['wide'=16,'field'=2] {'wide'}, dimensions={0} | all-to-all | bytes 1048576 | tf_op jit(solution)/shard_map/all_to_all | solution.py:405
  57.6 0.0 copy-done.1
  57.6 2.8 %restrict.1 = (bf16[16,16,512]{2,1,0:T(8,128)(2,1)}, bf16[8,16,512]{2,1,0:T(8,128)(2,1)}) custom-call(s32[1]{0:T(128)} %bitcast.place_ref, s32[16]{0:T(128)S(1)} %copy-done, f32[8]{0:T(128)S(1)} %copy-done.1, bf16[16,32,512]{2,1,0:T(8,128)(2,1)S(1)} %all_to_all.11.back_ref, bf16[8,512,512]{2,1,0:T(8,128)(2,1)S(1)} %project.2.refs_3_.refs_0_, ...), custom_call_target="tpu_custom_call" | custom-call | flops 134217728 | bytes 8388608 | tf_op jit(solution)/shard_map/restrict/pallas_call | solution.py:330
Async XLA Ops:
  1.6 10.6 %collective-permute-start = (f32[7,8,1024]{2,1,0:T(8,128)S(1)}, f32[7,8,1024]{2,1,0:T(8,128)S(1)}, u32[]{:S(2)}, u32[]{:S(2)}) collective-permute-start(f32[7,8,1024]{2,1,0:T(8,128)S(1)} %pad_maximum_fusion.refs_0_), channel_id=1, source_target_pairs={{1,0},{0,1},{3,2},{2,3},{5,4},{4,5},{7,6},{6,7},{9,8},{8,9},{11,10... | collective-permute-start | bytes 688136 | tf_op jit(solution)/shard_map/ppermute | solution.py:383
  4.6 7.6 %copy-start = (s32[16]{0:T(128)S(1)}, s32[16]{0:T(128)}, u32[]{:S(2)}) copy-start(s32[16]{0:T(128)} %fine_ids.1) | copy-start | bytes 196
  4.6 7.6 %copy-start.2 = (bf16[8,16,512]{2,1,0:T(8,128)(2,1)S(1)}, bf16[8,16,512]{2,1,0:T(8,128)(2,1)}, u32[]{:S(2)}) copy-start(bf16[8,16,512]{2,1,0:T(8,128)(2,1)} %refs_2_.1) | copy-start | bytes 393220
  4.6 7.6 %copy-start.3 = (s32[16,6]{0,1:T(8,128)S(1)}, s32[16,6]{0,1:T(8,128)}, u32[]{:S(2)}) copy-start(s32[16,6]{0,1:T(8,128)} %param.17) | copy-start | bytes 1156
  4.6 7.6 %copy-start.4 = (s32[16,1]{0,1:T(1,128)S(1)}, s32[16,1]{0,1:T(1,128)}, u32[]{:S(2)}) copy-start(s32[16,1]{0,1:T(1,128)} %param.15) | copy-start | bytes 196
  4.6 7.6 %copy-start.5 = (s32[16]{0:T(128)S(1)}, s32[16]{0:T(128)}, u32[]{:S(2)}) copy-start(s32[16]{0:T(128)} %refs_5_.1) | copy-start | bytes 196
  4.6 7.6 %copy-start.6 = (f32[16]{0:T(128)S(1)}, f32[16]{0:T(128)}, u32[]{:S(2)}) copy-start(f32[16]{0:T(128)} %refs_7_.1) | copy-start | bytes 196
  12.3 45.3 %copy-start.1 = (f32[8]{0:T(128)S(1)}, f32[8]{0:T(128)}, u32[]{:S(2)}) copy-start(f32[8]{0:T(128)} %inverse_ref.1) | copy-start | bytes 100

commit v5 on v2

--- a/solution.py
+++ b/solution.py
@@ -11,6 +11,7 @@
 NB = 8
 DIFFUSE = 0.125
 LANES = 128
+DIGIT = 7
 
 NT = (((1,), (1,)), ((), ()))
 NN = (((1,), (0,)), ((), ()))
@@ -24,8 +25,8 @@
     values = [jnp.ones_like(points), points]
     for degree in range(1, count - 1):
         values.append(
-            ((2 * degree + 1) * points * values[degree] - degree * values[degree - 1])
-            / (degree + 1)
+            ((2 * degree + 1) / (degree + 1)) * points * values[degree]
+            - (degree / (degree + 1)) * values[degree - 1]
         )
     values = values[:count]
     return [values[n] * math.sqrt((2 * n + 1) / 2.0) for n in range(count)]
@@ -35,37 +36,86 @@
     return slice(index * LANES, (index + 1) * LANES)
 
 
-def fill_table(table_ref, rows_ref, legs, base, pair):
-    here = pl.ds(pl.multiple_of(pair * NB, NB), NB)
-    for lane in range(legs.shape[1]):
-        first = legs[base, lane, here, :]
-        second = legs[base + 1, lane, here, :]
-        third = legs[base + 2, lane, here, :]
-        for a in range(NB):
-            rows_ref[lane, a * NB : (a + 1) * NB, :] = first[a : a + 1, :] * second
-        for ab in range(0, NB * NB, 2):
-            low = rows_ref[lane, ab : ab + 1, :] * third
-            high = rows_ref[lane, ab + 1 : ab + 2, :] * third
-            table_ref[ab * NB : (ab + 2) * NB, lanes(lane)] = jnp.concatenate(
-                [low, high], axis=0
-            ).astype(jnp.bfloat16)
+def spread(ref, coord, lane, row):
+    return jnp.broadcast_to(ref[coord, lane, pl.ds(row, 1), :], (NB, LANES))
+
+
+def fill_table(table_ref, legs, pair):
+    for side in range(2):
+        for lane in range(legs.shape[1]):
+            third = legs[2 * side + 1, lane, pl.ds(pair * NB, NB), :]
+            for b in range(0, NB, 2):
+                both = [
+                    spread(legs, 2 * side, lane, pair * NB + b + step) * third for step in range(2)
+                ]
+                table_ref[pair, side, b * NB : (b + 2) * NB, lanes(lane)] = jnp.concatenate(
+                    both, axis=0
+                ).astype(jnp.bfloat16)
+
+
+def transfer(coefs, table_ref, heads, pair, row, source):
+    block = coefs.shape[0]
+    quad = table_ref.shape[3]
+    side = lax.broadcasted_iota(jnp.int32, (block, LANES), 1) < NB * NB
+    keep = [
+        jnp.where(side, 1.0, 0.0).astype(jnp.bfloat16),
+        jnp.where(side, 0.0, 1.0).astype(jnp.bfloat16),
+    ]
+    masked = jnp.concatenate(
+        [coefs[:, lanes(a // 2)] * keep[a % 2] for a in range(NB)], axis=0
+    )
+    total = None
+    for start in range(0, quad, 2 * LANES):
+        columns = slice(start, start + 2 * LANES)
+        inward = table_ref[pair, source, :, columns]
+        outward = table_ref[pair, 1 - source, :, columns]
+        inner = lax.dot_general(
+            masked,
+            jnp.concatenate([inward, inward], axis=0),
+            NN,
+            preferred_element_type=jnp.float32,
+        )
+        outer = []
+        for half in range(2):
+            lane = start // LANES + half
+            pieces = [[] for _ in range(NB)]
+            for low in range(0, block, NB):
+                value = None
+                for a in range(NB):
+                    part = inner[a * block + low : a * block + low + NB, lanes(half)]
+                    part = part * spread(heads, source, lane, row + a)
+                    value = part if value is None else value + part
+                for a in range(NB):
+                    pieces[a].append(value * spread(heads, 1 - source, lane, row + a))
+            outer.append(jnp.concatenate([p for piece in pieces for p in piece], axis=0))
+        part = lax.dot_general(
+            jnp.concatenate(outer, axis=1).astype(jnp.bfloat16),
+            jnp.concatenate([outward, outward], axis=0),
+            NT,
+            preferred_element_type=jnp.float32,
+        )
+        total = part if total is None else total + part
+    return [
+        jnp.where(side, total[a * block : (a + 1) * block], total[(a + 1) * block : (a + 2) * block])
+        for a in range(0, NB, 2)
+    ]
 
 
 def facts(owner_ref, coarse_ref, faces_ref, inverse_ref, rows, pair_at):
-    elements, faces = faces_ref.shape
+    faces, elements = faces_ref.shape
     lane = lax.broadcasted_iota(jnp.int32, (1, LANES), 1)
     lines = []
     for row in range(rows):
         line = jnp.zeros((1, LANES), jnp.float32)
         if row < coarse_ref.shape[0]:
             pair = pair_at(row)
-            line = jnp.where(lane == 0, owner_ref[pair, 0].astype(jnp.float32), line)
+            line = jnp.where(lane == 0, owner_ref[0, pair].astype(jnp.float32), line)
             line = jnp.where(lane == 1, coarse_ref[pair].astype(jnp.float32), line)
         if row < elements:
             for face in range(faces):
-                name = faces_ref[row, face]
-                outer = lax.div(name, jnp.int32(elements))
-                inner = name - outer * elements
+                name = faces_ref[face, row]
+                outer = lax.shift_right_logical(name, DIGIT)
+                inner = name - lax.shift_left(outer, DIGIT)
                 line = jnp.where(lane == 2 + 2 * face, outer.astype(jnp.float32), line)
                 line = jnp.where(lane == 3 + 2 * face, inner.astype(jnp.float32), line)
             rest = jnp.full((1, LANES), inverse_ref[row], jnp.float32)
@@ -77,16 +127,18 @@
     return jnp.concatenate(lines, axis=0).astype(jnp.bfloat16)
 
 
-def project_kernel(shift, shifts, last, place_ref, fine_ref, *refs):
+def project_kernel(shift, shifts, place_ref, fine_ref, *refs):
+    last = shift == shifts - 1
+    refs = list(refs)
     if last:
         owner_ref, coarse_ref, faces_ref, inverse_ref = refs[:4]
         refs = refs[4:]
     points_ref, field_ref = refs[:2]
-    before = refs[2 : len(refs) - 12]
-    tile_ref, out_ref, legs, sums = refs[-12:-8]
-    rows, tables = refs[-8:-4], refs[-4:]
+    before = refs[2:-5]
+    table_ref, heads, out_ref, legs, sums = refs[-5:]
     pairs = points_ref.shape[1]
     block = field_ref.shape[1]
+    across = sums.shape[0]
 
     def pair_at(step, pair):
         part = place_ref[0] + step
@@ -94,42 +146,29 @@
 
     for lane in range(legs.shape[1]):
         for coord in range(6):
+            side, axis = divmod(coord, 3)
             values = legendre(points_ref[coord, :, lanes(lane)], NB)
             for n in range(NB):
-                value = values[n] * points_ref[6, :, lanes(lane)] if coord == 3 else values[n]
-                legs[coord, lane, pl.ds(n, pairs, stride=NB), :] = value
-
-    def fill(pair, slot):
-        fill_table(tables[2 * slot], rows[2 * slot], legs, 0, pair)
-        fill_table(tables[2 * slot + 1], rows[2 * slot + 1], legs, 3, pair)
-
-    def apply(pair, slot):
-        tile = lax.dot_general(
-            tables[2 * slot + 1][...], tables[2 * slot][...], NT, preferred_element_type=jnp.float32
-        ).astype(jnp.bfloat16)
-        tile_ref[pair] = tile
-        contrib = lax.dot_general(
-            field_ref[fine_ref[pair_at(shift, pair)]], tile, NT, preferred_element_type=jnp.float32
-        )
-        for lane in range(sums.shape[0]):
-            sums[lane, pl.ds(pair, block, stride=pairs), :] = contrib[:, lanes(lane)]
-
-    fill(0, 0)
-
-    @pl.loop(0, pairs // 2)
-    def _(step):
-        pair = 2 * step
-        fill(pair + 1, 1)
-        apply(pair, 0)
-        fill(jnp.minimum(pair + 2, pairs - 1), 0)
-        apply(pair + 1, 1)
+                rows = pl.ds(n, pairs, stride=NB)
+                if axis:
+                    legs[2 * side + axis - 1, lane, rows, :] = values[n]
+                elif side:
+                    heads[side, lane, rows, :] = values[n] * points_ref[6, :, lanes(lane)]
+                else:
+                    heads[side, lane, rows, :] = values[n]
+
+    for pair in range(pairs):
+        fill_table(table_ref, legs, pair)
+        coefs = field_ref[fine_ref[pair_at(shift, pair)]]
+        parts = transfer(coefs, table_ref, heads, pair, pair * NB, 0)
+        for lane in range(across):
+            sums[lane, pl.ds(pair, block, stride=pairs), :] = parts[lane]
 
     if not last:
         out_ref[...] = sums[...]
         return
     wide, total, span = out_ref.shape
     width = span - LANES
-    across = sums.shape[0]
     extra = facts(
         owner_ref,
         coarse_ref,
@@ -141,8 +180,7 @@
     sources = list(before) + [sums]
     for dest in range(wide):
         for piece in range(width // LANES):
-            column = dest * (width // LANES) + piece
-            row, lane = divmod(column, across)
+            row, lane = divmod(dest * (width // LANES) + piece, across)
             parts = [s[lane, row * pairs : (row + 1) * pairs, :] for s in sources]
             out_ref[dest, :, lanes(piece)] = jnp.concatenate(parts, axis=0).astype(jnp.bfloat16)
         out_ref[dest, :, lanes(width // LANES)] = extra
@@ -150,35 +188,34 @@
 
 def project(place, fine_ids, scalars, points, field, before, shift, shifts, wide):
     _, pairs, quad = points.shape
-    fine_count, block, basis = field.shape
+    _, block, basis = field.shape
     last = shift == shifts - 1
     across = basis // LANES
+    operands = [place, fine_ids] + (scalars if last else [])
+    vectors = [points, field] + (before if last else [])
     if last:
         out = jax.ShapeDtypeStruct(
             (wide, shifts * pairs, block * basis // wide + LANES), jnp.bfloat16
         )
     else:
         out = jax.ShapeDtypeStruct((across, block * pairs, LANES), jnp.float32)
-    operands = [place, fine_ids]
-    if last:
-        operands += scalars
-    specs = [SCALAR] * len(operands)
-    vectors = [points, field] + (before if last else [])
     return pl.pallas_call(
-        functools.partial(project_kernel, shift, shifts, last),
-        in_specs=specs + [VECTOR] * len(vectors),
-        out_specs=[VECTOR, VECTOR],
-        out_shape=[jax.ShapeDtypeStruct((pairs, basis, basis), jnp.bfloat16), out],
+        functools.partial(project_kernel, shift, shifts),
+        in_specs=[SCALAR] * len(operands) + [VECTOR] * len(vectors),
+        out_specs=[VECTOR] * 3,
+        out_shape=[
+            jax.ShapeDtypeStruct((pairs, 2, NB * NB, quad), jnp.bfloat16),
+            jax.ShapeDtypeStruct((2, quad // LANES, pairs * NB, LANES), jnp.float32),
+            out,
+        ],
         scratch_shapes=[
-            pltpu.VMEM((6, quad // LANES, pairs * NB, LANES), jnp.float32),
+            pltpu.VMEM((4, quad // LANES, pairs * NB, LANES), jnp.float32),
             pltpu.VMEM((across, block * pairs, LANES), jnp.float32),
-        ]
-        + [pltpu.VMEM((quad // LANES, NB * NB, LANES), jnp.float32)] * 4
-        + [pltpu.VMEM((basis, quad), jnp.bfloat16)] * 4,
+        ],
         compiler_params=pltpu.CompilerParams(vmem_limit_bytes=24 * 1024 * 1024),
         cost_estimate=pl.CostEstimate(
-            flops=2 * pairs * basis * basis * (quad + block),
-            bytes_accessed=2 * pairs * basis * basis,
+            flops=4 * pairs * NB * block * LANES * quad,
+            bytes_accessed=2 * pairs * NB * NB * quad,
             transcendentals=0,
         ),
         name="project",
@@ -200,7 +237,7 @@
         )
         hits = jnp.zeros((elements, count), jnp.float32)
         for face in range(faces):
-            index = fact[:elements, 2 + 2 * face : 3 + 2 * face] * elements
+            index = fact[:elements, 2 + 2 * face : 3 + 2 * face] * float(1 << DIGIT)
             index = index + fact[:elements, 3 + 2 * face : 4 + 2 * face]
             hits = hits + (index == name[:elements]).astype(jnp.float32)
         near[source * elements : (source + 1) * elements, :] = hits.astype(jnp.bfloat16)
@@ -250,8 +287,8 @@
 
 
 def restrict_kernel(shifts, place_ref, fine_ids, inverse_ref, back_ref, *refs):
-    tiles = refs[:shifts]
-    coarse_ref, fine_ref, rows, sums = refs[shifts:]
+    tables, heads = refs[:shifts], refs[shifts : 2 * shifts]
+    coarse_ref, fine_ref, rows, sums = refs[2 * shifts :]
     wide, targets, width = back_ref.shape
     elements, block, _ = coarse_ref.shape
     fine_count = fine_ref.shape[0]
@@ -271,29 +308,37 @@
     for shift in range(shifts):
         part = place_ref[0] + shift
         part = jnp.where(part >= shifts, part - shifts, part)
-        pairs = tiles[shift].shape[0]
-        for pair in range(pairs):
-            term = lax.dot_general(
-                picked(elements + shift * pairs + pair),
-                tiles[shift][pair],
-                NN,
-                preferred_element_type=jnp.float32,
-            )
+        pairs = tables[shift].shape[0]
+
+        def turn(pair):
+            start = pair * NB
+            if not isinstance(pair, int):
+                start = pl.multiple_of(start, NB)
+            coefs = picked(elements + shift * pairs + pair)
+            parts = transfer(coefs, tables[shift], heads[shift], pair, start, 1)
             fine = fine_ids[part * pairs + pair]
-            sums[fine] += term.astype(jnp.bfloat16).astype(jnp.float32)
+            for lane in range(across):
+                sums[fine, :, lanes(lane)] += parts[lane].astype(jnp.bfloat16).astype(jnp.float32)
+
+        if shifts <= 2:
+            for pair in range(pairs):
+                turn(pair)
+        else:
+            pl.loop(0, pairs)(turn)
     for element in range(elements):
         coarse_ref[element] = picked(element)
     for fine in range(fine_count):
         fine_ref[fine] = (inverse_ref[fine] * sums[fine]).astype(jnp.bfloat16)
 
 
-def restrict(place, fine_ids, inverse, back, tiles, elements, block):
-    pairs, basis, _ = tiles[0].shape
+def restrict(place, fine_ids, inverse, back, tables, heads, elements, block):
+    pairs, _, _, quad = tables[0].shape
     fine_count = inverse.shape[0]
     targets = back.shape[1]
+    basis = NB * NB * NB
     return pl.pallas_call(
-        functools.partial(restrict_kernel, len(tiles)),
-        in_specs=[SCALAR] * 3 + [VECTOR] * (1 + len(tiles)),
+        functools.partial(restrict_kernel, len(tables)),
+        in_specs=[SCALAR] * 3 + [VECTOR] * (1 + 2 * len(tables)),
         out_specs=[VECTOR, VECTOR],
         out_shape=[
             jax.ShapeDtypeStruct((elements, block, basis), jnp.bfloat16),
@@ -304,15 +349,15 @@
             pltpu.VMEM((fine_count, block, basis), jnp.float32),
         ],
         compiler_params=pltpu.CompilerParams(
-            vmem_limit_bytes=(16 if len(tiles) <= 2 else 56) * 1024 * 1024
+            vmem_limit_bytes=(24 if len(tables) <= 2 else 56) * 1024 * 1024
         ),
         cost_estimate=pl.CostEstimate(
-            flops=2 * len(tiles) * pairs * basis * basis * block,
-            bytes_accessed=2 * len(tiles) * pairs * basis * basis,
+            flops=4 * len(tables) * pairs * NB * block * LANES * quad,
+            bytes_accessed=2 * len(tables) * pairs * NB * NB * quad,
             transcendentals=0,
         ),
         name="restrict",
-    )(place, fine_ids, inverse, back, *tiles)
+    )(place, fine_ids, inverse, back, *tables, *heads)
 
 
 def shards(
@@ -346,19 +391,19 @@
         perm = [((i + shift) % nfield, i) for i in range(nfield)]
         points.append(lax.ppermute(own, "field", perm))
 
-    scalars = [pair_owner, pair_coarse, coarse_faces, coarse_inv_mass]
-    tiles = []
-    outs = []
+    scalars = [pair_owner.T, pair_coarse, coarse_faces.T, coarse_inv_mass]
+    tables, heads, outs = [], [], []
     for shift in range(nfield):
-        tile, out = project(
+        table, head, out = project(
             place, pair_fine, scalars, points[shift], fine_field_in, outs, shift, nfield, nwide
         )
-        tiles.append(tile)
+        tables.append(table)
+        heads.append(head)
         outs.append(out)
     arrived = lax.all_to_all(outs[-1], "wide", split_axis=0, concat_axis=0, tiled=True)
     smooth = coarse_stage(arrived, elements, faces)
     back = lax.all_to_all(smooth, "wide", split_axis=0, concat_axis=0, tiled=True)
-    return restrict(place, pair_fine, fine_inv_mass, back, tiles, elements, block)
+    return restrict(place, pair_fine, fine_inv_mass, back, tables, heads, elements, block)
 
 
 def solution(mesh):

time: 65.5 us -> 53.2 us (0.81)
  Pallas kernels: 23.1 us -> 10.3 us
  waiting for transfers between devices: 0.01 us -> 1.71 us
  local copies, waits for them, and re-layouts: 3.07 us -> 1.59 us
    pallas_call x3, Pallas kernels: 21.9 us -> 9.12 us  [the longest x2 4.84 us: project(): pl.pallas_call(functools.partial(project_kernel, shift, shifts), in_specs...]
    ppermute x1, waiting for transfers between devices: 0.01 us -> 1.71 us  [shards(): points.append(lax.ppermute(own, 'field', perm))]
    unnamed x14 -> x18, local copies, waits for them, and re-layouts: 3.07 us -> 1.59 us
  transfers between devices with their start and end apart: 1 -> 1, of which waited for: 0 -> 1; matrix products, arithmetic and copies ran while one was open for 2% -> 0% of each run, Pallas kernels for 14% -> 4%
where the time goes in v5:
time: 53.2 us; the launch traced here: 53 us
  blocking collectives  34.6 us (65%)
  Pallas kernels  10.3 us (19%)
  starting transfers between devices  3 us (6%)
  waiting for transfers between devices  1.71 us (3%)
  local copies, waits for them, and re-layouts  1.59 us (3%)
  other arithmetic  1.05 us (2%)
  between operations  0.74 us (1%)
    all_to_all x1, blocking collectives, shards(): lax.all_to_all(smooth, 'wide', split_axis=0, concat_axis=0, tiled=True)  17.5 us
    all_to_all x1, blocking collectives, shards(): lax.all_to_all(outs[-1], 'wide', split_axis=0, concat_axis=0, tiled=True)  17.1 us
    pallas_call x2, Pallas kernels, project(): pl.pallas_call(functools.partial(project_kernel, shift, shifts), in_specs...  4.84 us
    pallas_call x1, Pallas kernels, restrict(): pl.pallas_call(functools.partial(restrict_kernel, len(tables)), in_specs=...  4.28 us
    ppermute x1, starting transfers between devices, shards(): points.append(lax.ppermute(own, 'field', perm))  3 us
    ppermute x1, waiting for transfers between devices, shards(): points.append(lax.ppermute(own, 'field', perm))  1.71 us
    unnamed x18, local copies, waits for them, and re-layouts  1.59 us
    pallas_call x1, Pallas kernels, coarse_stage(): pl.pallas_call(functools.partial(coarse_kernel, faces, elements), in_spec...  1.2 us
  transfers between devices with their start and end apart: 1, of which 1 were waited for; matrix products, arithmetic and copies ran while one was open for 0% of the time, Pallas kernels for 4%

profile of v5, /device:TPU:0, one launch (start us, length us, event | category | flops | bytes accessed | tf_op | source)
XLA Modules:
  0.0 53.0 jit_solution(1260929555579020325)
XLA Ops:
  0.6 0.0 copy-start.4
  0.6 0.0 copy-start.8
  0.7 0.0 copy-start.5
  0.7 0.0 copy-start.7
  0.7 0.0 copy-start.6
  0.7 1.1 %pad_maximum_fusion.refs_0_ = f32[7,8,1024]{2,1,0:T(8,128)S(1)} fusion(f32[1,8,1024]{2,1,0:T(8,128)} %bitcast.10, f32[3,8,1024]{2,1,0:T(8,128)} %bitcast.8, f32[3,8,1024]{2,1,0:T(8,128)} %bitcast.9), kind=kLoop, calls=%fused_computation | loop fusion | flops 114688 | bytes 458752 | tf_op jit(solution)/shard_map/concatenate | solution.py:381
  1.7 3.0 %collective-permute-start = (f32[7,8,1024]{2,1,0:T(8,128)S(1)}, f32[7,8,1024]{2,1,0:T(8,128)S(1)}, u32[]{:S(2)}, u32[]{:S(2)}) collective-permute-start(f32[7,8,1024]{2,1,0:T(8,128)S(1)} %pad_maximum_fusion.refs_0_), channel_id=1, source_target_pairs={{1,0},{0,1},{3,2},{2,3},{5,4},{4,5},{7,6},{6,7},{9,8},{8,9},{11,10... | collective-permute-start | bytes 688136 | tf_op jit(solution)/shard_map/ppermute | solution.py:392
  4.7 0.0 copy-start
  4.7 0.7 %copy-done = s32[16]{0:T(128)S(1)} copy-done((s32[16]{0:T(128)S(1)}, s32[16]{0:T(128)}, u32[]{:S(2)}) %copy-start) | copy-done | bytes 88
  5.4 0.0 copy-start.3
  5.4 0.9 %copy-done.3 = bf16[8,16,512]{2,1,0:T(8,128)(2,1)S(1)} copy-done((bf16[8,16,512]{2,1,0:T(8,128)(2,1)S(1)}, bf16[8,16,512]{2,1,0:T(8,128)(2,1)}, u32[]{:S(2)}) %copy-start.3) | copy-done | bytes 131096
  6.3 2.3 %project.2 = (bf16[8,2,64,1024]{3,2,1,0:T(8,128)(2,1)S(1)}, f32[2,8,64,128]{3,2,1,0:T(8,128)S(1)}, f32[4,128,128]{2,1,0:T(8,128)S(1)}) custom-call(s32[1]{0:T(128)} %bitcast.place_ref, s32[16]{0:T(128)S(1)} %copy-done, f32[7,8,1024]{2,1,0:T(8,128)S(1)} %pad_maximum_fusion.refs_0_, bf16[8,16,512]{2,1,0:T(8,128)(2,1)S(1)} %copy-done.3), custom_call_target="tpu_custom_call" | custom-call | flops 536870912 | bytes 1048576 | tf_op jit(solution)/shard_map/project/pallas_call | solution.py:202
  8.6 1.7 %collective-permute-done.refs_4_ = f32[7,8,1024]{2,1,0:T(8,128)S(1)} collective-permute-done((f32[7,8,1024]{2,1,0:T(8,128)S(1)}, f32[7,8,1024]{2,1,0:T(8,128)S(1)}, u32[]{:S(2)}, u32[]{:S(2)}) %collective-permute-start) | collective-permute-done | bytes 229408 | tf_op jit(solution)/shard_map/ppermute | solution.py:392
  10.3 0.0 copy-done.4
  10.3 0.0 copy-done.8
  10.4 0.0 copy-done.5
  10.4 0.0 copy-done.7
  10.4 0.0 copy-done.6
  10.4 0.0 copy-start.1
  10.4 0.0 copy-start.2
  10.4 2.5 %project.3 = (bf16[8,2,64,1024]{3,2,1,0:T(8,128)(2,1)S(1)}, f32[2,8,64,128]{3,2,1,0:T(8,128)S(1)}, bf16[16,16,640]{2,1,0:T(8,128)(2,1)S(1)}) custom-call(s32[1]{0:T(128)} %bitcast.place_ref, s32[16]{0:T(128)S(1)} %copy-done, s32[1,16]{1,0:T(1,128)S(1)} %bitcast.7, s32[16]{0:T(128)S(1)} %copy-done.7, s32[6,16]{1,0:T(8,128)S(1)} %bitcast.6, f32[16]{0:T(128)S(1)} %copy-done.8, ...), custom_call_target="tpu_custom_call" | custom-call | flops 536870912 | bytes 1048576 | tf_op jit(solution)/shard_map/project/pallas_call | solution.py:202
  12.9 17.1 %all_to_all.10.arrived_ref = bf16[16,16,640]{2,1,0:T(8,128)(2,1)S(1)} all-to-all(bf16[16,16,640]{2,1,0:T(8,128)(2,1)S(1)} %get-tuple-element.9), channel_id=1, replica_groups=mesh['wide'=16,'field'=2] {'wide'}, dimensions={0} | all-to-all | bytes 655360 | tf_op jit(solution)/shard_map/all_to_all | solution.py:403
  30.0 1.2 %coarse_stage.1 = bf16[16,32,512]{2,1,0:T(8,128)(2,1)S(1)} custom-call(bf16[16,16,640]{2,1,0:T(8,128)(2,1)S(1)} %all_to_all.10.arrived_ref), custom_call_target="tpu_custom_call" | custom-call | flops 268435456 | bytes 524288 | tf_op jit(solution)/shard_map/coarse_stage/pallas_call | solution.py:269
  31.2 17.5 %all_to_all.11.back_ref = bf16[16,32,512]{2,1,0:T(8,128)(2,1)S(1)} all-to-all(bf16[16,32,512]{2,1,0:T(8,128)(2,1)S(1)} %coarse_stage.1), channel_id=1, replica_groups=mesh['wide'=16,'field'=2] {'wide'}, dimensions={0} | all-to-all | bytes 1048576 | tf_op jit(solution)/shard_map/all_to_all | solution.py:405
  48.7 0.0 copy-done.1
  48.7 0.0 copy-done.2
  48.7 4.3 %restrict.1 = (bf16[16,16,512]{2,1,0:T(8,128)(2,1)}, bf16[8,16,512]{2,1,0:T(8,128)(2,1)}) custom-call(s32[1]{0:T(128)} %bitcast.place_ref, s32[16]{0:T(128)S(1)} %copy-done.1, f32[8]{0:T(128)S(1)} %copy-done.2, bf16[16,32,512]{2,1,0:T(8,128)(2,1)S(1)} %all_to_all.11.back_ref, bf16[8,2,64,1024]{3,2,1,0:T(8,128)(2,1)S(1)} %get-tuple-element.10.refs_0_, ...), custom_call_target="tpu_custom_call" | custom-call | flops 1073741824 | bytes 2097152 | tf_op jit(solution)/shard_map/restrict/pallas_call | solution.py:339
Async XLA Ops:
  0.6 9.7 %copy-start.4 = (bf16[8,16,512]{2,1,0:T(8,128)(2,1)S(1)}, bf16[8,16,512]{2,1,0:T(8,128)(2,1)}, u32[]{:S(2)}) copy-start(bf16[8,16,512]{2,1,0:T(8,128)(2,1)} %refs_5_.1) | copy-start | bytes 393220
  0.6 9.7 %copy-start.8 = (f32[16]{0:T(128)S(1)}, f32[16]{0:T(128)}, u32[]{:S(2)}) copy-start(f32[16]{0:T(128)} %refs_3_.1) | copy-start | bytes 196
  0.7 9.7 %copy-start.5 = (s32[16,6]{0,1:T(8,128)S(1)}, s32[16,6]{0,1:T(8,128)}, u32[]{:S(2)}) copy-start(s32[16,6]{0,1:T(8,128)} %param.17) | copy-start | bytes 1156
  0.7 9.7 %copy-start.7 = (s32[16]{0:T(128)S(1)}, s32[16]{0:T(128)}, u32[]{:S(2)}) copy-start(s32[16]{0:T(128)} %refs_1_.3) | copy-start | bytes 196
  0.7 9.7 %copy-start.6 = (s32[16,1]{0,1:T(1,128)S(1)}, s32[16,1]{0,1:T(1,128)}, u32[]{:S(2)}) copy-start(s32[16,1]{0,1:T(1,128)} %param.15) | copy-start | bytes 196
  1.7 8.6 %collective-permute-start = (f32[7,8,1024]{2,1,0:T(8,128)S(1)}, f32[7,8,1024]{2,1,0:T(8,128)S(1)}, u32[]{:S(2)}, u32[]{:S(2)}) collective-permute-start(f32[7,8,1024]{2,1,0:T(8,128)S(1)} %pad_maximum_fusion.refs_0_), channel_id=1, source_target_pairs={{1,0},{0,1},{3,2},{2,3},{5,4},{4,5},{7,6},{6,7},{9,8},{8,9},{11,10... | collective-permute-start | bytes 688136 | tf_op jit(solution)/shard_map/ppermute | solution.py:392
  4.7 0.7 %copy-start = (s32[16]{0:T(128)S(1)}, s32[16]{0:T(128)}, u32[]{:S(2)}) copy-start(s32[16]{0:T(128)} %fine_ids.1) | copy-start | bytes 196
  5.4 0.9 %copy-start.3 = (bf16[8,16,512]{2,1,0:T(8,128)(2,1)S(1)}, bf16[8,16,512]{2,1,0:T(8,128)(2,1)}, u32[]{:S(2)}) copy-start(bf16[8,16,512]{2,1,0:T(8,128)(2,1)} %refs_5_.1) | copy-start | bytes 393220
  10.4 38.3 %copy-start.1 = (s32[16]{0:T(128)S(1)}, s32[16]{0:T(128)}, u32[]{:S(2)}) copy-start(s32[16]{0:T(128)} %fine_ids.1) | copy-start | bytes 196
  10.4 38.3 %copy-start.2 = (f32[8]{0:T(128)S(1)}, f32[8]{0:T(128)}, u32[]{:S(2)}) copy-start(f32[8]{0:T(128)} %inverse_ref.1) | copy-start | bytes 100

commit v6 on v5

--- a/solution.py
+++ b/solution.py
@@ -12,6 +12,7 @@
 DIFFUSE = 0.125
 LANES = 128
 DIGIT = 7
+PACK = 16
 
 NT = (((1,), (1,)), ((), ()))
 NN = (((1,), (0,)), ((), ()))
@@ -101,24 +102,23 @@
     ]
 
 
-def facts(owner_ref, coarse_ref, faces_ref, inverse_ref, rows, pair_at):
-    faces, elements = faces_ref.shape
+def facts(given_ref, total, elements, faces, rows, pair_at):
     lane = lax.broadcasted_iota(jnp.int32, (1, LANES), 1)
     lines = []
-    for row in range(rows):
-        line = jnp.zeros((1, LANES), jnp.float32)
-        if row < coarse_ref.shape[0]:
-            pair = pair_at(row)
-            line = jnp.where(lane == 0, owner_ref[0, pair].astype(jnp.float32), line)
-            line = jnp.where(lane == 1, coarse_ref[pair].astype(jnp.float32), line)
+    for row in rows:
+        pair = pair_at(row)
+        line = jnp.where(lane == 0, given_ref[total + pair], 0.0)
+        line = jnp.where(lane == 1, given_ref[2 * total + pair], line)
         if row < elements:
             for face in range(faces):
-                name = faces_ref[face, row]
+                name = given_ref[3 * total + face * elements + row].astype(jnp.int32)
                 outer = lax.shift_right_logical(name, DIGIT)
                 inner = name - lax.shift_left(outer, DIGIT)
                 line = jnp.where(lane == 2 + 2 * face, outer.astype(jnp.float32), line)
                 line = jnp.where(lane == 3 + 2 * face, inner.astype(jnp.float32), line)
-            rest = jnp.full((1, LANES), inverse_ref[row], jnp.float32)
+            rest = jnp.full(
+                (1, LANES), given_ref[3 * total + faces * elements + row], jnp.float32
+            )
             for part in range(3):
                 head = rest.astype(jnp.bfloat16).astype(jnp.float32)
                 line = jnp.where(lane == 2 + 2 * faces + part, head, line)
@@ -127,15 +127,23 @@
     return jnp.concatenate(lines, axis=0).astype(jnp.bfloat16)
 
 
-def project_kernel(shift, shifts, place_ref, fine_ref, *refs):
-    last = shift == shifts - 1
-    refs = list(refs)
-    if last:
-        owner_ref, coarse_ref, faces_ref, inverse_ref = refs[:4]
-        refs = refs[4:]
-    points_ref, field_ref = refs[:2]
-    before = refs[2:-5]
-    table_ref, heads, out_ref, legs, sums = refs[-5:]
+def project_kernel(
+    shift,
+    shifts,
+    fold,
+    width,
+    elements,
+    faces,
+    place_ref,
+    given_ref,
+    points_ref,
+    field_ref,
+    table_ref,
+    heads,
+    out_ref,
+    legs,
+    sums,
+):
     pairs = points_ref.shape[1]
     block = field_ref.shape[1]
     across = sums.shape[0]
@@ -159,54 +167,52 @@
 
     for pair in range(pairs):
         fill_table(table_ref, legs, pair)
-        coefs = field_ref[fine_ref[pair_at(shift, pair)]]
+        coefs = field_ref[given_ref[pair_at(shift, pair)].astype(jnp.int32)]
         parts = transfer(coefs, table_ref, heads, pair, pair * NB, 0)
         for lane in range(across):
             sums[lane, pl.ds(pair, block, stride=pairs), :] = parts[lane]
 
-    if not last:
-        out_ref[...] = sums[...]
-        return
-    wide, total, span = out_ref.shape
-    width = span - LANES
-    extra = facts(
-        owner_ref,
-        coarse_ref,
-        faces_ref,
-        inverse_ref,
-        total,
-        lambda row: pair_at(row // pairs, row % pairs),
-    )
-    sources = list(before) + [sums]
-    for dest in range(wide):
-        for piece in range(width // LANES):
-            row, lane = divmod(dest * (width // LANES) + piece, across)
-            parts = [s[lane, row * pairs : (row + 1) * pairs, :] for s in sources]
-            out_ref[dest, :, lanes(piece)] = jnp.concatenate(parts, axis=0).astype(jnp.bfloat16)
-        out_ref[dest, :, lanes(width // LANES)] = extra
-
-
-def project(place, fine_ids, scalars, points, field, before, shift, shifts, wide):
+    wide = out_ref.shape[0]
+    pieces = width // LANES
+    slices = block * across // pieces
+    for part in range(slices):
+        for piece in range(pieces // fold):
+            stack = []
+            for turn in range(fold):
+                row, lane = divmod(part * pieces + turn * (pieces // fold) + piece, across)
+                stack.append(sums[lane, row * pairs : (row + 1) * pairs, :])
+            value = jnp.concatenate(stack, axis=0).astype(jnp.bfloat16)
+            for dest in range(part, wide, slices):
+                out_ref[dest, :, lanes(piece)] = value
+    if shift == 0:
+        span = fold * pairs
+        for group in range(shifts // fold):
+            extra = facts(
+                given_ref,
+                shifts * pairs,
+                elements,
+                faces,
+                range(group * span, (group + 1) * span),
+                lambda row: pair_at(row // pairs, row % pairs),
+            )
+            for dest in range(wide):
+                out_ref[dest, :, lanes(pieces // fold + group)] = extra
+
+
+def project(place, given, points, field, shift, shifts, wide, fold, width, elements, faces):
     _, pairs, quad = points.shape
     _, block, basis = field.shape
-    last = shift == shifts - 1
     across = basis // LANES
-    operands = [place, fine_ids] + (scalars if last else [])
-    vectors = [points, field] + (before if last else [])
-    if last:
-        out = jax.ShapeDtypeStruct(
-            (wide, shifts * pairs, block * basis // wide + LANES), jnp.bfloat16
-        )
-    else:
-        out = jax.ShapeDtypeStruct((across, block * pairs, LANES), jnp.float32)
+    first = shift == 0
+    span = width // fold + (shifts // fold * LANES if first else 0)
     return pl.pallas_call(
-        functools.partial(project_kernel, shift, shifts),
-        in_specs=[SCALAR] * len(operands) + [VECTOR] * len(vectors),
+        functools.partial(project_kernel, shift, shifts, fold, width, elements, faces),
+        in_specs=[SCALAR] * 2 + [VECTOR] * 2,
         out_specs=[VECTOR] * 3,
         out_shape=[
             jax.ShapeDtypeStruct((pairs, 2, NB * NB, quad), jnp.bfloat16),
             jax.ShapeDtypeStruct((2, quad // LANES, pairs * NB, LANES), jnp.float32),
-            out,
+            jax.ShapeDtypeStruct((wide, fold * pairs, span), jnp.bfloat16),
         ],
         scratch_shapes=[
             pltpu.VMEM((4, quad // LANES, pairs * NB, LANES), jnp.float32),
@@ -219,71 +225,118 @@
             transcendentals=0,
         ),
         name="project",
-    )(*operands, *vectors)
-
-
-def coarse_kernel(faces, elements, arrived_ref, out_ref, pick, near, moved):
-    wide, rows, span = arrived_ref.shape
-    width = span - LANES
-    count = wide * elements
+    )(place, given, points, field)
+
+
+def plan_kernel(faces, elements, start, arrived_ref, pick, near, inverse):
+    wide, _, span = arrived_ref.shape
+    rows, count = pick.shape[0] // wide, pick.shape[1]
     name = lax.broadcasted_iota(jnp.int32, (rows, count), 1).astype(jnp.float32)
-    inverse = []
     for source in range(wide):
-        fact = arrived_ref[source, :, width:].astype(jnp.float32)
-        moved[source * rows : (source + 1) * rows, :] = arrived_ref[source, :, :width]
+        groups = [
+            arrived_ref[source, :, column : column + LANES].astype(jnp.float32)
+            for column in range(start, span, LANES)
+        ]
+        fact = jnp.concatenate(groups, axis=0)
         index = fact[:, 0:1] * elements + fact[:, 1:2]
         pick[source * rows : (source + 1) * rows, :] = (index == name).astype(jnp.float32).astype(
             jnp.bfloat16
         )
+        fact = fact[:elements]
         hits = jnp.zeros((elements, count), jnp.float32)
         for face in range(faces):
-            index = fact[:elements, 2 + 2 * face : 3 + 2 * face] * float(1 << DIGIT)
-            index = index + fact[:elements, 3 + 2 * face : 4 + 2 * face]
+            index = fact[:, 2 + 2 * face : 3 + 2 * face] * float(1 << DIGIT)
+            index = index + fact[:, 3 + 2 * face : 4 + 2 * face]
             hits = hits + (index == name[:elements]).astype(jnp.float32)
-        near[source * elements : (source + 1) * elements, :] = hits.astype(jnp.bfloat16)
+        here = slice(source * elements, (source + 1) * elements)
+        near[here, :] = hits.astype(jnp.bfloat16)
         first = 2 + 2 * faces
-        inverse.append(
-            fact[:elements, first : first + 1]
-            + fact[:elements, first + 1 : first + 2]
-            + fact[:elements, first + 2 : first + 3]
+        value = (
+            fact[:, first : first + 1]
+            + fact[:, first + 1 : first + 2]
+            + fact[:, first + 2 : first + 3]
         )
+        inverse[here, :] = jnp.broadcast_to(value, (elements, LANES))
+
+
+def plan(arrived, elements, faces, rows, start):
+    wide = arrived.shape[0]
+    count = wide * elements
+    return pl.pallas_call(
+        functools.partial(plan_kernel, faces, elements, start),
+        in_specs=[VECTOR],
+        out_specs=[VECTOR] * 3,
+        out_shape=[
+            jax.ShapeDtypeStruct((wide * rows, count), jnp.bfloat16),
+            jax.ShapeDtypeStruct((count, count), jnp.bfloat16),
+            jax.ShapeDtypeStruct((count, LANES), jnp.float32),
+        ],
+        compiler_params=pltpu.CompilerParams(vmem_limit_bytes=24 * 1024 * 1024),
+        cost_estimate=pl.CostEstimate(
+            flops=16 * count * count, bytes_accessed=4 * count * count, transcendentals=0
+        ),
+        name="plan",
+    )(arrived)
+
+
+def coarse_kernel(
+    faces, elements, shifts, half_ref, pick, near, inverse_ref, *refs
+):
+    arrived = refs[:shifts]
+    out_ref, moved = refs[shifts:]
+    slices, _, width = out_ref.shape
+    wide, depth, part = arrived[-1].shape
+    fold = width // part
+    pairs = depth // fold
+    rows = shifts * pairs
+    for source in range(wide):
+        values = [a[source, :, :part].astype(jnp.float32) for a in arrived]
+        for turn in range(fold):
+            stack = [v[turn * pairs : (turn + 1) * pairs] for v in values]
+            moved[source * rows : (source + 1) * rows, turn * part : (turn + 1) * part] = (
+                jnp.concatenate(stack, axis=0).astype(jnp.bfloat16)
+            )
     load = lax.dot_general(pick[...], moved[...], TN, preferred_element_type=jnp.float32)
-    solved = jnp.concatenate(inverse, axis=0) * load
+    solved = inverse_ref[:, 0:1] * load
     high = solved.astype(jnp.bfloat16)
     low = (solved - high.astype(jnp.float32)).astype(jnp.bfloat16)
     beside = lax.dot_general(near[...], high, NN, preferred_element_type=jnp.float32)
     beside = beside + lax.dot_general(near[...], low, NN, preferred_element_type=jnp.float32)
     smooth = (solved + DIFFUSE * (beside - float(faces) * solved)).astype(jnp.bfloat16)
-    reply = lax.dot_general(pick[...], smooth, NN, preferred_element_type=jnp.float32).astype(
-        jnp.bfloat16
-    )
-    for dest in range(wide):
-        out_ref[dest, :elements, :] = smooth[dest * elements : (dest + 1) * elements, :]
+    moved_rows = slices * rows
+    mine = pl.ds(pl.multiple_of(half_ref[0] * moved_rows, moved_rows), moved_rows)
+    reply = lax.dot_general(
+        pick[mine, :], smooth, NN, preferred_element_type=jnp.float32
+    ).astype(jnp.bfloat16)
+    for dest in range(slices):
         out_ref[dest, elements:, :] = reply[dest * rows : (dest + 1) * rows, :]
-
-
-def coarse_stage(arrived, elements, faces):
-    wide, rows, span = arrived.shape
-    width = span - LANES
-    count = wide * elements
+    held = slices * elements
+    for half in range(wide // slices):
+
+        @pl.when(half_ref[0] == half)
+        def _():
+            for dest in range(slices):
+                start = half * held + dest * elements
+                out_ref[dest, :elements, :] = smooth[start : start + elements, :]
+
+
+def coarse_stage(half, pick, near, inverse, arrived, elements, faces, slices, width):
+    total, count = pick.shape
+    wide = arrived[0].shape[0]
     return pl.pallas_call(
-        functools.partial(coarse_kernel, faces, elements),
-        in_specs=[VECTOR],
+        functools.partial(coarse_kernel, faces, elements, len(arrived)),
+        in_specs=[SCALAR] + [VECTOR] * (3 + len(arrived)),
         out_specs=VECTOR,
-        out_shape=jax.ShapeDtypeStruct((wide, elements + rows, width), jnp.bfloat16),
-        scratch_shapes=[
-            pltpu.VMEM((wide * rows, count), jnp.bfloat16),
-            pltpu.VMEM((count, count), jnp.bfloat16),
-            pltpu.VMEM((wide * rows, width), jnp.bfloat16),
-        ],
-        compiler_params=pltpu.CompilerParams(vmem_limit_bytes=48 * 1024 * 1024),
+        out_shape=jax.ShapeDtypeStruct((slices, elements + total // wide, width), jnp.bfloat16),
+        scratch_shapes=[pltpu.VMEM((total, width), jnp.bfloat16)],
+        compiler_params=pltpu.CompilerParams(vmem_limit_bytes=40 * 1024 * 1024),
         cost_estimate=pl.CostEstimate(
-            flops=8 * count * wide * rows * width,
-            bytes_accessed=4 * wide * rows * width,
+            flops=8 * count * total * width,
+            bytes_accessed=4 * total * width,
             transcendentals=0,
         ),
         name="coarse_stage",
-    )(arrived)
+    )(half, pick, near, inverse, *arrived)
 
 
 def restrict_kernel(shifts, place_ref, fine_ids, inverse_ref, back_ref, *refs):
@@ -391,18 +444,41 @@
         perm = [((i + shift) % nfield, i) for i in range(nfield)]
         points.append(lax.ppermute(own, "field", perm))
 
-    scalars = [pair_owner.T, pair_coarse, coarse_faces.T, coarse_inv_mass]
-    tables, heads, outs = [], [], []
+    given = [pair_fine, pair_owner.reshape(-1), pair_coarse, coarse_faces.T.reshape(-1)]
+    given = jnp.concatenate([g.astype(jnp.float32) for g in given] + [coarse_inv_mass])
+    halves = 2 if nwide % 2 == 0 else 1
+    slices = nwide // halves
+    width = block * fine_field_in.shape[2] // slices
+    pairs = fine_points.shape[0]
+    fold = max(1, PACK // pairs)
+    if width % (fold * LANES) or nfield % fold:
+        fold = 1
+    half = (lax.axis_index("wide") // slices).astype(jnp.int32).reshape(1)
+
+    tables, heads, arrived = [], [], []
     for shift in range(nfield):
         table, head, out = project(
-            place, pair_fine, scalars, points[shift], fine_field_in, outs, shift, nfield, nwide
+            place,
+            given,
+            points[shift],
+            fine_field_in,
+            shift,
+            nfield,
+            nwide,
+            fold,
+            width,
+            elements,
+            faces,
         )
         tables.append(table)
         heads.append(head)
-        outs.append(out)
-    arrived = lax.all_to_all(outs[-1], "wide", split_axis=0, concat_axis=0, tiled=True)
-    smooth = coarse_stage(arrived, elements, faces)
-    back = lax.all_to_all(smooth, "wide", split_axis=0, concat_axis=0, tiled=True)
+        arrived.append(lax.all_to_all(out, "wide", split_axis=0, concat_axis=0, tiled=True))
+    pick, near, inverse = plan(arrived[0], elements, faces, nfield * pairs, width // fold)
+    smooth = coarse_stage(half, pick, near, inverse, arrived, elements, faces, slices, width)
+    groups = [list(range(first, first + slices)) for first in range(0, nwide, slices)]
+    back = lax.all_to_all(
+        smooth, "wide", split_axis=0, concat_axis=0, axis_index_groups=groups, tiled=True
+    )
     return restrict(place, pair_fine, fine_inv_mass, back, tables, heads, elements, block)
 
 

time: 53.2 us -> 66.7 us (1.25)
  blocking collectives: 34.6 us -> 11.3 us
  starting transfers between devices: 3 us -> 14.9 us
  waiting for transfers between devices: 1.71 us -> 12.2 us
  local copies, waits for them, and re-layouts: 1.59 us -> 9.48 us
  Pallas kernels: 10.3 us -> 13.9 us
  other arithmetic: 1.05 us -> 3.64 us
    all_to_all x2 -> x1, blocking collectives: 34.6 us -> 11.3 us  [shards(): lax.all_to_all(smooth, 'wide', split_axis=0, concat_axis=0, axis_index_gr...]
    all_to_all x0 -> x2, starting transfers between devices: none -> 13.3 us  [shards(): lax.all_to_all(out, 'wide', split_axis=0, concat_axis=0, tiled=True)]
    unnamed x18 -> x26, local copies, waits for them, and re-layouts: 1.59 us -> 8.67 us
    all_to_all x0 -> x2, waiting for transfers between devices: none -> 5.85 us  [shards(): lax.all_to_all(out, 'wide', split_axis=0, concat_axis=0, tiled=True)]
    ppermute x1, waiting for transfers between devices: 1.71 us -> 6.36 us  [shards(): points.append(lax.ppermute(own, 'field', perm))]
    pallas_call x3 -> x4, Pallas kernels: 6.03 us -> 9.65 us  [the longest x2 5.54 us: project(): pl.pallas_call(functools.partial(project_kernel, shift, shifts, fold, wid...]
    convert_element_type x0 -> x4, other arithmetic: none -> 2.66 us  [shards(): g.astype(jnp.float32)]
    ppermute x1, starting transfers between devices: 3 us -> 1.55 us  [shards(): points.append(lax.ppermute(own, 'field', perm))]
  transfers between devices with their start and end apart: 1 -> 3, of which waited for: 1 -> 2; matrix products, arithmetic and copies ran while one was open for 0% -> 0% of each run, Pallas kernels for 4% -> 7%
where the time goes in v6:
time: 66.7 us; the launch traced here: 66.2 us
  starting transfers between devices  14.9 us (22%)
  Pallas kernels  13.9 us (21%)
  waiting for transfers between devices  12.2 us (18%)
  blocking collectives  11.3 us (17%)
  local copies, waits for them, and re-layouts  9.48 us (14%)
  other arithmetic  3.64 us (5%)
  between operations  0.72 us (1%)
    all_to_all x2, starting transfers between devices, shards(): lax.all_to_all(out, 'wide', split_axis=0, concat_axis=0, tiled=True)  13.3 us
    all_to_all x1, blocking collectives, shards(): lax.all_to_all(smooth, 'wide', split_axis=0, concat_axis=0, axis_index_gr...  11.3 us
    unnamed x26, local copies, waits for them, and re-layouts  8.67 us
    ppermute x1, waiting for transfers between devices, shards(): points.append(lax.ppermute(own, 'field', perm))  6.36 us
    all_to_all x2, waiting for transfers between devices, shards(): lax.all_to_all(out, 'wide', split_axis=0, concat_axis=0, tiled=True)  5.85 us
    pallas_call x2, Pallas kernels, project(): pl.pallas_call(functools.partial(project_kernel, shift, shifts, fold, wid...  5.54 us
    pallas_call x1, Pallas kernels, restrict(): pl.pallas_call(functools.partial(restrict_kernel, len(tables)), in_specs=...  4.28 us
    convert_element_type x4, other arithmetic, shards(): g.astype(jnp.float32)  2.66 us
  transfers between devices with their start and end apart: 3, of which 2 were waited for; matrix products, arithmetic and copies ran while one was open for 0% of the time, Pallas kernels for 7%

profile of v6, /device:TPU:0, one launch (start us, length us, event | category | flops | bytes accessed | tf_op | source)
XLA Modules:
  0.0 66.2 jit_solution(11230735208077052818)
XLA Ops:
  0.6 0.7 convert_bitcast_fusion.1
  1.3 0.7 convert_element_type.24
  2.0 0.7 convert_element_type.21
  2.6 0.7 %convert_bitcast_fusion = f32[6,16]{1,0:T(8,128)S(1)} fusion(s32[16,6]{0,1:T(8,128)} %param.17), kind=kLoop, calls=%fused_computation.1 | loop fusion | flops 96 | bytes 768 | tf_op jit(solution)/shard_map/convert_element_type | solution.py:448
  3.3 0.1 convert_element_type.27
  3.4 1.0 %pad_maximum_fusion.points_ref = f32[7,8,1024]{2,1,0:T(8,128)S(1)} fusion(f32[1,8,1024]{2,1,0:T(8,128)} %bitcast.11, f32[3,8,1024]{2,1,0:T(8,128)} %bitcast.9, f32[3,8,1024]{2,1,0:T(8,128)} %bitcast.10), kind=kLoop, calls=%fused_computation | loop fusion | flops 114688 | bytes 458752 | tf_op jit(solution)/shard_map/concatenate | solution.py:434
  4.4 0.7 %concatenate.6.given_ref = f32[160]{0:T(256)S(1)} concatenate(f32[16]{0:T(128)S(1)} %convert_element_type.21, f32[16]{0:T(128)S(1)} %convert_bitcast_fusion.1, f32[16]{0:T(128)S(1)} %convert_element_type.24, f32[96]{0:T(128)S(1)} %convert_element_type.27, f32[16]{0:T(128)} %param.18), dimensions={0} | concatenate | bytes 1280 | tf_op jit(solution)/shard_map/concatenate | solution.py:448
  5.1 0.0 copy-start.5
  5.1 0.9 %copy-done.5 = bf16[8,16,512]{2,1,0:T(8,128)(2,1)S(1)} copy-done((bf16[8,16,512]{2,1,0:T(8,128)(2,1)S(1)}, bf16[8,16,512]{2,1,0:T(8,128)(2,1)}, u32[]{:S(2)}) %copy-start.5) | copy-done | bytes 131096
  6.0 3.2 %project.2 = (bf16[8,2,64,1024]{3,2,1,0:T(8,128)(2,1)S(1)}, f32[2,8,64,128]{3,2,1,0:T(8,128)S(1)}, bf16[16,16,640]{2,1,0:T(8,128)(2,1)}) custom-call(s32[1]{0:T(128)} %bitcast.place_ref, f32[160]{0:T(256)S(1)} %concatenate.6.given_ref, f32[7,8,1024]{2,1,0:T(8,128)S(1)} %pad_maximum_fusion.points_ref, bf16[8,16,512]{2,1,0:T(8,128)(2,1)S(1)} %copy-done.5), custom_call_target="tpu_custom_call" | custom-call | flops 536870912 | bytes 1048576 | tf_op jit(solution)/shard_map/project/pallas_call | solution.py:208
  9.2 7.4 %all-to-all-start = ((bf16[16,16,640]{2,1,0:T(8,128)(2,1)}), bf16[16,16,640]{2,1,0:T(8,128)(2,1)S(1)}, u32[]{:S(2)}, u32[]{:S(2)}) async-start(bf16[16,16,640]{2,1,0:T(8,128)(2,1)} %get-tuple-element.11), calls=%async_computation | async-start | bytes 655360 | tf_op jit(solution)/shard_map/all_to_all | solution.py:475
  16.6 1.6 %collective-permute-start = (f32[7,8,1024]{2,1,0:T(8,128)S(1)}, f32[7,8,1024]{2,1,0:T(8,128)S(1)}, u32[]{:S(2)}, u32[]{:S(2)}) collective-permute-start(f32[7,8,1024]{2,1,0:T(8,128)S(1)} %pad_maximum_fusion.points_ref), channel_id=1, source_target_pairs={{1,0},{0,1},{3,2},{2,3},{5,4},{4,5},{7,6},{6,7},{9,8},{8,9},{11,10... | collective-permute-start | bytes 688136 | tf_op jit(solution)/shard_map/ppermute | solution.py:445
  18.1 6.4 %collective-permute-done.points_ref = f32[7,8,1024]{2,1,0:T(8,128)S(1)} collective-permute-done((f32[7,8,1024]{2,1,0:T(8,128)S(1)}, f32[7,8,1024]{2,1,0:T(8,128)S(1)}, u32[]{:S(2)}, u32[]{:S(2)}) %collective-permute-start) | collective-permute-done | bytes 229408 | tf_op jit(solution)/shard_map/ppermute | solution.py:445
  24.5 0.0 copy-start.6
  24.5 0.9 %copy-done.6 = bf16[8,16,512]{2,1,0:T(8,128)(2,1)S(1)} copy-done((bf16[8,16,512]{2,1,0:T(8,128)(2,1)S(1)}, bf16[8,16,512]{2,1,0:T(8,128)(2,1)}, u32[]{:S(2)}) %copy-start.6) | copy-done | bytes 131096
  25.4 2.4 %project.3 = (bf16[8,2,64,1024]{3,2,1,0:T(8,128)(2,1)S(1)}, f32[2,8,64,128]{3,2,1,0:T(8,128)S(1)}, bf16[16,16,512]{2,1,0:T(8,128)(2,1)S(1)}) custom-call(s32[1]{0:T(128)} %bitcast.place_ref, f32[160]{0:T(256)S(1)} %concatenate.6.given_ref, f32[7,8,1024]{2,1,0:T(8,128)S(1)} %collective-permute-done.points_ref, bf16[8,16,512]{2,1,0:T(8,128)(2,1)S(1)} %copy-done.6), custom_call_target="tpu_custom_call" | custom-call | flops 536870912 | bytes 1048576 | tf_op jit(solution)/shard_map/project/pallas_call | solution.py:208
  27.8 0.0 copy-start
  27.8 1.3 %copy-done = bf16[8,2,64,1024]{3,2,1,0:T(8,128)(2,1)} copy-done((bf16[8,2,64,1024]{3,2,1,0:T(8,128)(2,1)}, bf16[8,2,64,1024]{3,2,1,0:T(8,128)(2,1)S(1)}, u32[]{:S(2)}) %copy-start) | copy-done | bytes 2097176
  29.1 0.0 copy-start.2
  29.1 0.7 %copy-done.2 = bf16[16,16,512]{2,1,0:T(8,128)(2,1)} copy-done((bf16[16,16,512]{2,1,0:T(8,128)(2,1)}, bf16[16,16,512]{2,1,0:T(8,128)(2,1)S(1)}, u32[]{:S(2)}) %copy-start.2) | copy-done | bytes 262168
  29.8 0.0 copy-start.3
  29.8 0.0 copy-start.4
  29.8 0.0 all-to-all-done.arrived_ref.refs_0_
  29.8 5.9 %all-to-all-start.1 = ((bf16[16,16,512]{2,1,0:T(8,128)(2,1)}), bf16[16,16,512]{2,1,0:T(8,128)(2,1)}, u32[]{:S(2)}, u32[]{:S(2)}) async-start(bf16[16,16,512]{2,1,0:T(8,128)(2,1)} %copy-done.2), calls=%async_computation.1 | async-start | bytes 524288 | tf_op jit(solution)/shard_map/all_to_all | solution.py:475
  35.8 2.3 %plan.1 = (bf16[256,256]{1,0:T(8,128)(2,1)S(1)}, bf16[256,256]{1,0:T(8,128)(2,1)S(1)}, f32[256,128]{1,0:T(8,128)S(1)}) custom-call(bf16[16,16,640]{2,1,0:T(8,128)(2,1)S(1)} %all-to-all-done.arrived_ref.refs_0_), custom_call_target="tpu_custom_call" | custom-call | flops 1048576 | bytes 262144 | tf_op jit(solution)/shard_map/plan/pallas_call | solution.py:265
  38.0 0.0 copy-start.7
  38.0 0.6 copy-done.7
  38.7 0.0 copy-start.9
  38.7 0.7 copy-done.9
  39.4 0.0 copy-start.11
  39.4 0.6 copy-done.11
  40.0 5.8 %all-to-all-done.1.refs_1_ = bf16[16,16,512]{2,1,0:T(8,128)(2,1)} async-done(((bf16[16,16,512]{2,1,0:T(8,128)(2,1)}), bf16[16,16,512]{2,1,0:T(8,128)(2,1)}, u32[]{:S(2)}, u32[]{:S(2)}) %all-to-all-start.1) | async-done | bytes 262176 | tf_op jit(solution)/shard_map/all_to_all | solution.py:475
  45.9 0.0 copy-start.1
  45.9 0.0 copy-start.8
  45.9 1.1 %copy-done.8 = bf16[256,256]{1,0:T(8,128)(2,1)S(1)} copy-done((bf16[256,256]{1,0:T(8,128)(2,1)S(1)}, bf16[256,256]{1,0:T(8,128)(2,1)}, u32[]{:S(2)}) %copy-start.8) | copy-done | bytes 131096
  46.9 0.0 copy-start.10
  46.9 0.9 %copy-done.10 = bf16[256,256]{1,0:T(8,128)(2,1)S(1)} copy-done((bf16[256,256]{1,0:T(8,128)(2,1)S(1)}, bf16[256,256]{1,0:T(8,128)(2,1)}, u32[]{:S(2)}) %copy-start.10) | copy-done | bytes 131096
  47.8 0.0 copy-start.12
  47.8 0.9 %copy-done.12 = f32[256,128]{1,0:T(8,128)S(1)} copy-done((f32[256,128]{1,0:T(8,128)S(1)}, f32[256,128]{1,0:T(8,128)}, u32[]{:S(2)}) %copy-start.12) | copy-done | bytes 131096
  48.7 1.8 %coarse_stage.1 = bf16[8,32,1024]{2,1,0:T(8,128)(2,1)S(1)} custom-call(s32[1]{0:T(128)} %bitcast.1.half_ref, bf16[256,256]{1,0:T(8,128)(2,1)S(1)} %copy-done.8, bf16[256,256]{1,0:T(8,128)(2,1)S(1)} %copy-done.10, f32[256,128]{1,0:T(8,128)S(1)} %copy-done.12, bf16[16,16,640]{2,1,0:T(8,128)(2,1)S(1)} %all-to-all-done.arrived_ref.refs_0_, ...), custom_call_target="tpu_custom_call" | custom-call | flops 536870912 | bytes 1048576 | tf_op jit(solution)/shard_map/coarse_stage/pallas_call | solution.py:326
  50.6 11.3 %all_to_all.15.back_ref = bf16[8,32,1024]{2,1,0:T(8,128)(2,1)S(1)} all-to-all(bf16[8,32,1024]{2,1,0:T(8,128)(2,1)S(1)} %coarse_stage.1), channel_id=1, replica_groups={{0,2,4,6,8,10,12,14},{16,18,20,22,24,26,28,30},{1,3,5,7,9,11,13,15},{17..., dimensions={0} | all-to-all | bytes 1048576 | tf_op jit(solution)/shard_map/all_to_all | solution.py:479
  61.9 0.0 copy-done.3
  61.9 0.0 copy-done.4
  61.9 0.0 copy-done.1
  61.9 4.3 %restrict.1 = (bf16[16,16,512]{2,1,0:T(8,128)(2,1)}, bf16[8,16,512]{2,1,0:T(8,128)(2,1)}) custom-call(s32[1]{0:T(128)} %bitcast.place_ref, s32[16]{0:T(128)S(1)} %copy-done.3, f32[8]{0:T(128)S(1)} %copy-done.4, bf16[8,32,1024]{2,1,0:T(8,128)(2,1)S(1)} %all_to_all.15.back_ref, bf16[8,2,64,1024]{3,2,1,0:T(8,128)(2,1)S(1)} %get-tuple-element.16.refs_0_, ...), custom_call_target="tpu_custom_call" | custom-call | flops 1073741824 | bytes 2097152 | tf_op jit(solution)/shard_map/restrict/pallas_call | solution.py:392
Async XLA Ops:
  5.1 0.9 %copy-start.5 = (bf16[8,16,512]{2,1,0:T(8,128)(2,1)S(1)}, bf16[8,16,512]{2,1,0:T(8,128)(2,1)}, u32[]{:S(2)}) copy-start(bf16[8,16,512]{2,1,0:T(8,128)(2,1)} %field_ref.3) | copy-start | bytes 393220
  9.2 20.6 %all-to-all-start = ((bf16[16,16,640]{2,1,0:T(8,128)(2,1)}), bf16[16,16,640]{2,1,0:T(8,128)(2,1)S(1)}, u32[]{:S(2)}, u32[]{:S(2)}) async-start(bf16[16,16,640]{2,1,0:T(8,128)(2,1)} %get-tuple-element.11), calls=%async_computation | async-start | bytes 655360 | tf_op jit(solution)/shard_map/all_to_all | solution.py:475
  16.6 7.9 %collective-permute-start = (f32[7,8,1024]{2,1,0:T(8,128)S(1)}, f32[7,8,1024]{2,1,0:T(8,128)S(1)}, u32[]{:S(2)}, u32[]{:S(2)}) collective-permute-start(f32[7,8,1024]{2,1,0:T(8,128)S(1)} %pad_maximum_fusion.points_ref), channel_id=1, source_target_pairs={{1,0},{0,1},{3,2},{2,3},{5,4},{4,5},{7,6},{6,7},{9,8},{8,9},{11,10... | collective-permute-start | bytes 688136 | tf_op jit(solution)/shard_map/ppermute | solution.py:445
  24.5 0.9 %copy-start.6 = (bf16[8,16,512]{2,1,0:T(8,128)(2,1)S(1)}, bf16[8,16,512]{2,1,0:T(8,128)(2,1)}, u32[]{:S(2)}) copy-start(bf16[8,16,512]{2,1,0:T(8,128)(2,1)} %field_ref.3) | copy-start | bytes 393220
  27.8 1.3 %copy-start = (bf16[8,2,64,1024]{3,2,1,0:T(8,128)(2,1)}, bf16[8,2,64,1024]{3,2,1,0:T(8,128)(2,1)S(1)}, u32[]{:S(2)}) copy-start(bf16[8,2,64,1024]{3,2,1,0:T(8,128)(2,1)S(1)} %get-tuple-element.17.refs_1_) | copy-start | bytes 6291460
  29.1 0.7 %copy-start.2 = (bf16[16,16,512]{2,1,0:T(8,128)(2,1)}, bf16[16,16,512]{2,1,0:T(8,128)(2,1)S(1)}, u32[]{:S(2)}) copy-start(bf16[16,16,512]{2,1,0:T(8,128)(2,1)S(1)} %get-tuple-element.15) | copy-start | bytes 786436
  29.8 32.1 %copy-start.3 = (s32[16]{0:T(128)S(1)}, s32[16]{0:T(128)}, u32[]{:S(2)}) copy-start(s32[16]{0:T(128)} %fine_ids.1) | copy-start | bytes 196
  29.8 32.1 %copy-start.4 = (f32[8]{0:T(128)S(1)}, f32[8]{0:T(128)}, u32[]{:S(2)}) copy-start(f32[8]{0:T(128)} %inverse_ref.1) | copy-start | bytes 100
  29.8 16.0 %all-to-all-start.1 = ((bf16[16,16,512]{2,1,0:T(8,128)(2,1)}), bf16[16,16,512]{2,1,0:T(8,128)(2,1)}, u32[]{:S(2)}, u32[]{:S(2)}) async-start(bf16[16,16,512]{2,1,0:T(8,128)(2,1)} %copy-done.2), calls=%async_computation.1 | async-start | bytes 524288 | tf_op jit(solution)/shard_map/all_to_all | solution.py:475
  38.0 0.7 copy-start.7
  38.7 0.7 copy-start.9
  39.4 0.6 copy-start.11
  45.9 16.0 %copy-start.1 = (bf16[8,2,64,1024]{3,2,1,0:T(8,128)(2,1)S(1)}, bf16[8,2,64,1024]{3,2,1,0:T(8,128)(2,1)}, u32[]{:S(2)}) copy-start(bf16[8,2,64,1024]{3,2,1,0:T(8,128)(2,1)} %copy-done) | copy-start | bytes 6291460
  45.9 1.1 %copy-start.8 = (bf16[256,256]{1,0:T(8,128)(2,1)S(1)}, bf16[256,256]{1,0:T(8,128)(2,1)}, u32[]{:S(2)}) copy-start(bf16[256,256]{1,0:T(8,128)(2,1)} %copy-done.7) | copy-start | bytes 393220
  46.9 0.9 %copy-start.10 = (bf16[256,256]{1,0:T(8,128)(2,1)S(1)}, bf16[256,256]{1,0:T(8,128)(2,1)}, u32[]{:S(2)}) copy-start(bf16[256,256]{1,0:T(8,128)(2,1)} %copy-done.9) | copy-start | bytes 393220
  47.8 0.9 %copy-start.12 = (f32[256,128]{1,0:T(8,128)S(1)}, f32[256,128]{1,0:T(8,128)}, u32[]{:S(2)}) copy-start(f32[256,128]{1,0:T(8,128)} %copy-done.11) | copy-start | bytes 393220

commit v7 on v5

--- a/solution.py
+++ b/solution.py
@@ -56,22 +56,19 @@
 def transfer(coefs, table_ref, heads, pair, row, source):
     block = coefs.shape[0]
     quad = table_ref.shape[3]
-    side = lax.broadcasted_iota(jnp.int32, (block, LANES), 1) < NB * NB
-    keep = [
-        jnp.where(side, 1.0, 0.0).astype(jnp.bfloat16),
-        jnp.where(side, 0.0, 1.0).astype(jnp.bfloat16),
-    ]
-    masked = jnp.concatenate(
-        [coefs[:, lanes(a // 2)] * keep[a % 2] for a in range(NB)], axis=0
-    )
+    pieces = []
+    for lane in range(coefs.shape[1] // LANES):
+        piece = coefs[:, lanes(lane)]
+        pieces += [piece, pltpu.roll(piece, NB * NB, axis=1)]
+    packed = jnp.concatenate(pieces, axis=0).astype(jnp.bfloat16)[:, : NB * NB]
     total = None
     for start in range(0, quad, 2 * LANES):
         columns = slice(start, start + 2 * LANES)
         inward = table_ref[pair, source, :, columns]
         outward = table_ref[pair, 1 - source, :, columns]
         inner = lax.dot_general(
-            masked,
-            jnp.concatenate([inward, inward], axis=0),
+            packed,
+            inward,
             NN,
             preferred_element_type=jnp.float32,
         )
@@ -90,15 +87,13 @@
             outer.append(jnp.concatenate([p for piece in pieces for p in piece], axis=0))
         part = lax.dot_general(
             jnp.concatenate(outer, axis=1).astype(jnp.bfloat16),
-            jnp.concatenate([outward, outward], axis=0),
+            outward,
             NT,
             preferred_element_type=jnp.float32,
         )
         total = part if total is None else total + part
-    return [
-        jnp.where(side, total[a * block : (a + 1) * block], total[(a + 1) * block : (a + 2) * block])
-        for a in range(0, NB, 2)
-    ]
+    parts = [total[a * block : (a + 1) * block] for a in range(NB)]
+    return [jnp.concatenate(parts[a : a + 2], axis=1) for a in range(0, NB, 2)]
 
 
 def facts(owner_ref, coarse_ref, faces_ref, inverse_ref, rows, pair_at):
@@ -159,7 +154,7 @@
 
     for pair in range(pairs):
         fill_table(table_ref, legs, pair)
-        coefs = field_ref[fine_ref[pair_at(shift, pair)]]
+        coefs = field_ref[fine_ref[pair_at(shift, pair)]].astype(jnp.float32)
         parts = transfer(coefs, table_ref, heads, pair, pair * NB, 0)
         for lane in range(across):
             sums[lane, pl.ds(pair, block, stride=pairs), :] = parts[lane]
@@ -302,7 +297,7 @@
 
     def picked(target):
         parts = [rows[lane, pl.ds(target, block, stride=targets), :] for lane in range(across)]
-        return jnp.concatenate(parts, axis=1).astype(jnp.bfloat16)
+        return jnp.concatenate(parts, axis=1)
 
     sums[...] = jnp.zeros_like(sums)
     for shift in range(shifts):
@@ -326,7 +321,7 @@
         else:
             pl.loop(0, pairs)(turn)
     for element in range(elements):
-        coarse_ref[element] = picked(element)
+        coarse_ref[element] = picked(element).astype(jnp.bfloat16)
     for fine in range(fine_count):
         fine_ref[fine] = (inverse_ref[fine] * sums[fine]).astype(jnp.bfloat16)
 

time: 53.2 us -> 53.7 us (level)
  Pallas kernels: 10.3 us -> 10.9 us
  transfers between devices with their start and end apart: 1 -> 1, of which waited for: 1 -> 1; matrix products, arithmetic and copies ran while one was open for 0% -> 0% of each run, Pallas kernels for 4% -> 5%
where the time goes in v7:
time: 53.7 us; the launch traced here: 53.4 us
  blocking collectives  34.6 us (64%)
  Pallas kernels  10.9 us (20%)
  starting transfers between devices  3 us (6%)
  waiting for transfers between devices  1.6 us (3%)
  local copies, waits for them, and re-layouts  1.59 us (3%)
  other arithmetic  1.05 us (2%)
  between operations  0.74 us (1%)
    all_to_all x1, blocking collectives, shards(): lax.all_to_all(smooth, 'wide', split_axis=0, concat_axis=0, tiled=True)  17.5 us
    all_to_all x1, blocking collectives, shards(): lax.all_to_all(outs[-1], 'wide', split_axis=0, concat_axis=0, tiled=True)  17.1 us
    pallas_call x2, Pallas kernels, project(): pl.pallas_call(functools.partial(project_kernel, shift, shifts), in_specs...  5.09 us
    pallas_call x1, Pallas kernels, restrict(): pl.pallas_call(functools.partial(restrict_kernel, len(tables)), in_specs=...  4.58 us
    ppermute x1, starting transfers between devices, shards(): points.append(lax.ppermute(own, 'field', perm))  3 us
    ppermute x1, waiting for transfers between devices, shards(): points.append(lax.ppermute(own, 'field', perm))  1.6 us
    unnamed x18, local copies, waits for them, and re-layouts  1.59 us
    pallas_call x1, Pallas kernels, coarse_stage(): pl.pallas_call(functools.partial(coarse_kernel, faces, elements), in_spec...  1.19 us
  transfers between devices with their start and end apart: 1, of which 1 were waited for; matrix products, arithmetic and copies ran while one was open for 0% of the time, Pallas kernels for 5%

profile of v7, /device:TPU:0, one launch (start us, length us, event | category | flops | bytes accessed | tf_op | source)
XLA Modules:
  0.0 53.4 jit_solution(2613646728478782318)
XLA Ops:
  0.6 0.0 copy-start.4
  0.6 0.0 copy-start.8
  0.7 0.0 copy-start.5
  0.7 0.0 copy-start.7
  0.7 0.0 copy-start.6
  0.7 1.1 %pad_maximum_fusion.refs_0_ = f32[7,8,1024]{2,1,0:T(8,128)S(1)} fusion(f32[1,8,1024]{2,1,0:T(8,128)} %bitcast.10, f32[3,8,1024]{2,1,0:T(8,128)} %bitcast.8, f32[3,8,1024]{2,1,0:T(8,128)} %bitcast.9), kind=kLoop, calls=%fused_computation | loop fusion | flops 114688 | bytes 458752 | tf_op jit(solution)/shard_map/concatenate | solution.py:376
  1.7 3.0 %collective-permute-start = (f32[7,8,1024]{2,1,0:T(8,128)S(1)}, f32[7,8,1024]{2,1,0:T(8,128)S(1)}, u32[]{:S(2)}, u32[]{:S(2)}) collective-permute-start(f32[7,8,1024]{2,1,0:T(8,128)S(1)} %pad_maximum_fusion.refs_0_), channel_id=1, source_target_pairs={{1,0},{0,1},{3,2},{2,3},{5,4},{4,5},{7,6},{6,7},{9,8},{8,9},{11,10... | collective-permute-start | bytes 688136 | tf_op jit(solution)/shard_map/ppermute | solution.py:387
  4.7 0.0 copy-start
  4.7 0.7 %copy-done = s32[16]{0:T(128)S(1)} copy-done((s32[16]{0:T(128)S(1)}, s32[16]{0:T(128)}, u32[]{:S(2)}) %copy-start) | copy-done | bytes 88
  5.4 0.0 copy-start.3
  5.4 0.9 %copy-done.3 = bf16[8,16,512]{2,1,0:T(8,128)(2,1)S(1)} copy-done((bf16[8,16,512]{2,1,0:T(8,128)(2,1)S(1)}, bf16[8,16,512]{2,1,0:T(8,128)(2,1)}, u32[]{:S(2)}) %copy-start.3) | copy-done | bytes 131096
  6.3 2.4 %project.2 = (bf16[8,2,64,1024]{3,2,1,0:T(8,128)(2,1)S(1)}, f32[2,8,64,128]{3,2,1,0:T(8,128)S(1)}, f32[4,128,128]{2,1,0:T(8,128)S(1)}) custom-call(s32[1]{0:T(128)} %bitcast.place_ref, s32[16]{0:T(128)S(1)} %copy-done, f32[7,8,1024]{2,1,0:T(8,128)S(1)} %pad_maximum_fusion.refs_0_, bf16[8,16,512]{2,1,0:T(8,128)(2,1)S(1)} %copy-done.3), custom_call_target="tpu_custom_call" | custom-call | flops 536870912 | bytes 1048576 | tf_op jit(solution)/shard_map/project/pallas_call | solution.py:197
  8.7 1.6 %collective-permute-done.refs_4_ = f32[7,8,1024]{2,1,0:T(8,128)S(1)} collective-permute-done((f32[7,8,1024]{2,1,0:T(8,128)S(1)}, f32[7,8,1024]{2,1,0:T(8,128)S(1)}, u32[]{:S(2)}, u32[]{:S(2)}) %collective-permute-start) | collective-permute-done | bytes 229408 | tf_op jit(solution)/shard_map/ppermute | solution.py:387
  10.3 0.0 copy-done.4
  10.3 0.0 copy-done.8
  10.4 0.0 copy-done.5
  10.4 0.0 copy-done.7
  10.4 0.0 copy-done.6
  10.4 0.0 copy-start.1
  10.4 0.0 copy-start.2
  10.4 2.7 %project.3 = (bf16[8,2,64,1024]{3,2,1,0:T(8,128)(2,1)S(1)}, f32[2,8,64,128]{3,2,1,0:T(8,128)S(1)}, bf16[16,16,640]{2,1,0:T(8,128)(2,1)S(1)}) custom-call(s32[1]{0:T(128)} %bitcast.place_ref, s32[16]{0:T(128)S(1)} %copy-done, s32[1,16]{1,0:T(1,128)S(1)} %bitcast.7, s32[16]{0:T(128)S(1)} %copy-done.7, s32[6,16]{1,0:T(8,128)S(1)} %bitcast.6, f32[16]{0:T(128)S(1)} %copy-done.8, ...), custom_call_target="tpu_custom_call" | custom-call | flops 536870912 | bytes 1048576 | tf_op jit(solution)/shard_map/project/pallas_call | solution.py:197
  13.1 17.1 %all_to_all.10.arrived_ref = bf16[16,16,640]{2,1,0:T(8,128)(2,1)S(1)} all-to-all(bf16[16,16,640]{2,1,0:T(8,128)(2,1)S(1)} %get-tuple-element.9), channel_id=1, replica_groups=mesh['wide'=16,'field'=2] {'wide'}, dimensions={0} | all-to-all | bytes 655360 | tf_op jit(solution)/shard_map/all_to_all | solution.py:398
  30.2 1.2 %coarse_stage.1 = bf16[16,32,512]{2,1,0:T(8,128)(2,1)S(1)} custom-call(bf16[16,16,640]{2,1,0:T(8,128)(2,1)S(1)} %all_to_all.10.arrived_ref), custom_call_target="tpu_custom_call" | custom-call | flops 268435456 | bytes 524288 | tf_op jit(solution)/shard_map/coarse_stage/pallas_call | solution.py:264
  31.4 17.5 %all_to_all.11.back_ref = bf16[16,32,512]{2,1,0:T(8,128)(2,1)S(1)} all-to-all(bf16[16,32,512]{2,1,0:T(8,128)(2,1)S(1)} %coarse_stage.1), channel_id=1, replica_groups=mesh['wide'=16,'field'=2] {'wide'}, dimensions={0} | all-to-all | bytes 1048576 | tf_op jit(solution)/shard_map/all_to_all | solution.py:400
  48.9 0.0 copy-done.1
  48.9 0.0 copy-done.2
  48.9 4.6 %restrict.1 = (bf16[16,16,512]{2,1,0:T(8,128)(2,1)}, bf16[8,16,512]{2,1,0:T(8,128)(2,1)}) custom-call(s32[1]{0:T(128)} %bitcast.place_ref, s32[16]{0:T(128)S(1)} %copy-done.1, f32[8]{0:T(128)S(1)} %copy-done.2, bf16[16,32,512]{2,1,0:T(8,128)(2,1)S(1)} %all_to_all.11.back_ref, bf16[8,2,64,1024]{3,2,1,0:T(8,128)(2,1)S(1)} %get-tuple-element.10.refs_0_, ...), custom_call_target="tpu_custom_call" | custom-call | flops 1073741824 | bytes 2097152 | tf_op jit(solution)/shard_map/restrict/pallas_call | solution.py:334
Async XLA Ops:
  0.6 9.7 %copy-start.4 = (bf16[8,16,512]{2,1,0:T(8,128)(2,1)S(1)}, bf16[8,16,512]{2,1,0:T(8,128)(2,1)}, u32[]{:S(2)}) copy-start(bf16[8,16,512]{2,1,0:T(8,128)(2,1)} %refs_5_.1) | copy-start | bytes 393220
  0.6 9.7 %copy-start.8 = (f32[16]{0:T(128)S(1)}, f32[16]{0:T(128)}, u32[]{:S(2)}) copy-start(f32[16]{0:T(128)} %refs_3_.1) | copy-start | bytes 196
  0.7 9.7 %copy-start.5 = (s32[16,6]{0,1:T(8,128)S(1)}, s32[16,6]{0,1:T(8,128)}, u32[]{:S(2)}) copy-start(s32[16,6]{0,1:T(8,128)} %param.17) | copy-start | bytes 1156
  0.7 9.7 %copy-start.7 = (s32[16]{0:T(128)S(1)}, s32[16]{0:T(128)}, u32[]{:S(2)}) copy-start(s32[16]{0:T(128)} %refs_1_.3) | copy-start | bytes 196
  0.7 9.7 %copy-start.6 = (s32[16,1]{0,1:T(1,128)S(1)}, s32[16,1]{0,1:T(1,128)}, u32[]{:S(2)}) copy-start(s32[16,1]{0,1:T(1,128)} %param.15) | copy-start | bytes 196
  1.7 8.6 %collective-permute-start = (f32[7,8,1024]{2,1,0:T(8,128)S(1)}, f32[7,8,1024]{2,1,0:T(8,128)S(1)}, u32[]{:S(2)}, u32[]{:S(2)}) collective-permute-start(f32[7,8,1024]{2,1,0:T(8,128)S(1)} %pad_maximum_fusion.refs_0_), channel_id=1, source_target_pairs={{1,0},{0,1},{3,2},{2,3},{5,4},{4,5},{7,6},{6,7},{9,8},{8,9},{11,10... | collective-permute-start | bytes 688136 | tf_op jit(solution)/shard_map/ppermute | solution.py:387
  4.7 0.7 %copy-start = (s32[16]{0:T(128)S(1)}, s32[16]{0:T(128)}, u32[]{:S(2)}) copy-start(s32[16]{0:T(128)} %fine_ids.1) | copy-start | bytes 196
  5.4 0.9 %copy-start.3 = (bf16[8,16,512]{2,1,0:T(8,128)(2,1)S(1)}, bf16[8,16,512]{2,1,0:T(8,128)(2,1)}, u32[]{:S(2)}) copy-start(bf16[8,16,512]{2,1,0:T(8,128)(2,1)} %refs_5_.1) | copy-start | bytes 393220
  10.4 38.5 %copy-start.1 = (s32[16]{0:T(128)S(1)}, s32[16]{0:T(128)}, u32[]{:S(2)}) copy-start(s32[16]{0:T(128)} %fine_ids.1) | copy-start | bytes 196
  10.4 38.5 %copy-start.2 = (f32[8]{0:T(128)S(1)}, f32[8]{0:T(128)}, u32[]{:S(2)}) copy-start(f32[8]{0:T(128)} %inverse_ref.1) | copy-start | bytes 100

commit v8 on v5

--- a/solution.py
+++ b/solution.py
@@ -78,15 +78,17 @@
         outer = []
         for half in range(2):
             lane = start // LANES + half
+            enter = [spread(heads, source, lane, row + a) for a in range(NB)]
+            leave = [spread(heads, 1 - source, lane, row + a) for a in range(NB)]
             pieces = [[] for _ in range(NB)]
             for low in range(0, block, NB):
                 value = None
                 for a in range(NB):
                     part = inner[a * block + low : a * block + low + NB, lanes(half)]
-                    part = part * spread(heads, source, lane, row + a)
+                    part = part * enter[a]
                     value = part if value is None else value + part
                 for a in range(NB):
-                    pieces[a].append(value * spread(heads, 1 - source, lane, row + a))
+                    pieces[a].append(value * leave[a])
             outer.append(jnp.concatenate([p for piece in pieces for p in piece], axis=0))
         part = lax.dot_general(
             jnp.concatenate(outer, axis=1).astype(jnp.bfloat16),

time: 53.2 us -> 53.2 us (level)
  no operation moved by 1% of the time
where the time goes in v8:
time: 53.2 us; the launch traced here: 53 us
  blocking collectives  34.6 us (65%)
  Pallas kernels  10.3 us (19%)
  starting transfers between devices  3 us (6%)
  waiting for transfers between devices  1.71 us (3%)
  local copies, waits for them, and re-layouts  1.59 us (3%)
  other arithmetic  1.05 us (2%)
  between operations  0.74 us (1%)
    all_to_all x1, blocking collectives, shards(): lax.all_to_all(smooth, 'wide', split_axis=0, concat_axis=0, tiled=True)  17.5 us
    all_to_all x1, blocking collectives, shards(): lax.all_to_all(outs[-1], 'wide', split_axis=0, concat_axis=0, tiled=True)  17.1 us
    pallas_call x2, Pallas kernels, project(): pl.pallas_call(functools.partial(project_kernel, shift, shifts), in_specs...  4.84 us
    pallas_call x1, Pallas kernels, restrict(): pl.pallas_call(functools.partial(restrict_kernel, len(tables)), in_specs=...  4.28 us
    ppermute x1, starting transfers between devices, shards(): points.append(lax.ppermute(own, 'field', perm))  3 us
    ppermute x1, waiting for transfers between devices, shards(): points.append(lax.ppermute(own, 'field', perm))  1.71 us
    unnamed x18, local copies, waits for them, and re-layouts  1.59 us
    pallas_call x1, Pallas kernels, coarse_stage(): pl.pallas_call(functools.partial(coarse_kernel, faces, elements), in_spec...  1.2 us
  transfers between devices with their start and end apart: 1, of which 1 were waited for; matrix products, arithmetic and copies ran while one was open for 0% of the time, Pallas kernels for 4%

profile of v8, /device:TPU:0, one launch (start us, length us, event | category | flops | bytes accessed | tf_op | source)
XLA Modules:
  0.0 53.0 jit_solution(6925923053931829976)
XLA Ops:
  0.6 0.0 copy-start.4
  0.6 0.0 copy-start.8
  0.7 0.0 copy-start.5
  0.7 0.0 copy-start.7
  0.7 0.0 copy-start.6
  0.7 1.1 %pad_maximum_fusion.refs_0_ = f32[7,8,1024]{2,1,0:T(8,128)S(1)} fusion(f32[1,8,1024]{2,1,0:T(8,128)} %bitcast.10, f32[3,8,1024]{2,1,0:T(8,128)} %bitcast.8, f32[3,8,1024]{2,1,0:T(8,128)} %bitcast.9), kind=kLoop, calls=%fused_computation | loop fusion | flops 114688 | bytes 458752 | tf_op jit(solution)/shard_map/concatenate | solution.py:383
  1.7 3.0 %collective-permute-start = (f32[7,8,1024]{2,1,0:T(8,128)S(1)}, f32[7,8,1024]{2,1,0:T(8,128)S(1)}, u32[]{:S(2)}, u32[]{:S(2)}) collective-permute-start(f32[7,8,1024]{2,1,0:T(8,128)S(1)} %pad_maximum_fusion.refs_0_), channel_id=1, source_target_pairs={{1,0},{0,1},{3,2},{2,3},{5,4},{4,5},{7,6},{6,7},{9,8},{8,9},{11,10... | collective-permute-start | bytes 688136 | tf_op jit(solution)/shard_map/ppermute | solution.py:394
  4.7 0.0 copy-start
  4.7 0.7 %copy-done = s32[16]{0:T(128)S(1)} copy-done((s32[16]{0:T(128)S(1)}, s32[16]{0:T(128)}, u32[]{:S(2)}) %copy-start) | copy-done | bytes 88
  5.4 0.0 copy-start.3
  5.4 0.9 %copy-done.3 = bf16[8,16,512]{2,1,0:T(8,128)(2,1)S(1)} copy-done((bf16[8,16,512]{2,1,0:T(8,128)(2,1)S(1)}, bf16[8,16,512]{2,1,0:T(8,128)(2,1)}, u32[]{:S(2)}) %copy-start.3) | copy-done | bytes 131096
  6.3 2.3 %project.2 = (bf16[8,2,64,1024]{3,2,1,0:T(8,128)(2,1)S(1)}, f32[2,8,64,128]{3,2,1,0:T(8,128)S(1)}, f32[4,128,128]{2,1,0:T(8,128)S(1)}) custom-call(s32[1]{0:T(128)} %bitcast.place_ref, s32[16]{0:T(128)S(1)} %copy-done, f32[7,8,1024]{2,1,0:T(8,128)S(1)} %pad_maximum_fusion.refs_0_, bf16[8,16,512]{2,1,0:T(8,128)(2,1)S(1)} %copy-done.3), custom_call_target="tpu_custom_call" | custom-call | flops 536870912 | bytes 1048576 | tf_op jit(solution)/shard_map/project/pallas_call | solution.py:204
  8.6 1.7 %collective-permute-done.refs_4_ = f32[7,8,1024]{2,1,0:T(8,128)S(1)} collective-permute-done((f32[7,8,1024]{2,1,0:T(8,128)S(1)}, f32[7,8,1024]{2,1,0:T(8,128)S(1)}, u32[]{:S(2)}, u32[]{:S(2)}) %collective-permute-start) | collective-permute-done | bytes 229408 | tf_op jit(solution)/shard_map/ppermute | solution.py:394
  10.3 0.0 copy-done.4
  10.3 0.0 copy-done.8
  10.4 0.0 copy-done.5
  10.4 0.0 copy-done.7
  10.4 0.0 copy-done.6
  10.4 0.0 copy-start.1
  10.4 0.0 copy-start.2
  10.4 2.5 %project.3 = (bf16[8,2,64,1024]{3,2,1,0:T(8,128)(2,1)S(1)}, f32[2,8,64,128]{3,2,1,0:T(8,128)S(1)}, bf16[16,16,640]{2,1,0:T(8,128)(2,1)S(1)}) custom-call(s32[1]{0:T(128)} %bitcast.place_ref, s32[16]{0:T(128)S(1)} %copy-done, s32[1,16]{1,0:T(1,128)S(1)} %bitcast.7, s32[16]{0:T(128)S(1)} %copy-done.7, s32[6,16]{1,0:T(8,128)S(1)} %bitcast.6, f32[16]{0:T(128)S(1)} %copy-done.8, ...), custom_call_target="tpu_custom_call" | custom-call | flops 536870912 | bytes 1048576 | tf_op jit(solution)/shard_map/project/pallas_call | solution.py:204
  12.9 17.1 %all_to_all.10.arrived_ref = bf16[16,16,640]{2,1,0:T(8,128)(2,1)S(1)} all-to-all(bf16[16,16,640]{2,1,0:T(8,128)(2,1)S(1)} %get-tuple-element.9), channel_id=1, replica_groups=mesh['wide'=16,'field'=2] {'wide'}, dimensions={0} | all-to-all | bytes 655360 | tf_op jit(solution)/shard_map/all_to_all | solution.py:405
  30.0 1.2 %coarse_stage.1 = bf16[16,32,512]{2,1,0:T(8,128)(2,1)S(1)} custom-call(bf16[16,16,640]{2,1,0:T(8,128)(2,1)S(1)} %all_to_all.10.arrived_ref), custom_call_target="tpu_custom_call" | custom-call | flops 268435456 | bytes 524288 | tf_op jit(solution)/shard_map/coarse_stage/pallas_call | solution.py:271
  31.2 17.5 %all_to_all.11.back_ref = bf16[16,32,512]{2,1,0:T(8,128)(2,1)S(1)} all-to-all(bf16[16,32,512]{2,1,0:T(8,128)(2,1)S(1)} %coarse_stage.1), channel_id=1, replica_groups=mesh['wide'=16,'field'=2] {'wide'}, dimensions={0} | all-to-all | bytes 1048576 | tf_op jit(solution)/shard_map/all_to_all | solution.py:407
  48.7 0.0 copy-done.1
  48.7 0.0 copy-done.2
  48.7 4.3 %restrict.1 = (bf16[16,16,512]{2,1,0:T(8,128)(2,1)}, bf16[8,16,512]{2,1,0:T(8,128)(2,1)}) custom-call(s32[1]{0:T(128)} %bitcast.place_ref, s32[16]{0:T(128)S(1)} %copy-done.1, f32[8]{0:T(128)S(1)} %copy-done.2, bf16[16,32,512]{2,1,0:T(8,128)(2,1)S(1)} %all_to_all.11.back_ref, bf16[8,2,64,1024]{3,2,1,0:T(8,128)(2,1)S(1)} %get-tuple-element.10.refs_0_, ...), custom_call_target="tpu_custom_call" | custom-call | flops 1073741824 | bytes 2097152 | tf_op jit(solution)/shard_map/restrict/pallas_call | solution.py:341
Async XLA Ops:
  0.6 9.7 %copy-start.4 = (bf16[8,16,512]{2,1,0:T(8,128)(2,1)S(1)}, bf16[8,16,512]{2,1,0:T(8,128)(2,1)}, u32[]{:S(2)}) copy-start(bf16[8,16,512]{2,1,0:T(8,128)(2,1)} %refs_5_.1) | copy-start | bytes 393220
  0.6 9.7 %copy-start.8 = (f32[16]{0:T(128)S(1)}, f32[16]{0:T(128)}, u32[]{:S(2)}) copy-start(f32[16]{0:T(128)} %refs_3_.1) | copy-start | bytes 196
  0.7 9.7 %copy-start.5 = (s32[16,6]{0,1:T(8,128)S(1)}, s32[16,6]{0,1:T(8,128)}, u32[]{:S(2)}) copy-start(s32[16,6]{0,1:T(8,128)} %param.17) | copy-start | bytes 1156
  0.7 9.7 %copy-start.7 = (s32[16]{0:T(128)S(1)}, s32[16]{0:T(128)}, u32[]{:S(2)}) copy-start(s32[16]{0:T(128)} %refs_1_.3) | copy-start | bytes 196
  0.7 9.7 %copy-start.6 = (s32[16,1]{0,1:T(1,128)S(1)}, s32[16,1]{0,1:T(1,128)}, u32[]{:S(2)}) copy-start(s32[16,1]{0,1:T(1,128)} %param.15) | copy-start | bytes 196
  1.7 8.6 %collective-permute-start = (f32[7,8,1024]{2,1,0:T(8,128)S(1)}, f32[7,8,1024]{2,1,0:T(8,128)S(1)}, u32[]{:S(2)}, u32[]{:S(2)}) collective-permute-start(f32[7,8,1024]{2,1,0:T(8,128)S(1)} %pad_maximum_fusion.refs_0_), channel_id=1, source_target_pairs={{1,0},{0,1},{3,2},{2,3},{5,4},{4,5},{7,6},{6,7},{9,8},{8,9},{11,10... | collective-permute-start | bytes 688136 | tf_op jit(solution)/shard_map/ppermute | solution.py:394
  4.7 0.7 %copy-start = (s32[16]{0:T(128)S(1)}, s32[16]{0:T(128)}, u32[]{:S(2)}) copy-start(s32[16]{0:T(128)} %fine_ids.1) | copy-start | bytes 196
  5.4 0.9 %copy-start.3 = (bf16[8,16,512]{2,1,0:T(8,128)(2,1)S(1)}, bf16[8,16,512]{2,1,0:T(8,128)(2,1)}, u32[]{:S(2)}) copy-start(bf16[8,16,512]{2,1,0:T(8,128)(2,1)} %refs_5_.1) | copy-start | bytes 393220
  10.4 38.3 %copy-start.1 = (s32[16]{0:T(128)S(1)}, s32[16]{0:T(128)}, u32[]{:S(2)}) copy-start(s32[16]{0:T(128)} %fine_ids.1) | copy-start | bytes 196
  10.4 38.3 %copy-start.2 = (f32[8]{0:T(128)S(1)}, f32[8]{0:T(128)}, u32[]{:S(2)}) copy-start(f32[8]{0:T(128)} %inverse_ref.1) | copy-start | bytes 100

commit v9 on v8

--- a/solution.py
+++ b/solution.py
@@ -12,6 +12,7 @@
 DIFFUSE = 0.125
 LANES = 128
 DIGIT = 7
+SPAN = 4
 
 NT = (((1,), (1,)), ((), ()))
 NN = (((1,), (0,)), ((), ()))
@@ -65,8 +66,8 @@
         [coefs[:, lanes(a // 2)] * keep[a % 2] for a in range(NB)], axis=0
     )
     total = None
-    for start in range(0, quad, 2 * LANES):
-        columns = slice(start, start + 2 * LANES)
+    for start in range(0, quad, SPAN * LANES):
+        columns = slice(start, start + SPAN * LANES)
         inward = table_ref[pair, source, :, columns]
         outward = table_ref[pair, 1 - source, :, columns]
         inner = lax.dot_general(
@@ -76,7 +77,7 @@
             preferred_element_type=jnp.float32,
         )
         outer = []
-        for half in range(2):
+        for half in range(SPAN):
             lane = start // LANES + half
             enter = [spread(heads, source, lane, row + a) for a in range(NB)]
             leave = [spread(heads, 1 - source, lane, row + a) for a in range(NB)]

time: 53.2 us -> 53.2 us (level)
  no operation moved by 1% of the time
where the time goes in v9:
time: 53.2 us; the launch traced here: 53 us
  blocking collectives  34.6 us (65%)
  Pallas kernels  10.3 us (19%)
  starting transfers between devices  3 us (6%)
  waiting for transfers between devices  1.68 us (3%)
  local copies, waits for them, and re-layouts  1.59 us (3%)
  other arithmetic  1.05 us (2%)
  between operations  0.74 us (1%)
    all_to_all x1, blocking collectives, shards(): lax.all_to_all(smooth, 'wide', split_axis=0, concat_axis=0, tiled=True)  17.5 us
    all_to_all x1, blocking collectives, shards(): lax.all_to_all(outs[-1], 'wide', split_axis=0, concat_axis=0, tiled=True)  17.1 us
    pallas_call x2, Pallas kernels, project(): pl.pallas_call(functools.partial(project_kernel, shift, shifts), in_specs...  4.89 us
    pallas_call x1, Pallas kernels, restrict(): pl.pallas_call(functools.partial(restrict_kernel, len(tables)), in_specs=...  4.21 us
    ppermute x1, starting transfers between devices, shards(): points.append(lax.ppermute(own, 'field', perm))  3 us
    ppermute x1, waiting for transfers between devices, shards(): points.append(lax.ppermute(own, 'field', perm))  1.68 us
    unnamed x18, local copies, waits for them, and re-layouts  1.59 us
    pallas_call x1, Pallas kernels, coarse_stage(): pl.pallas_call(functools.partial(coarse_kernel, faces, elements), in_spec...  1.2 us
  transfers between devices with their start and end apart: 1, of which 1 were waited for; matrix products, arithmetic and copies ran while one was open for 0% of the time, Pallas kernels for 4%

profile of v9, /device:TPU:0, one launch (start us, length us, event | category | flops | bytes accessed | tf_op | source)
XLA Modules:
  0.0 53.0 jit_solution(1891518464621709320)
XLA Ops:
  0.6 0.0 copy-start.4
  0.6 0.0 copy-start.8
  0.7 0.0 copy-start.5
  0.7 0.0 copy-start.7
  0.7 0.0 copy-start.6
  0.7 1.1 %pad_maximum_fusion.refs_0_ = f32[7,8,1024]{2,1,0:T(8,128)S(1)} fusion(f32[1,8,1024]{2,1,0:T(8,128)} %bitcast.10, f32[3,8,1024]{2,1,0:T(8,128)} %bitcast.8, f32[3,8,1024]{2,1,0:T(8,128)} %bitcast.9), kind=kLoop, calls=%fused_computation | loop fusion | flops 114688 | bytes 458752 | tf_op jit(solution)/shard_map/concatenate | solution.py:384
  1.7 3.0 %collective-permute-start = (f32[7,8,1024]{2,1,0:T(8,128)S(1)}, f32[7,8,1024]{2,1,0:T(8,128)S(1)}, u32[]{:S(2)}, u32[]{:S(2)}) collective-permute-start(f32[7,8,1024]{2,1,0:T(8,128)S(1)} %pad_maximum_fusion.refs_0_), channel_id=1, source_target_pairs={{1,0},{0,1},{3,2},{2,3},{5,4},{4,5},{7,6},{6,7},{9,8},{8,9},{11,10... | collective-permute-start | bytes 688136 | tf_op jit(solution)/shard_map/ppermute | solution.py:395
  4.7 0.0 copy-start
  4.7 0.7 %copy-done = s32[16]{0:T(128)S(1)} copy-done((s32[16]{0:T(128)S(1)}, s32[16]{0:T(128)}, u32[]{:S(2)}) %copy-start) | copy-done | bytes 88
  5.4 0.0 copy-start.3
  5.4 0.9 %copy-done.3 = bf16[8,16,512]{2,1,0:T(8,128)(2,1)S(1)} copy-done((bf16[8,16,512]{2,1,0:T(8,128)(2,1)S(1)}, bf16[8,16,512]{2,1,0:T(8,128)(2,1)}, u32[]{:S(2)}) %copy-start.3) | copy-done | bytes 131096
  6.3 2.4 %project.2 = (bf16[8,2,64,1024]{3,2,1,0:T(8,128)(2,1)S(1)}, f32[2,8,64,128]{3,2,1,0:T(8,128)S(1)}, f32[4,128,128]{2,1,0:T(8,128)S(1)}) custom-call(s32[1]{0:T(128)} %bitcast.place_ref, s32[16]{0:T(128)S(1)} %copy-done, f32[7,8,1024]{2,1,0:T(8,128)S(1)} %pad_maximum_fusion.refs_0_, bf16[8,16,512]{2,1,0:T(8,128)(2,1)S(1)} %copy-done.3), custom_call_target="tpu_custom_call" | custom-call | flops 536870912 | bytes 1048576 | tf_op jit(solution)/shard_map/project/pallas_call | solution.py:205
  8.7 1.7 %collective-permute-done.refs_4_ = f32[7,8,1024]{2,1,0:T(8,128)S(1)} collective-permute-done((f32[7,8,1024]{2,1,0:T(8,128)S(1)}, f32[7,8,1024]{2,1,0:T(8,128)S(1)}, u32[]{:S(2)}, u32[]{:S(2)}) %collective-permute-start) | collective-permute-done | bytes 229408 | tf_op jit(solution)/shard_map/ppermute | solution.py:395
  10.3 0.0 copy-done.4
  10.3 0.0 copy-done.8
  10.4 0.0 copy-done.5
  10.4 0.0 copy-done.7
  10.4 0.0 copy-done.6
  10.4 0.0 copy-start.1
  10.4 0.0 copy-start.2
  10.4 2.5 %project.3 = (bf16[8,2,64,1024]{3,2,1,0:T(8,128)(2,1)S(1)}, f32[2,8,64,128]{3,2,1,0:T(8,128)S(1)}, bf16[16,16,640]{2,1,0:T(8,128)(2,1)S(1)}) custom-call(s32[1]{0:T(128)} %bitcast.place_ref, s32[16]{0:T(128)S(1)} %copy-done, s32[1,16]{1,0:T(1,128)S(1)} %bitcast.7, s32[16]{0:T(128)S(1)} %copy-done.7, s32[6,16]{1,0:T(8,128)S(1)} %bitcast.6, f32[16]{0:T(128)S(1)} %copy-done.8, ...), custom_call_target="tpu_custom_call" | custom-call | flops 536870912 | bytes 1048576 | tf_op jit(solution)/shard_map/project/pallas_call | solution.py:205
  12.9 17.1 %all_to_all.10.arrived_ref = bf16[16,16,640]{2,1,0:T(8,128)(2,1)S(1)} all-to-all(bf16[16,16,640]{2,1,0:T(8,128)(2,1)S(1)} %get-tuple-element.9), channel_id=1, replica_groups=mesh['wide'=16,'field'=2] {'wide'}, dimensions={0} | all-to-all | bytes 655360 | tf_op jit(solution)/shard_map/all_to_all | solution.py:406
  30.0 1.2 %coarse_stage.1 = bf16[16,32,512]{2,1,0:T(8,128)(2,1)S(1)} custom-call(bf16[16,16,640]{2,1,0:T(8,128)(2,1)S(1)} %all_to_all.10.arrived_ref), custom_call_target="tpu_custom_call" | custom-call | flops 268435456 | bytes 524288 | tf_op jit(solution)/shard_map/coarse_stage/pallas_call | solution.py:272
  31.2 17.5 %all_to_all.11.back_ref = bf16[16,32,512]{2,1,0:T(8,128)(2,1)S(1)} all-to-all(bf16[16,32,512]{2,1,0:T(8,128)(2,1)S(1)} %coarse_stage.1), channel_id=1, replica_groups=mesh['wide'=16,'field'=2] {'wide'}, dimensions={0} | all-to-all | bytes 1048576 | tf_op jit(solution)/shard_map/all_to_all | solution.py:408
  48.7 0.0 copy-done.1
  48.7 0.0 copy-done.2
  48.7 4.2 %restrict.1 = (bf16[16,16,512]{2,1,0:T(8,128)(2,1)}, bf16[8,16,512]{2,1,0:T(8,128)(2,1)}) custom-call(s32[1]{0:T(128)} %bitcast.place_ref, s32[16]{0:T(128)S(1)} %copy-done.1, f32[8]{0:T(128)S(1)} %copy-done.2, bf16[16,32,512]{2,1,0:T(8,128)(2,1)S(1)} %all_to_all.11.back_ref, bf16[8,2,64,1024]{3,2,1,0:T(8,128)(2,1)S(1)} %get-tuple-element.10.refs_0_, ...), custom_call_target="tpu_custom_call" | custom-call | flops 1073741824 | bytes 2097152 | tf_op jit(solution)/shard_map/restrict/pallas_call | solution.py:342
Async XLA Ops:
  0.6 9.7 %copy-start.4 = (bf16[8,16,512]{2,1,0:T(8,128)(2,1)S(1)}, bf16[8,16,512]{2,1,0:T(8,128)(2,1)}, u32[]{:S(2)}) copy-start(bf16[8,16,512]{2,1,0:T(8,128)(2,1)} %refs_5_.1) | copy-start | bytes 393220
  0.6 9.7 %copy-start.8 = (f32[16]{0:T(128)S(1)}, f32[16]{0:T(128)}, u32[]{:S(2)}) copy-start(f32[16]{0:T(128)} %refs_3_.1) | copy-start | bytes 196
  0.7 9.7 %copy-start.5 = (s32[16,6]{0,1:T(8,128)S(1)}, s32[16,6]{0,1:T(8,128)}, u32[]{:S(2)}) copy-start(s32[16,6]{0,1:T(8,128)} %param.17) | copy-start | bytes 1156
  0.7 9.7 %copy-start.7 = (s32[16]{0:T(128)S(1)}, s32[16]{0:T(128)}, u32[]{:S(2)}) copy-start(s32[16]{0:T(128)} %refs_1_.3) | copy-start | bytes 196
  0.7 9.7 %copy-start.6 = (s32[16,1]{0,1:T(1,128)S(1)}, s32[16,1]{0,1:T(1,128)}, u32[]{:S(2)}) copy-start(s32[16,1]{0,1:T(1,128)} %param.15) | copy-start | bytes 196
  1.7 8.6 %collective-permute-start = (f32[7,8,1024]{2,1,0:T(8,128)S(1)}, f32[7,8,1024]{2,1,0:T(8,128)S(1)}, u32[]{:S(2)}, u32[]{:S(2)}) collective-permute-start(f32[7,8,1024]{2,1,0:T(8,128)S(1)} %pad_maximum_fusion.refs_0_), channel_id=1, source_target_pairs={{1,0},{0,1},{3,2},{2,3},{5,4},{4,5},{7,6},{6,7},{9,8},{8,9},{11,10... | collective-permute-start | bytes 688136 | tf_op jit(solution)/shard_map/ppermute | solution.py:395
  4.7 0.7 %copy-start = (s32[16]{0:T(128)S(1)}, s32[16]{0:T(128)}, u32[]{:S(2)}) copy-start(s32[16]{0:T(128)} %fine_ids.1) | copy-start | bytes 196
  5.4 0.9 %copy-start.3 = (bf16[8,16,512]{2,1,0:T(8,128)(2,1)S(1)}, bf16[8,16,512]{2,1,0:T(8,128)(2,1)}, u32[]{:S(2)}) copy-start(bf16[8,16,512]{2,1,0:T(8,128)(2,1)} %refs_5_.1) | copy-start | bytes 393220
  10.4 38.4 %copy-start.1 = (s32[16]{0:T(128)S(1)}, s32[16]{0:T(128)}, u32[]{:S(2)}) copy-start(s32[16]{0:T(128)} %fine_ids.1) | copy-start | bytes 196
  10.4 38.4 %copy-start.2 = (f32[8]{0:T(128)S(1)}, f32[8]{0:T(128)}, u32[]{:S(2)}) copy-start(f32[8]{0:T(128)} %inverse_ref.1) | copy-start | bytes 100
